TPU v7x, 256 devices: a whole 4x4x8 slice. The times are simulated.
256 devices in a mesh: bx: 16 (over y, x), by: 8 (over z), cz: 2 (over core).
Axes of the slice: x: 4, y: 4, z: 8, core: 2. Of those that a mesh axis runs over, the one named last changes fastest.
Arguments:
- latents: bfloat16 [256, 16, 16, 16, 64], P(('bx', 'by', 'cz')), may hold values from -6 to 6
- target: bfloat16 [256, 16, 16, 16, 64], P(('bx', 'by', 'cz')), may hold values from -6 to 6
- block_coords: int32 [256, 3], P(('bx', 'by', 'cz')), may hold values from -1 to 1, as said below
- timestep: int32 [1], replicated, may hold values from 0 to 999
- conv_weight: bfloat16 [27, 64, 64], replicated, may hold values from -0.15625 to 0.15625
- coarse_weight: bfloat16 [27, 64, 64], replicated, may hold values from -0.15625 to 0.15625
- out_weight: bfloat16 [64, 64], replicated, may hold values from -0.75 to 0.75
- time_weight: bfloat16 [256, 64], replicated, may hold values from -0.5 to 0.5
- norm_gain: float32 [64], replicated, may hold values from 0.5 to 1.5
- norm_bias: float32 [64], replicated, may hold values from -3 to 3
Outputs:
- predicted: bfloat16 [256, 16, 16, 16, 64], P(('bx', 'by', 'cz'))
- mean_loss: float32 [1], replicated
- grad_conv: float32 [27, 64, 64], replicated
- grad_coarse: float32 [27, 64, 64], replicated
- grad_out: float32 [64, 64], replicated
- grad_time: float32 [256, 64], replicated
- grad_gain: float32 [64], replicated
- grad_bias: float32 [64], replicated
Inputs may be any that keep to these rules, and one draw needn't show every extreme that they name: `block_coords`: each row is x, y, z of a block position within its region, x below 2, y below 2, z below 2; a device's live slots come first and hold distinct positions, its other slots are -1 in all three; every device has a live slot and some device fills all 1.
All inputs are finite; a program needn't handle non-finite values.
Results may differ from a plain program's by a relative error of at most 0.0045.
The roundings to bfloat16 on the way count: a program that leaves them out, or rounds other values in their place, can miss the bound.
Values may be sent and summed in bfloat16 or wider, within the bound.
No kernel may reach another device: no remote copies, remote signals or barrier semaphores. Data moves between devices by JAX's collectives and lax.ppermute only.
A program may use at most 128 MiB of HBM per device.

v0:
```python
import math

import jax
import jax.numpy as jnp
import numpy as np
from jax import lax
from jax.experimental import pallas as pl
from jax.experimental.pallas import tpu as pltpu
from jax.sharding import PartitionSpec as P

ALL = ("bx", "by", "cz")
CHIPS = ("bx", "by")
BF = jnp.bfloat16
F32 = jnp.float32
EPS = 1e-05
GROUP = 2
VMEM_LIMIT = 56 * 1024 * 1024
SHIFT_LANE = 65


def face_spec(dim, index):
    shape = tuple(1 if d == dim else 16 for d in range(3)) + (64,)
    where = tuple(index if d == dim else 0 for d in range(4))
    return pl.BlockSpec(shape, lambda i: where)


def call(kernel, outs, args, scratch=(), faces=()):
    vmem = pl.BlockSpec(memory_space=pltpu.VMEM)
    specs = list(faces) + [vmem] * (len(args) - 1 - len(faces))
    return pl.pallas_call(
        kernel,
        grid=(1,),
        out_shape=outs,
        in_specs=[pl.BlockSpec(memory_space=pltpu.SMEM)] + specs,
        out_specs=[vmem] * len(outs),
        scratch_shapes=list(scratch),
        compiler_params=pltpu.CompilerParams(vmem_limit_bytes=VMEM_LIMIT),
    )(*args)


def like(shape, dtype):
    return jax.ShapeDtypeStruct(shape, dtype)


def keep(cond, value):
    return jnp.where(cond, value, jnp.zeros_like(value))


def bits(info):
    return info[0, 0], info[0, 1], info[0, 2], lax.axis_index("cz")


def start16(bit):
    return pl.multiple_of(bit * 16, 16)


def cell_rows(first, second, face, on):
    rows = []
    for r in range(4):
        for s in range(4):
            here = on & (first == r // 2) & (second == s // 2)
            rows.append(keep(here, face[r % 2][s % 2]))
    return jnp.concatenate(rows, axis=0)


def row_of(cells, p):
    return cells[p : p + 1]


def z_message(info, lat, out, pooled):
    px, py, pz, kz = bits(info)
    on = pz == 1 - kz
    zsel = 15 * (1 - kz)
    out[...] = jnp.zeros(out.shape, BF)
    pick = lax.broadcasted_iota(jnp.int32, (16, 16, 64), 1) == zsel
    sums = [[None, None], [None, None]]
    for y in range(16):
        slab = lat[:, y].astype(F32)
        face = jnp.sum(jnp.where(pick, slab, 0.0), axis=1)
        out[py * 16 + y, pl.ds(start16(px), 16), :] = keep(on, face).astype(BF)
        for a in range(2):
            part = jnp.sum(slab[8 * a : 8 * a + 8], axis=0)
            old = sums[a][y // 8]
            sums[a][y // 8] = part if old is None else old + part
    cells = []
    for a in range(2):
        for b in range(2):
            for c in range(2):
                cells.append(jnp.sum(sums[a][b][8 * c : 8 * c + 8], axis=0, keepdims=True))
    cells = jnp.concatenate(cells, axis=0) * (1.0 / math.sqrt(512.0))
    cells = cells.astype(BF).astype(F32)
    pooled[...] = jnp.concatenate([cells, jnp.zeros((8, 64), F32)], axis=0).astype(BF)
    face = [
        [jnp.where(kz == 0, row_of(cells, 4 * a + 2 * b + 1), row_of(cells, 4 * a + 2 * b)) for a in range(2)]
        for b in range(2)
    ]
    rows = cell_rows(py, px, face, on)
    out[32] = jnp.concatenate([rows, jnp.zeros((16, 64), F32)], axis=0).astype(BF)


def y_messages(info, low, high, rz, pooled, down, up):
    px, py, pz, kz = bits(info)
    cells = pooled[...].astype(F32)
    halo = rz[32].astype(F32)
    for out, face, bit, line, q in ((down, low, 0, 0, 0), (up, high, 1, 31, 1)):
        on = py == bit
        out[...] = jnp.zeros(out.shape, BF)
        out[pl.ds(start16(px), 16), pl.ds(start16(pz), 16), :] = keep(on, face[:, 0])
        out[32] = rz[line]
        picked = [[row_of(cells, 4 * a + 2 * q + c) for c in range(2)] for a in range(2)]
        rows = cell_rows(px, pz, picked, on)
        tail = halo[12:16] if q else halo[0:4]
        out[33] = jnp.concatenate([rows, tail, jnp.zeros((12, 64), F32)], axis=0).astype(BF)


def x_messages(info, low, high, rz, rym, ryp, pooled, down, up):
    px, py, pz, kz = bits(info)
    cells = pooled[...].astype(F32)
    halo = rz[32].astype(F32)
    halo_m = rym[33].astype(F32)
    halo_p = ryp[33].astype(F32)
    line_m = rym[32].astype(F32)
    line_p = ryp[32].astype(F32)
    where16 = lax.broadcasted_iota(jnp.int32, (32, 16, 64), 1)
    for out, face, bit, line, q in ((down, low, 0, 0, 0), (up, high, 1, 31, 1)):
        on = px == bit
        out[...] = jnp.zeros(out.shape, BF)
        out[pl.ds(start16(py), 16), pl.ds(start16(pz), 16), :] = keep(on, face[0])
        slab = rz[0:32, 16 * q : 16 * q + 16, :].astype(F32)
        out[32] = jnp.sum(jnp.where(where16 == 15 * q, slab, 0.0), axis=1).astype(BF)
        out[33] = rym[line]
        out[34] = ryp[line]
        picked = [[row_of(cells, 4 * q + 2 * b + c) for c in range(2)] for b in range(2)]
        rows = cell_rows(py, pz, picked, on)
        corners = [line_m[line : line + 1], line_p[line : line + 1], jnp.zeros((14, 64), F32)]
        out[35] = jnp.concatenate(corners + [rows], axis=0).astype(BF)
        c0 = 3 * q
        parts = [row_of(halo, 4 * cy + c0) for cy in range(4)]
        parts += [halo_m[4 * c0 : 4 * c0 + 4], halo_p[4 * c0 : 4 * c0 + 4]]
        parts += [row_of(halo_m, 16 + c0), row_of(halo_p, 16 + c0), jnp.zeros((18, 64), F32)]
        out[36] = jnp.concatenate(parts, axis=0).astype(BF)


def coarse_table():
    pooled, rz, rym, ryp, rxm, rxp = 0, 16, 32, 64, 96, 128
    table = np.zeros((16, 224, 160), np.float32)
    for combo in range(16):
        bit = ((combo >> 3) & 1, (combo >> 2) & 1, (combo >> 1) & 1)
        core = combo & 1
        for tap in range(27):
            off = (tap // 9, tap // 3 % 3, tap % 3)
            for p in range(8):
                at = (p // 4, p // 2 % 2, p % 2)
                pos = [2 * bit[d] - 1 + off[d] + at[d] for d in range(3)]
                x, y, z = pos
                out_z = z < 0 or z > 3
                if out_z and (z < 0) != (core == 1):
                    continue
                if x < 0 or x > 3:
                    base = rxm if x < 0 else rxp
                    if y < 0 or y > 3:
                        side = 0 if y < 0 else 1
                        row = 16 + (12 + side if out_z else 4 + 4 * side + z)
                    else:
                        row = 16 + y if out_z else 4 * y + z
                    row = base + row
                elif y < 0 or y > 3:
                    row = (rym if y < 0 else ryp) + (16 + x if out_z else 4 * x + z)
                elif out_z:
                    row = rz + 4 * y + x
                else:
                    own = [pos[d] - 2 * bit[d] for d in range(3)]
                    if min(own) < 0 or max(own) > 1:
                        continue
                    row = pooled + 4 * own[0] + 2 * own[1] + own[2]
                table[combo, 8 * tap + p, row] = 1.0
    return table


class Window:
    def __init__(self, info, rz, rym, ryp):
        px, py, pz, kz = bits(info)
        self.pz, self.rz, self.rym, self.ryp = pz, rz, rym, ryp
        self.z0 = pl.ds(start16(pz), 16)
        self.z1 = pl.ds(start16(1 - pz), 16)
        self.xs = pl.ds(start16(px), 16)
        self.ys = pl.ds(start16(py), 16)
        self.xlo, self.xhi, self.ylo, self.yhi = px == 0, px == 1, py == 0, py == 1
        self.on_low = (pz == 0) & (kz == 1)
        self.on_high = (pz == 1) & (kz == 0)
        self.row16 = lax.broadcasted_iota(jnp.int32, (16, 16, 64), 1)
        self.z_row = lax.broadcasted_iota(jnp.int32, (9, 16, 128), 1)

    def edge(self, block):
        return jnp.sum(jnp.where(self.row16[: block.shape[0]] == 15 * self.pz, block.astype(F32), 0.0), axis=1)

    def edge1(self, ref, i):
        return self.edge(ref[i : i + 1, self.z1, :])

    def low_of(self, e, h):
        return keep(self.pz == 1, e) + keep(self.on_low, h)

    def high_of(self, e, h):
        return keep(self.pz == 0, e) + keep(self.on_high, h)

    def offsets(self, evens, odds, first, last, zl, zh):
        left = jnp.concatenate([first[None], odds], axis=0)
        right = jnp.concatenate([evens, last[None]], axis=0)
        tile = jnp.concatenate([left, right], axis=2)
        wide = tile.astype(F32)
        down = jnp.where(self.z_row == 0, zl, pltpu.roll(wide, 1, 1)).astype(BF)
        up = jnp.where(self.z_row == 15, zh, pltpu.roll(wide, 15, 1)).astype(BF)
        return down, tile, up


def one(ref, i, j):
    return ref[i].astype(F32)[j : j + 1]


def interior(info, lat, rz, rym, ryp, weight, raw, scene, columns):
    w = Window(info, rz, rym, ryp)
    y_low = keep(w.ylo, rym[w.xs, w.z0, :])
    y_high = keep(w.yhi, ryp[w.xs, w.z0, :])
    e_low = keep(w.ylo, w.edge(rym[w.xs, w.z1, :]))
    e_high = keep(w.yhi, w.edge(ryp[w.xs, w.z1, :]))
    h_low = jnp.where(w.ylo, rym[32, w.xs, :], rz[15, w.xs, :]).astype(F32)
    h_high = jnp.where(w.yhi, ryp[32, w.xs, :], rz[16, w.xs, :]).astype(F32)
    h_mid = rz[w.ys, w.xs, :].astype(F32)

    def packed(of):
        rows = [of(e_low, h_low)] + [of(jnp.zeros((16, 64), F32), h_mid[y]) for y in range(16)]
        rows.append(of(e_high, h_high))
        return [jnp.concatenate([rows[2 * k], rows[2 * k + 1]], axis=1) for k in range(9)]

    below, above = packed(w.low_of), packed(w.high_of)
    inner = [None] * 3
    for x in range(16):
        zl = jnp.concatenate([below[k][x : x + 1][None] for k in range(9)], axis=0)
        zh = jnp.concatenate([above[k][x : x + 1][None] for k in range(9)], axis=0)
        planes = w.offsets(lat[x, :, 0], lat[x, :, 1], y_low[x], y_high[x], zl, zh)
        for oz, plane in enumerate(planes):
            scene[oz, x] = plane
            wide = plane.astype(F32)
            inner[oz] = wide if x == 0 else inner[oz] + wide
    for oz in range(3):
        columns[oz] = jnp.sum(inner[oz], axis=1)
    for first, count in ((1, 4), (5, 4), (9, 4), (13, 2)):
        pieces = []
        for tap in range(9):
            ox, oz = tap // 3, tap % 3
            for dk in range(2):
                at = first + ox - 1
                pieces.append(scene[oz, at : at + count, dk : dk + 8].reshape(128 * count, 128))
        value = jnp.dot(jnp.concatenate(pieces, axis=1), weight[...], preferred_element_type=F32)
        raw[(first - 1) * 128 : (first - 1 + count) * 128] = value


def forward(info, near_low, near_high, raw, columns, rz, rym, ryp, rxm, rxp, pooled, table, weight, coarse_weight, time_bias, act, ends, patch_out, stats, shift):
    w = Window(info, rz, rym, ryp)
    nought = jnp.zeros((16, 64), BF)

    def sides(rx, out, inner):
        first = jnp.where(
            out,
            jnp.where(w.ylo, rx[33, w.z0, :], rx[15, w.z0, :]),
            jnp.where(w.ylo, rym[inner, w.z0, :], nought),
        )
        last = jnp.where(
            out,
            jnp.where(w.yhi, rx[34, w.z0, :], rx[16, w.z0, :]),
            jnp.where(w.yhi, ryp[inner, w.z0, :], nought),
        )
        return first, last

    def side_columns(rx, out, inner, of):
        half = rz[w.ys, 0:16, :] if inner < 16 else rz[w.ys, 16:32, :]
        inner_h = jnp.sum(jnp.where(w.row16 == inner % 16, half.astype(F32), 0.0), axis=1)
        e_mid = keep(out, w.edge(rx[w.ys, w.z1, :]))
        hh = jnp.where(out, rx[32, w.ys, :].astype(F32), inner_h)
        e_first = jnp.where(
            out,
            jnp.where(w.ylo, w.edge1(rx, 33), w.edge1(rx, 15)),
            keep(w.ylo, w.edge1(rym, inner)),
        )
        h_first = jnp.where(
            out,
            jnp.where(w.ylo, one(rx, 35, 0), one(rx, 32, 15)),
            jnp.where(w.ylo, one(rym, 32, inner), one(rz, 15, inner)),
        )
        e_last = jnp.where(
            out,
            jnp.where(w.yhi, w.edge1(rx, 34), w.edge1(rx, 16)),
            keep(w.yhi, w.edge1(ryp, inner)),
        )
        h_last = jnp.where(
            out,
            jnp.where(w.yhi, one(rx, 35, 1), one(rx, 32, 16)),
            jnp.where(w.yhi, one(ryp, 32, inner), one(rz, 16, inner)),
        )
        mid = of(e_mid, hh)
        rows = [of(e_first, h_first)] + [mid[y : y + 1] for y in range(16)] + [of(e_last, h_last)]
        return [jnp.concatenate([rows[2 * k], rows[2 * k + 1]], axis=1)[None] for k in range(9)]

    for e, rx, out, inner in ((0, rxm, w.xlo, 15), (1, rxp, w.xhi, 16)):
        zl = jnp.concatenate(side_columns(rx, out, inner, w.low_of), axis=0)
        zh = jnp.concatenate(side_columns(rx, out, inner, w.high_of), axis=0)
        first, last = sides(rx, out, inner)
        plane = keep(out, rx[w.ys, w.z0, :]).reshape(8, 2, 16, 64)
        for oz, tile in enumerate(w.offsets(plane[:, 0], plane[:, 1], first, last, zl, zh)):
            ends[e, oz] = tile

    source = jnp.concatenate(
        [pooled[...], rz[32, 0:16, :], rym[33], ryp[33], rxm[35, 16:32, :], rxm[36, 0:16, :], rxp[35, 16:32, :], rxp[36, 0:16, :]],
        axis=0,
    )
    taps = jnp.dot(table[...], source, preferred_element_type=F32)
    patch = jnp.concatenate([taps[8 * t : 8 * t + 8] for t in range(27)], axis=1)
    patch_out[...] = jnp.concatenate([patch, patch], axis=0).astype(BF)
    coarse = jnp.dot(patch_out[...], coarse_weight[...], preferred_element_type=F32)
    coarse = coarse.astype(BF).astype(F32)
    coarse = jnp.concatenate([coarse, coarse], axis=1)
    z_half = lax.broadcasted_iota(jnp.int32, (16, 128), 0) < 8
    added = []
    for q in range(4):
        added.append(jnp.where(z_half, coarse[2 * q : 2 * q + 1], coarse[2 * q + 1 : 2 * q + 2]) + time_bias[...])

    pieces = []
    for tap in range(9):
        ox, oz = tap // 3, tap % 3
        low = ends[0, oz] if ox == 0 else near_low[oz, ox - 1]
        high = ends[1, oz] if ox == 2 else near_high[oz, ox]
        for dk in range(2):
            pieces.append(jnp.concatenate([low[dk : dk + 8], high[dk : dk + 8]], axis=0).reshape(256, 128))
    edges = jnp.dot(jnp.concatenate(pieces, axis=1), weight[...], preferred_element_type=F32)

    total = jnp.zeros((1, 128), F32)
    squares = jnp.zeros((1, 128), F32)
    for x in range(16):
        if x == 0:
            value = edges[:128]
        elif x == 15:
            value = edges[128:]
        else:
            value = raw[(x - 1) * 128 : x * 128]
        value = value.reshape(2, 4, 16, 128)
        a = x // 8
        value = jnp.concatenate([(value[b] + added[2 * a + b][None])[None] for b in range(2)], axis=0).reshape(128, 128)
        act[x * 128 : x * 128 + 128] = value
        total = total + jnp.sum(value, axis=0, keepdims=True)
        squares = squares + jnp.sum(value * value, axis=0, keepdims=True)
    shift[...] = jnp.zeros(shift.shape, F32)

    def place(tap, slot, value):
        row = SHIFT_LANE + 2 * (tap // 4 + slot)
        u = tap % 4
        shift[u // 2, row : row + 1, 64 * (u % 2) : 64 * (u % 2) + 64] = value

    for oz in range(3):
        inner = columns[oz]
        planes = (ends[0, oz], near_low[oz, 0], near_high[oz, 1], ends[1, oz])
        outer = [jnp.sum(plane.astype(F32), axis=1) for plane in planes]
        for ox, part in enumerate((inner + outer[0] - outer[2], inner, inner - outer[1] + outer[3])):
            all_columns = jnp.sum(part, axis=0, keepdims=True)
            whole = all_columns[:, :64] + all_columns[:, 64:]
            y0, y1 = part[0:1, :64], part[0:1, 64:]
            y16, y17 = part[8:9, :64], part[8:9, 64:]
            for oy, window in enumerate((whole - y16 - y17, whole - y0 - y17, whole - y0 - y1)):
                place(9 * ox + 3 * oy + oz, 0, window)
    for t in range(27):
        place(t, 7, 512.0 * jnp.sum(taps[8 * t : 8 * t + 8], axis=0, keepdims=True))

    lane = lax.broadcasted_iota(jnp.int32, (1, 128), 1)
    pairs = pair_sum(squares + pltpu.roll(squares, 64, 1))
    row = jnp.where(lane < 64, total + pltpu.roll(total, 64, 1), jnp.where(lane % 2 == 0, pairs, 0.0))
    for u in range(2):
        stats[128 * u : 128 * u + 128] = shift[u].T + row


def pair_sum(row):
    lane = lax.broadcasted_iota(jnp.int32, row.shape, 1)
    return row + jnp.where(lane % 2 == 0, pltpu.roll(row, 127, 1), pltpu.roll(row, 1, 1))


def halves(row):
    lane = lax.broadcasted_iota(jnp.int32, row.shape, 1)
    other = pltpu.roll(row, 64, 1)
    return jnp.where(lane < 64, row, other), jnp.where(lane < 64, other, row)


def moments(gathered, count):
    row = jnp.sum(gathered[...], axis=0, keepdims=True)
    sums, upper = halves(row)
    lane = lax.broadcasted_iota(jnp.int32, row.shape, 1)
    squares = jnp.where(lane % 2 == 0, upper, pltpu.roll(upper, 1, 1))
    mean = pair_sum(sums) / count
    var = squares / count - mean * mean
    return row, sums, mean, 1.0 / jnp.sqrt(var + EPS)


def backward(voxels):
    count = float(voxels * GROUP)
    scale = 1.0 / (voxels * 64)

    def kernel(info, act, gathered, target, gain, bias, weight, weight_t, scene, ends, patch, stats, predicted, payload, cotangent):
        kz = lax.axis_index("cz")
        _, _, mean, rstd = moments(gathered, count)
        gains = jnp.zeros((1, 128), F32)
        biases = jnp.zeros((1, 128), F32)
        lost = jnp.zeros((1, 128), F32)
        outer = jnp.zeros((128, 128), F32)
        cells = [[None] * 4, [None] * 4]
        for x in range(0, 16, 2):
            rows = slice(x * 128, x * 128 + 256)
            normalized = (act[rows] - mean) * rstd
            shifted = normalized * gain[...] + bias[...]
            sigma = jax.nn.sigmoid(shifted)
            hidden = (shifted * sigma).astype(BF)
            output = jnp.dot(hidden, weight[...], preferred_element_type=F32)
            goal = jnp.concatenate([target[x : x + 2, :, 0], target[x : x + 2, :, 1]], axis=3)
            residue = output - goal.reshape(256, 128).astype(F32)
            shown = output.astype(BF).reshape(2, 8, 16, 128)
            predicted[x : x + 2, :, 0] = shown[..., :64]
            predicted[x : x + 2, :, 1] = shown[..., 64:]
            upstream = (2.0 * scale * residue).astype(BF)
            back = jnp.dot(upstream, weight_t[...], preferred_element_type=F32)
            value = back * sigma * (1.0 + shifted * (1.0 - sigma))
            gains = gains + jnp.sum(value * normalized, axis=0, keepdims=True)
            biases = biases + jnp.sum(value, axis=0, keepdims=True)
            lost = lost + jnp.sum(residue * residue, axis=0, keepdims=True)
            outer = outer + lax.dot_general(hidden, upstream, (((0,), (0,)), ((), ())), preferred_element_type=F32)
            value = value * (gain[...] * rstd)
            for part, wide in enumerate((value, normalized)):
                flipped = wide.T.astype(BF)
                cotangent[64 * part : 64 * part + 64, rows] = flipped[:64]
                cotangent[128 + 64 * part : 192 + 64 * part, rows] = flipped[64:]
                planes = wide.reshape(2, 2, 4, 16, 128)
                for b in range(2):
                    q = 2 * (x // 8) + b
                    cell = jnp.sum(planes[:, b], axis=(0, 1))
                    old = cells[part][q]
                    cells[part][q] = cell if old is None else old + cell

        def store(tap, slot, value):
            u = tap % 4
            half = jnp.where(kz == u // 2, 0, 1)
            payload.at[half][pl.ds(1024 * (u % 2) + slot + tap // 4, 64, stride=16), :] = value

        rows = []
        for q in range(4):
            for c in range(2):
                sums = [jnp.sum(cells[p][q][8 * c : 8 * c + 8], axis=0, keepdims=True) for p in range(2)]
                rows.append(jnp.concatenate([r[:, :64] + r[:, 64:] for r in sums], axis=1))
        rows = jnp.concatenate(rows, axis=0)
        high = rows.astype(BF)
        split = jnp.concatenate([high.astype(F32), rows - high.astype(F32)], axis=0).astype(BF)
        coarse = lax.dot_general(patch[...], split, (((0,), (0,)), ((), ())), preferred_element_type=F32)
        for t in range(27):
            store(t, 7, coarse[64 * t : 64 * t + 64])
        for ox in range(3):
            for oz in range(3):
                parts = []
                for dk in range(2):
                    planes = [scene[oz, max(ox - 1, 0) : min(ox + 15, 16), dk : dk + 8]]
                    if ox == 0:
                        planes = [ends[0, oz, dk : dk + 8][None]] + planes
                    if ox == 2:
                        planes = planes + [ends[1, oz, dk : dk + 8][None]]
                    parts.append(jnp.concatenate(planes, axis=0).reshape(2048, 128))
                window = jnp.concatenate(parts, axis=1)
                product = jnp.dot(cotangent[...], window, preferred_element_type=F32).T
                for oy in range(3):
                    value = product[64 * oy : 64 * oy + 64, :128] + product[64 * oy + 64 : 64 * oy + 128, 128:]
                    store(9 * ox + 3 * oy + oz, 0, value)
        nought = jnp.zeros((64, 64), F32)
        store(27, 0, jnp.concatenate([outer[:64, :64] + outer[64:, 64:], nought], axis=1))
        loss = jnp.broadcast_to(jnp.sum(lost, axis=1, keepdims=True), (64, 128))
        high = loss.astype(BF).astype(F32)
        lane = lax.broadcasted_iota(jnp.int32, (64, 128), 1)
        mine = jnp.where(lane == 2 * kz, high, jnp.where(lane == 2 * kz + 1, loss - high, 0.0))
        store(27, 7, mine)
        lane = lax.broadcasted_iota(jnp.int32, (1, 128), 1)
        row = jnp.where(lane < 64, gains + pltpu.roll(gains, 64, 1), biases + pltpu.roll(biases, 64, 1))
        wide = jnp.broadcast_to(row, (128, 128))
        for half in range(2):
            payload.at[half][pl.ds(14, 128, stride=16), :] = wide
            slot = jnp.where(kz == half, 0, 1)
            payload.at[slot][pl.ds(15, 128, stride=16), :] = stats[128 * half : 128 * half + 128]

    return kernel


def slopes(norms, gain, count):
    grad_gain, grad_bias = halves(norms)
    return pair_sum(gain * grad_bias) / count, pair_sum(gain * grad_gain) / count


def pair_add(voxels):
    total_count = float(voxels * GROUP)
    count = float(2 * 4096 * GROUP)

    def kernel(info, mine, other, gathered, gain, out):
        _, _, _, rstd = moments(gathered, total_count)
        total = (mine[...] + other[...]).reshape(-1, 16, 128)
        m1, m2 = slopes(total[0, 14:15], gain[...], count)
        row = lax.broadcasted_iota(jnp.int32, total.shape, 1)
        lane = lax.broadcasted_iota(jnp.int32, total.shape, 2)
        picked = (lane == SHIFT_LANE + 2 * row) & (row < 14)
        ones = jnp.sum(jnp.where(picked, total[:, 15:16], 0.0), axis=2, keepdims=True)
        centred = total - (m1 * rstd)[None] * ones - (m2 * rstd)[None] * pltpu.roll(total, 64, 2)
        total = jnp.where((lane < 64) & (row < 14), centred, total)
        lost = pltpu.roll(total - total.astype(BF).astype(F32), 1, 1)
        out[...] = jnp.where(row == 15, lost, total).astype(BF)

    return kernel


def combine(voxels):
    count = float(voxels * GROUP)
    pair_count = float(2 * 4096 * GROUP)

    def kernel(info, pieces, gathered, gain, copies, act_sum, grads):
        _, sums, mean, rstd = moments(gathered, count)
        value = pieces[...].astype(F32)
        chips = value.shape[0]
        seen = value[:, 14] + value[:, 15]
        norms = jnp.sum(seen, axis=0, keepdims=True)
        grads[...] = norms
        grad_gain, grad_bias = halves(norms)
        m1, m2 = slopes(norms, gain[...], count)
        centred = (sums - voxels * mean) * rstd
        act_sum[...] = rstd * (gain[...] * grad_bias - voxels * m1 - m2 * centred)
        own1, own2 = slopes(seen, gain[...], pair_count)
        delta1, delta2 = (own1 - m1) * rstd, (own2 - m2) * rstd
        ones = gathered[0:chips] + gathered[chips : 2 * chips]
        back = lax.dot_general(
            ones, delta1, (((0,), (0,)), ((), ())), preferred_element_type=F32, precision=lax.Precision.HIGHEST
        )
        back = [back[SHIFT_LANE + 2 * r : SHIFT_LANE + 2 * r + 1] for r in range(14)]
        back = jnp.concatenate(back + [jnp.zeros((2, 128), F32)], axis=0)
        total = jnp.sum(value + delta2[:, None] * pltpu.roll(value, 64, 2), axis=0) + back
        lane = lax.broadcasted_iota(jnp.int32, (7, 128), 1)
        both = jnp.where(lane < 64, total[:7], pltpu.roll(total[7:14], 64, 1))
        lost = both[6:7] - both[6:7].astype(BF).astype(F32)
        piece = jnp.concatenate([both, lost], axis=0).astype(BF)
        copies[...] = jnp.broadcast_to(piece[None], copies.shape)

    return kernel


def spread(info, near, far, conv, coarse, out, loss, rows):
    kz = lax.axis_index("cz")
    rows[pl.ds(pl.multiple_of(1024 * kz, 1024), 1024), :] = near[...].astype(F32).reshape(1024, 128)
    rows[pl.ds(pl.multiple_of(1024 * (1 - kz), 1024), 1024), :] = far[...].astype(F32).reshape(1024, 128)
    for tap in range(28):
        tile = rows[pl.ds(512 * (tap % 4) + tap // 4, 64, stride=8), :]
        if tap < 27:
            conv[tap] = tile[:, :64]
            coarse[tap] = tile[:, 64:]
        else:
            out[...] = tile[:, :64]
            parts = tile[0:1] + rows[2048 - 512 + 7 : 2048 - 512 + 8, :]
            lane = lax.broadcasted_iota(jnp.int32, (1, 128), 1)
            whole = jnp.sum(jnp.where((lane >= 64) & (lane < 68), parts, 0.0), axis=1, keepdims=True)
            loss[...] = jnp.broadcast_to(whole, (1, 128))


def exchange(rows):
    out = lax.all_to_all(rows.reshape(rows.shape[0], 1, 128), ("cz",) + CHIPS, 0, 0, tiled=True)
    return out.reshape(rows.shape)


def neighbours(down, up, axis):
    ends = lax.axis_size(axis) - 1
    before = lax.ppermute(up, axis, [(i, i + 1) for i in range(ends)])
    after = lax.ppermute(down, axis, [(i + 1, i) for i in range(ends)])
    return before, after


def time_embedding(timestep, width):
    halfway = width // 2
    indices = jnp.arange(halfway).astype(F32)
    freqs = jnp.exp(indices * (-math.log(10000.0) / halfway))
    angles = timestep[0].astype(F32) * freqs
    return jnp.concatenate([jnp.sin(angles), jnp.cos(angles)])


def twice(row):
    return jnp.concatenate([row, row]).reshape(1, 128)


def diagonal(square):
    nought = jnp.zeros_like(square)
    return jnp.block([[square, nought], [nought, square]])


def shards(latents, target, block_coords, timestep, conv_weight, coarse_weight, out_weight, time_weight, norm_gain, norm_bias):
    devices = lax.axis_size("bx") * lax.axis_size("by") * lax.axis_size("cz")
    voxels = devices * 4096
    core = lax.axis_index("cz").astype(jnp.int32)
    at = block_coords[0]
    info = block_coords
    lat = latents[0]
    lat_pairs = lat.reshape(16, 8, 2, 16, 64)

    mz, pooled = call(z_message, [like((33, 32, 64), BF), like((16, 64), BF)], [info, lat])
    rz = lax.ppermute(mz, "cz", [(0, 1), (1, 0)])
    plane = like((34, 32, 64), BF)
    down, up = call(y_messages, [plane, plane], [info, lat, lat, rz, pooled], (), [face_spec(1, 0), face_spec(1, 15)])
    rym, ryp = neighbours(down, up, "by")
    plane = like((37, 32, 64), BF)
    down, up = call(x_messages, [plane, plane], [info, lat, lat, rz, rym, ryp, pooled], (), [face_spec(0, 0), face_spec(0, 15)])
    rxm, rxp = neighbours(down, up, "bx")

    temb = time_embedding(timestep, time_weight.shape[0])
    time_bias = jnp.sum(temb[:, None] * time_weight.astype(F32), axis=0)
    taps = conv_weight.reshape(3, 3, 3, 64, 64).transpose(0, 2, 1, 3, 4)
    taps = jnp.stack(
        [jnp.pad(taps, ((0, 0), (0, 0), (b, 1 - b), (0, 0), (0, 0))) for b in range(2)], axis=4
    ).reshape(9 * 256, 128)
    combo = 8 * at[0] + 4 * at[1] + 2 * at[2] + core
    table = lax.dynamic_index_in_dim(jnp.asarray(coarse_table(), BF), combo, keepdims=False)

    raw, scene, columns = call(
        interior,
        [like((1792, 128), F32), like((3, 16, 9, 16, 128), BF), like((3, 9, 128), F32)],
        [info, lat_pairs, rz, rym, ryp, taps],
    )
    pair = (3, 2, 9, 16, 128)
    act, ends, patch, stats = call(
        forward,
        [like((2048, 128), F32), like((2, 3, 9, 16, 128), BF), like((16, 1728), BF), like((devices, 128), F32)],
        [info, scene, scene, raw, columns, rz, rym, ryp, rxm, rxp, pooled, table, taps]
        + [coarse_weight.reshape(1728, 64), twice(time_bias)],
        [pltpu.VMEM((2, 128, 128), F32)],
        [pl.BlockSpec(pair, lambda i: (0, 0, 0, 0, 0)), pl.BlockSpec(pair, lambda i: (0, 7, 0, 0, 0))],
    )
    first = exchange(stats)
    gain, bias = twice(norm_gain), twice(norm_bias)
    weights = [diagonal(out_weight), diagonal(out_weight.T)]
    predicted, payload = call(
        backward(voxels),
        [like((16, 8, 2, 16, 64), BF), like((2, 2048, 128), F32)],
        [info, act, first, target.reshape(16, 8, 2, 16, 64), gain, bias] + weights + [scene, ends, patch, stats],
        [pltpu.VMEM((256, 2048), BF)],
    )
    swap = [(0, 1), (1, 0)]
    chips = devices // 2
    other = lax.ppermute(payload[1], "cz", swap)
    (pieces,) = call(pair_add(voxels), [like((chips, 16, 128), BF)], [info, payload[0], other, first, gain])
    pieces = lax.all_to_all(pieces, CHIPS, 0, 0, tiled=True)
    copies, act_sum, grads = call(
        combine(voxels),
        [like((chips, 8, 128), BF), like((1, 128), F32), like((1, 128), F32)],
        [info, pieces, first, gain],
    )
    near = lax.all_to_all(copies, CHIPS, 0, 0, tiled=True)
    far = lax.ppermute(near, "cz", swap)
    grad_conv, grad_coarse, grad_out, loss = call(
        spread,
        [like((27, 64, 64), F32), like((27, 64, 64), F32), like((64, 64), F32), like((1, 128), F32)],
        [info, near, far],
        [pltpu.VMEM((2048, 128), F32)],
    )
    return (
        predicted.reshape(latents.shape),
        loss[0, :1] * (1.0 / (voxels * 64)),
        grad_conv,
        grad_coarse,
        grad_out,
        temb[:, None] * act_sum[:, :64],
        grads[0, :64],
        grads[0, 64:],
    )


def solution(mesh):
    blocks = P(ALL, None, None, None, None)
    return jax.shard_map(
        shards,
        mesh=mesh,
        in_specs=(blocks, blocks, P(ALL, None)) + (P(),) * 7,
        out_specs=(blocks,) + (P(),) * 7,
        check_vma=False,
    )
```

profile of v0, /device:TPU:1, one launch (start us, length us, event | category | flops | bytes accessed | tf_op | source)
XLA Modules:
  0.0 156.4 jit_solution(15470576444909664434)
XLA Ops:
  0.6 2.8 %shard_map.170 = (bf16[33,32,64]{2,1,0:T(8,128)(2,1)}, bf16[16,64]{1,0:T(8,128)(2,1)}) custom-call(s32[1,3]{1,0:T(1,128)} %info.17, bf16[16,16,16,64]{3,2,1,0:T(8,128)(2,1)} %bitcast.39), custom_call_target="tpu_custom_call" | custom-call | tf_op jit(solution)/shard_map/pallas_call | solution.py:30
  3.4 3.2 %collective-permute-start = (bf16[33,32,64]{2,1,0:T(8,128)(2,1)}, bf16[33,32,64]{2,1,0:T(8,128)(2,1)S(1)}, u32[]{:S(2)}, u32[]{:S(2)}) collective-permute-start(bf16[33,32,64]{2,1,0:T(8,128)(2,1)} %get-tuple-element.30), channel_id=1, source_target_pairs={{0,1},{1,0},{2,3},{3,2},{4,5},{5,4},{6,7},{7,6},{8,9},{9,8},{10,11... | collective-permute-start | bytes 405512 | tf_op jit(solution)/shard_map/ppermute | solution.py:606
  6.6 1.4 fusion.8
  8.7 0.9 multiply_reduce_fusion
  9.6 1.4 pad_bitcast_fusion.1
  11.7 1.9 %shard_map.171 = (bf16[34,32,64]{2,1,0:T(8,128)(2,1)}, bf16[34,32,64]{2,1,0:T(8,128)(2,1)}) custom-call(s32[1,3]{1,0:T(1,128)} %info.17, bf16[16,16,16,64]{3,2,1,0:T(8,128)(2,1)} %bitcast.40, bf16[16,16,16,64]{3,2,1,0:T(8,128)(2,1)} %bitcast.41, bf16[33,32,64]{2,1,0:T(8,128)(2,1)} %copy-done, bf16[16,64]{1,0:T(8,128)(2,1)} %get-tuple-element.31.pooled), custom_call_target="tpu_custom_call" | custom-call | tf_op jit(solution)/shard_map/pallas_call | solution.py:30
  13.7 1.8 %collective-permute-start.1 = (bf16[34,32,64]{2,1,0:T(8,128)(2,1)}, bf16[34,32,64]{2,1,0:T(8,128)(2,1)S(1)}, u32[]{:S(2)}, u32[]{:S(2)}) collective-permute-start(bf16[34,32,64]{2,1,0:T(8,128)(2,1)} %get-tuple-element.32), channel_id=1, source_target_pairs={{0,2},{2,4},{4,6},{6,8},{8,10},{10,12},{12,14},{1,3},{3,5},{5,7},{... | collective-permute-start | bytes 417800 | tf_op jit(solution)/shard_map/ppermute | solution.py:574
  15.5 1.3 collective-permute-start.2
  17.1 4.8 %collective-permute-done.1.rym = bf16[34,32,64]{2,1,0:T(8,128)(2,1)S(1)} collective-permute-done((bf16[34,32,64]{2,1,0:T(8,128)(2,1)}, bf16[34,32,64]{2,1,0:T(8,128)(2,1)S(1)}, u32[]{:S(2)}, u32[]{:S(2)}) %collective-permute-start.1) | collective-permute-done | bytes 139296 | tf_op jit(solution)/shard_map/ppermute | solution.py:574
  21.9 4.1 %collective-permute-done.2.ryp = bf16[34,32,64]{2,1,0:T(8,128)(2,1)S(1)} collective-permute-done((bf16[34,32,64]{2,1,0:T(8,128)(2,1)}, bf16[34,32,64]{2,1,0:T(8,128)(2,1)S(1)}, u32[]{:S(2)}, u32[]{:S(2)}) %collective-permute-start.2) | collective-permute-done | bytes 139296 | tf_op jit(solution)/shard_map/ppermute | solution.py:575
  26.7 2.2 %shard_map.173 = (bf16[37,32,64]{2,1,0:T(8,128)(2,1)}, bf16[37,32,64]{2,1,0:T(8,128)(2,1)}) custom-call(s32[1,3]{1,0:T(1,128)} %info.17, bf16[16,16,16,64]{3,2,1,0:T(8,128)(2,1)} %bitcast.42, bf16[16,16,16,64]{3,2,1,0:T(8,128)(2,1)} %bitcast.43, bf16[33,32,64]{2,1,0:T(8,128)(2,1)} %copy-done, bf16[34,32,64]{2,1,0:T(8,128)(2,1)} %copy-done.1, ...), custom_call_target="tpu_custom_call" | custom-call | tf_op jit(solution)/shard_map/pallas_call | solution.py:30
  28.9 3.1 %collective-permute-start.3 = (bf16[37,32,64]{2,1,0:T(8,128)(2,1)}, bf16[37,32,64]{2,1,0:T(8,128)(2,1)S(1)}, u32[]{:S(2)}, u32[]{:S(2)}) collective-permute-start(bf16[37,32,64]{2,1,0:T(8,128)(2,1)} %get-tuple-element.37), channel_id=1, source_target_pairs={{0,16},{16,32},{32,48},{48,64},{64,80},{80,96},{96,112},{112,128},... | collective-permute-start | bytes 454664 | tf_op jit(solution)/shard_map/ppermute | solution.py:574
  32.0 1.3 collective-permute-start.4
  35.9 1.2 copy.30
  37.1 1.4 reshape.65.weight
  38.5 1.6 dynamic-slice_bitcast_fusion.table
  40.1 5.3 %shard_map.172 = (f32[1792,128]{1,0:T(8,128)}, bf16[3,16,9,16,128]{4,3,2,1,0:T(8,128)(2,1)}, f32[3,9,128]{2,1,0:T(8,128)}) custom-call(s32[1,3]{1,0:T(1,128)} %info.17, bf16[16,8,2,16,64]{4,3,2,1,0:T(8,128)(2,1)} %bitcast.44, bf16[33,32,64]{2,1,0:T(8,128)(2,1)} %copy-done, bf16[34,32,64]{2,1,0:T(8,128)(2,1)} %copy-done.1, bf16[34,32,64]{2,1,0:T(8,128)(2,1)} %copy-done.2, ...), custom_call_target="tpu_custom_call" | custom-call | tf_op jit(solution)/shard_map/pallas_call | solution.py:30
  46.2 4.1 %shard_map.174 = (f32[2048,128]{1,0:T(8,128)}, bf16[2,3,9,16,128]{4,3,2,1,0:T(8,128)(2,1)}, bf16[16,1728]{1,0:T(8,128)(2,1)}, f32[256,128]{1,0:T(8,128)}) custom-call(s32[1,3]{1,0:T(1,128)} %info.17, bf16[3,16,9,16,128]{4,3,2,1,0:T(8,128)(2,1)} %get-tuple-element.34.near_low.near_high.scene, ...), custom_call_target="tpu_custom_call" | custom-call | tf_op jit(solution)/shard_map/pallas_call | solution.py:30
  50.4 16.2 %all-to-all-start = ((f32[256,1,128]{2,1,0:T(1,128)}), f32[256,1,128]{2,1,0:T(1,128)S(1)}, u32[]{:S(2)}, u32[]{:S(2)}) async-start(f32[256,1,128]{2,1,0:T(1,128)} %bitcast.49), calls=%async_computation | async-start | bytes 262144 | tf_op jit(solution)/shard_map/all_to_all | solution.py:568
  68.0 11.4 %all-to-all-done = f32[256,1,128]{2,1,0:T(1,128)S(1)} async-done(((f32[256,1,128]{2,1,0:T(1,128)}), f32[256,1,128]{2,1,0:T(1,128)S(1)}, u32[]{:S(2)}, u32[]{:S(2)}) %all-to-all-start) | async-done | bytes 131104 | tf_op jit(solution)/shard_map/all_to_all | solution.py:568
  80.0 8.8 %shard_map.175 = (bf16[16,8,2,16,64]{4,3,2,1,0:T(8,128)(2,1)}, f32[2,2048,128]{2,1,0:T(8,128)}) custom-call(s32[1,3]{1,0:T(1,128)} %info.17, f32[2048,128]{1,0:T(8,128)} %get-tuple-element.39.act, f32[256,128]{1,0:T(8,128)} %bitcast.45, bf16[16,8,2,16,64]{4,3,2,1,0:T(8,128)(2,1)} %bitcast.48, f32[1,128]{1,0:T(1,128)} %get-tuple-element.65.gain, ...), custom_call_target="tpu_custom_call" | custom-call | tf_op jit(solution)/shard_map/pallas_call | solution.py:30
  88.9 2.7 %slice_bitcast_fusion = (f32[2048,128]{1,0:T(8,128)S(1)}, f32[2048,128]{1,0:T(8,128)}) fusion(f32[2,2048,128]{2,1,0:T(8,128)} %get-tuple-element.44), kind=kLoop, calls=%fused_computation.1 | loop fusion | bytes 4194304 | tf_op jit(solution)/shard_map/squeeze | solution.py:648
  92.2 2.3 %collective-permute-done.5.other = f32[2048,128]{1,0:T(8,128)S(1)} collective-permute-done((f32[2048,128]{1,0:T(8,128)S(1)}, f32[2048,128]{1,0:T(8,128)S(1)}, u32[]{:S(2)}, u32[]{:S(2)}) %collective-permute-start.5) | collective-permute-done | bytes 1048608 | tf_op jit(solution)/shard_map/ppermute | solution.py:648
  94.5 1.0 copy-done.4
  95.4 3.2 %shard_map.176 = bf16[128,16,128]{2,1,0:T(8,128)(2,1)} custom-call(s32[1,3]{1,0:T(1,128)} %info.17, f32[2048,128]{1,0:T(8,128)} %get-tuple-element.53.mine, f32[2048,128]{1,0:T(8,128)} %copy-done.4, f32[256,128]{1,0:T(8,128)} %bitcast.46, f32[1,128]{1,0:T(1,128)} %get-tuple-element.65.gain), custom_call_target="tpu_custom_call" | custom-call | tf_op jit(solution)/shard_map/pallas_call | solution.py:30
  98.6 26.7 %all_to_all.15.pieces = bf16[128,16,128]{2,1,0:T(8,128)(2,1)} all-to-all(bf16[128,16,128]{2,1,0:T(8,128)(2,1)} %shard_map.176), channel_id=1, replica_groups=mesh['bx'=16,'by'=8,'cz'=2] {'bx','by'}, dimensions={0} | all-to-all | bytes 1048576 | tf_op jit(solution)/shard_map/all_to_all | solution.py:650
  125.4 2.5 %shard_map.177 = (bf16[128,8,128]{2,1,0:T(8,128)(2,1)}, f32[1,128]{1,0:T(1,128)}, f32[1,128]{1,0:T(1,128)}) custom-call(s32[1,3]{1,0:T(1,128)} %info.17, bf16[128,16,128]{2,1,0:T(8,128)(2,1)} %all_to_all.15.pieces, f32[256,128]{1,0:T(8,128)} %bitcast.47, f32[1,128]{1,0:T(1,128)} %get-tuple-element.65.gain), custom_call_target="tpu_custom_call" | custom-call | tf_op jit(solution)/shard_map/pallas_call | solution.py:30
  127.8 6.2 %all-to-all-start.2 = ((bf16[128,8,128]{2,1,0:T(8,128)(2,1)}), bf16[128,8,128]{2,1,0:T(8,128)(2,1)S(1)}, u32[]{:S(2)}, u32[]{:S(2)}) async-start(bf16[128,8,128]{2,1,0:T(8,128)(2,1)} %get-tuple-element.45), calls=%async_computation.2 | async-start | bytes 524288 | tf_op jit(solution)/shard_map/all_to_all | solution.py:656
  134.0 1.3 slice_bitcast_fusion.2
  135.3 11.4 %all-to-all-done.2.near = bf16[128,8,128]{2,1,0:T(8,128)(2,1)S(1)} async-done(((bf16[128,8,128]{2,1,0:T(8,128)(2,1)}), bf16[128,8,128]{2,1,0:T(8,128)(2,1)S(1)}, u32[]{:S(2)}, u32[]{:S(2)}) %all-to-all-start.2) | async-done | bytes 262176 | tf_op jit(solution)/shard_map/all_to_all | solution.py:656
  146.8 3.3 %collective-permute-start.6 = (bf16[128,8,128]{2,1,0:T(8,128)(2,1)S(1)}, bf16[128,8,128]{2,1,0:T(8,128)(2,1)S(1)}, u32[]{:S(2)}, u32[]{:S(2)}) collective-permute-start(bf16[128,8,128]{2,1,0:T(8,128)(2,1)S(1)} %all-to-all-done.2.near), channel_id=1, source_target_pairs={{0,1},{1,0},{2,3},{3,2},{4,5},{5,4},{6,7},{7,6},{8,9},{9,8},{10,11... | collective-permute-start | bytes 786440 | tf_op jit(solution)/shard_map/ppermute | solution.py:657
  152.1 2.5 %shard_map.178 = (f32[27,64,64]{2,1,0:T(8,128)}, f32[27,64,64]{2,1,0:T(8,128)}, f32[64,64]{1,0:T(8,128)}, f32[1,128]{1,0:T(1,128)}) custom-call(s32[1,3]{1,0:T(1,128)} %info.17, bf16[128,8,128]{2,1,0:T(8,128)(2,1)} %copy-done.5, bf16[128,8,128]{2,1,0:T(8,128)(2,1)} %copy-done.8), custom_call_target="tpu_custom_call" | custom-call | tf_op jit(solution)/shard_map/pallas_call | solution.py:30
  (37 shorter events, 8.0 us)
Async XLA Ops:
  3.4 7.6 %collective-permute-start = (bf16[33,32,64]{2,1,0:T(8,128)(2,1)}, bf16[33,32,64]{2,1,0:T(8,128)(2,1)S(1)}, u32[]{:S(2)}, u32[]{:S(2)}) collective-permute-start(bf16[33,32,64]{2,1,0:T(8,128)(2,1)} %get-tuple-element.30), channel_id=1, source_target_pairs={{0,1},{1,0},{2,3},{3,2},{4,5},{5,4},{6,7},{7,6},{8,9},{9,8},{10,11... | collective-permute-start | bytes 405512 | tf_op jit(solution)/shard_map/ppermute | solution.py:606
  11.0 0.7 copy-start
  13.7 8.2 %collective-permute-start.1 = (bf16[34,32,64]{2,1,0:T(8,128)(2,1)}, bf16[34,32,64]{2,1,0:T(8,128)(2,1)S(1)}, u32[]{:S(2)}, u32[]{:S(2)}) collective-permute-start(bf16[34,32,64]{2,1,0:T(8,128)(2,1)} %get-tuple-element.32), channel_id=1, source_target_pairs={{0,2},{2,4},{4,6},{6,8},{8,10},{10,12},{12,14},{1,3},{3,5},{5,7},{... | collective-permute-start | bytes 417800 | tf_op jit(solution)/shard_map/ppermute | solution.py:574
  15.5 10.4 %collective-permute-start.2 = (bf16[34,32,64]{2,1,0:T(8,128)(2,1)}, bf16[34,32,64]{2,1,0:T(8,128)(2,1)S(1)}, u32[]{:S(2)}, u32[]{:S(2)}) collective-permute-start(bf16[34,32,64]{2,1,0:T(8,128)(2,1)} %get-tuple-element.33), channel_id=1, source_target_pairs={{2,0},{4,2},{6,4},{8,6},{10,8},{12,10},{14,12},{3,1},{5,3},{7,5},{... | collective-permute-start | bytes 417800 | tf_op jit(solution)/shard_map/ppermute | solution.py:575
  21.9 4.1 %copy-start.1 = (bf16[34,32,64]{2,1,0:T(8,128)(2,1)}, bf16[34,32,64]{2,1,0:T(8,128)(2,1)S(1)}, u32[]{:S(2)}) copy-start(bf16[34,32,64]{2,1,0:T(8,128)(2,1)S(1)} %collective-permute-done.1.rym) | copy-start | bytes 417796
  25.9 0.7 copy-start.2
  28.9 16.6 %collective-permute-start.3 = (bf16[37,32,64]{2,1,0:T(8,128)(2,1)}, bf16[37,32,64]{2,1,0:T(8,128)(2,1)S(1)}, u32[]{:S(2)}, u32[]{:S(2)}) collective-permute-start(bf16[37,32,64]{2,1,0:T(8,128)(2,1)} %get-tuple-element.37), channel_id=1, source_target_pairs={{0,16},{16,32},{32,48},{48,64},{64,80},{80,96},{96,112},{112,128},... | collective-permute-start | bytes 454664 | tf_op jit(solution)/shard_map/ppermute | solution.py:574
  32.0 13.4 %collective-permute-start.4 = (bf16[37,32,64]{2,1,0:T(8,128)(2,1)}, bf16[37,32,64]{2,1,0:T(8,128)(2,1)S(1)}, u32[]{:S(2)}, u32[]{:S(2)}) collective-permute-start(bf16[37,32,64]{2,1,0:T(8,128)(2,1)} %get-tuple-element.38), channel_id=1, source_target_pairs={{16,0},{32,16},{48,32},{64,48},{80,64},{96,80},{112,96},{128,112},... | collective-permute-start | bytes 454664 | tf_op jit(solution)/shard_map/ppermute | solution.py:575
  45.4 0.7 copy-start.6
  45.4 0.8 copy-start.7
  46.2 20.3 %copy-start.9 = (bf16[64,64]{1,0:T(8,128)(2,1)S(1)}, bf16[64,64]{1,0:T(8,128)(2,1)}, u32[]{:S(2)}) copy-start(bf16[64,64]{1,0:T(8,128)(2,1)} %param.17) | copy-start | bytes 24580
  46.2 20.4 %copy-start.10 = (f32[64]{0:T(128)S(1)}, f32[64]{0:T(128)}, u32[]{:S(2)}) copy-start(f32[64]{0:T(128)} %param.19) | copy-start | bytes 772
  46.2 20.4 %copy-start.11 = (f32[64]{0:T(128)S(1)}, f32[64]{0:T(128)}, u32[]{:S(2)}) copy-start(f32[64]{0:T(128)} %param.20) | copy-start | bytes 772
  50.4 29.0 %all-to-all-start = ((f32[256,1,128]{2,1,0:T(1,128)}), f32[256,1,128]{2,1,0:T(1,128)S(1)}, u32[]{:S(2)}, u32[]{:S(2)}) async-start(f32[256,1,128]{2,1,0:T(1,128)} %bitcast.49), calls=%async_computation | async-start | bytes 262144 | tf_op jit(solution)/shard_map/all_to_all | solution.py:568
  79.4 0.7 copy-start.3
  91.5 2.9 %collective-permute-start.5 = (f32[2048,128]{1,0:T(8,128)S(1)}, f32[2048,128]{1,0:T(8,128)S(1)}, u32[]{:S(2)}, u32[]{:S(2)}) collective-permute-start(f32[2048,128]{1,0:T(8,128)S(1)} %get-tuple-element.52), channel_id=1, source_target_pairs={{0,1},{1,0},{2,3},{3,2},{4,5},{5,4},{6,7},{7,6},{8,9},{9,8},{10,11... | collective-permute-start | bytes 3145736 | tf_op jit(solution)/shard_map/ppermute | solution.py:648
  94.5 1.0 copy-start.4
  127.8 18.9 %all-to-all-start.2 = ((bf16[128,8,128]{2,1,0:T(8,128)(2,1)}), bf16[128,8,128]{2,1,0:T(8,128)(2,1)S(1)}, u32[]{:S(2)}, u32[]{:S(2)}) async-start(bf16[128,8,128]{2,1,0:T(8,128)(2,1)} %get-tuple-element.45), calls=%async_computation.2 | async-start | bytes 524288 | tf_op jit(solution)/shard_map/all_to_all | solution.py:656
  146.8 4.6 %copy-start.5 = (bf16[128,8,128]{2,1,0:T(8,128)(2,1)}, bf16[128,8,128]{2,1,0:T(8,128)(2,1)S(1)}, u32[]{:S(2)}) copy-start(bf16[128,8,128]{2,1,0:T(8,128)(2,1)S(1)} %all-to-all-done.2.near) | copy-start | bytes 786436
  146.8 4.6 %collective-permute-start.6 = (bf16[128,8,128]{2,1,0:T(8,128)(2,1)S(1)}, bf16[128,8,128]{2,1,0:T(8,128)(2,1)S(1)}, u32[]{:S(2)}, u32[]{:S(2)}) collective-permute-start(bf16[128,8,128]{2,1,0:T(8,128)(2,1)S(1)} %all-to-all-done.2.near), channel_id=1, source_target_pairs={{0,1},{1,0},{2,3},{3,2},{4,5},{5,4},{6,7},{7,6},{8,9},{9,8},{10,11... | collective-permute-start | bytes 786440 | tf_op jit(solution)/shard_map/ppermute | solution.py:657
  151.4 0.7 copy-start.8
where the time goes:
time: 157 us; the launch traced here: 156 us
  starting transfers between devices  37 us (24%)
  waiting for transfers between devices  34 us (22%)
  Pallas kernels  33.4 us (21%)
  blocking collectives  26.7 us (17%)
  local copies, waits for them, and re-layouts  16.3 us (10%)
  between operations  5.18 us (3%)
  other arithmetic  3.85 us (2%)
    pallas_call x9, Pallas kernels, call(): pl.pallas_call(kernel, grid=(1,), out_shape=outs, in_specs=[pl.BlockSpec(...  33.4 us
    all_to_all x1, blocking collectives, shards(): pieces = lax.all_to_all(pieces, CHIPS, 0, 0, tiled=True)  26.7 us
    all_to_all x1, starting transfers between devices, exchange(): lax.all_to_all(rows.reshape(rows.shape[0], 1, 128), ('cz',) + CHIPS, 0, 0...  16.2 us
    all_to_all x1, waiting for transfers between devices, shards(): near = lax.all_to_all(copies, CHIPS, 0, 0, tiled=True)  11.4 us
    all_to_all x1, waiting for transfers between devices, exchange(): lax.all_to_all(rows.reshape(rows.shape[0], 1, 128), ('cz',) + CHIPS, 0, 0...  11.4 us
    all_to_all x1, starting transfers between devices, shards(): near = lax.all_to_all(copies, CHIPS, 0, 0, tiled=True)  6.18 us
    ppermute x2, starting transfers between devices, neighbours(): before = lax.ppermute(up, axis, [(i, i + 1) for i in range(ends)])  4.93 us
    ppermute x2, waiting for transfers between devices, neighbours(): before = lax.ppermute(up, axis, [(i, i + 1) for i in range(ends)])  4.8 us
  transfers between devices with their start and end apart: 9, of which 5 were waited for; matrix products, arithmetic and copies ran while one was open for 8% of the time, Pallas kernels for 3%

commit v1 on v0

--- a/solution.py
+++ b/solution.py
@@ -1,3 +1,4 @@
+import functools
 import math
 
 import jax
@@ -24,15 +25,16 @@
     return pl.BlockSpec(shape, lambda i: where)
 
 
-def call(kernel, outs, args, scratch=(), faces=()):
+def call(kernel, outs, args, scratch=(), faces=(), far_args=0, far_outs=0):
     vmem = pl.BlockSpec(memory_space=pltpu.VMEM)
-    specs = list(faces) + [vmem] * (len(args) - 1 - len(faces))
+    far = pl.BlockSpec(memory_space=pl.ANY)
+    specs = list(faces) + [vmem] * (len(args) - 1 - len(faces) - far_args) + [far] * far_args
     return pl.pallas_call(
         kernel,
         grid=(1,),
         out_shape=outs,
         in_specs=[pl.BlockSpec(memory_space=pltpu.SMEM)] + specs,
-        out_specs=[vmem] * len(outs),
+        out_specs=[vmem] * (len(outs) - far_outs) + [far] * far_outs,
         scratch_shapes=list(scratch),
         compiler_params=pltpu.CompilerParams(vmem_limit_bytes=VMEM_LIMIT),
     )(*args)
@@ -67,17 +69,53 @@
     return cells[p : p + 1]
 
 
+Z_TILES, Y_TILES, X_TILES = 1, 2, 5
+
+
+def message(tiles):
+    return like((9 + tiles, 16, 128), BF)
+
+
+def plane(tiles):
+    return pltpu.VMEM((32 + tiles, 32, 64), BF)
+
+
+def side_by_side(rows):
+    half = rows.shape[0] // 2
+    return jnp.concatenate([rows[:half], rows[half:]], axis=rows.ndim - 1)
+
+
+def write_message(out, face, tiles, first, second, on):
+    out[0:8] = side_by_side(face)
+    for t, rows in enumerate(tiles):
+        out[8 + t] = side_by_side(rows).astype(BF)
+    row = lax.broadcasted_iota(jnp.int32, (16, 128), 0)
+    here = jnp.where(on, 2 * first + second, 99)
+    out[8 + len(tiles)] = jnp.where(row == here, 1.0, 0.0).astype(BF)
+
+
+def open_message(ref, out):
+    tiles = ref.shape[0] - 9
+    face = jnp.concatenate([ref[0:8, :, :64], ref[0:8, :, 64:]], axis=0)
+    flags = ref[8 + tiles].astype(F32)
+    for q in range(4):
+        here = jnp.broadcast_to(flags[q : q + 1, :64], (16, 64))[None]
+        out[16 * (q // 2) : 16 * (q // 2) + 16, 16 * (q % 2) : 16 * (q % 2) + 16, :] = jnp.where(
+            here > 0.5, face.astype(F32), 0.0
+        ).astype(BF)
+    for t in range(tiles):
+        out[32 + t] = jnp.concatenate([ref[8 + t, :, :64], ref[8 + t, :, 64:]], axis=0)
+
+
 def z_message(info, lat, out, pooled):
     px, py, pz, kz = bits(info)
-    on = pz == 1 - kz
     zsel = 15 * (1 - kz)
-    out[...] = jnp.zeros(out.shape, BF)
     pick = lax.broadcasted_iota(jnp.int32, (16, 16, 64), 1) == zsel
     sums = [[None, None], [None, None]]
+    faces = []
     for y in range(16):
         slab = lat[:, y].astype(F32)
-        face = jnp.sum(jnp.where(pick, slab, 0.0), axis=1)
-        out[py * 16 + y, pl.ds(start16(px), 16), :] = keep(on, face).astype(BF)
+        faces.append(jnp.sum(jnp.where(pick, slab, 0.0), axis=1)[None])
         for a in range(2):
             part = jnp.sum(slab[8 * a : 8 * a + 8], axis=0)
             old = sums[a][y // 8]
@@ -90,31 +128,32 @@
     cells = jnp.concatenate(cells, axis=0) * (1.0 / math.sqrt(512.0))
     cells = cells.astype(BF).astype(F32)
     pooled[...] = jnp.concatenate([cells, jnp.zeros((8, 64), F32)], axis=0).astype(BF)
+    on = pz == 1 - kz
     face = [
         [jnp.where(kz == 0, row_of(cells, 4 * a + 2 * b + 1), row_of(cells, 4 * a + 2 * b)) for a in range(2)]
         for b in range(2)
     ]
-    rows = cell_rows(py, px, face, on)
-    out[32] = jnp.concatenate([rows, jnp.zeros((16, 64), F32)], axis=0).astype(BF)
-
-
-def y_messages(info, low, high, rz, pooled, down, up):
+    rows = jnp.concatenate([cell_rows(py, px, face, on), jnp.zeros((16, 64), F32)], axis=0)
+    write_message(out, jnp.concatenate(faces, axis=0).astype(BF), [rows], py, px, on)
+
+
+def y_messages(info, low, high, rz_in, pooled, down, up, rz):
     px, py, pz, kz = bits(info)
+    open_message(rz_in, rz)
     cells = pooled[...].astype(F32)
     halo = rz[32].astype(F32)
     for out, face, bit, line, q in ((down, low, 0, 0, 0), (up, high, 1, 31, 1)):
         on = py == bit
-        out[...] = jnp.zeros(out.shape, BF)
-        out[pl.ds(start16(px), 16), pl.ds(start16(pz), 16), :] = keep(on, face[:, 0])
-        out[32] = rz[line]
         picked = [[row_of(cells, 4 * a + 2 * q + c) for c in range(2)] for a in range(2)]
-        rows = cell_rows(px, pz, picked, on)
         tail = halo[12:16] if q else halo[0:4]
-        out[33] = jnp.concatenate([rows, tail, jnp.zeros((12, 64), F32)], axis=0).astype(BF)
-
-
-def x_messages(info, low, high, rz, rym, ryp, pooled, down, up):
+        rows = jnp.concatenate([cell_rows(px, pz, picked, on), tail, jnp.zeros((12, 64), F32)], axis=0)
+        write_message(out, face[:, 0], [rz[line], rows], px, pz, on)
+
+
+def x_messages(info, low, high, rz_in, rym_in, ryp_in, pooled, down, up, rz, rym, ryp):
     px, py, pz, kz = bits(info)
+    for ref, out in ((rz_in, rz), (rym_in, rym), (ryp_in, ryp)):
+        open_message(ref, out)
     cells = pooled[...].astype(F32)
     halo = rz[32].astype(F32)
     halo_m = rym[33].astype(F32)
@@ -124,21 +163,17 @@
     where16 = lax.broadcasted_iota(jnp.int32, (32, 16, 64), 1)
     for out, face, bit, line, q in ((down, low, 0, 0, 0), (up, high, 1, 31, 1)):
         on = px == bit
-        out[...] = jnp.zeros(out.shape, BF)
-        out[pl.ds(start16(py), 16), pl.ds(start16(pz), 16), :] = keep(on, face[0])
         slab = rz[0:32, 16 * q : 16 * q + 16, :].astype(F32)
-        out[32] = jnp.sum(jnp.where(where16 == 15 * q, slab, 0.0), axis=1).astype(BF)
-        out[33] = rym[line]
-        out[34] = ryp[line]
+        z_line = jnp.sum(jnp.where(where16 == 15 * q, slab, 0.0), axis=1).astype(BF)
         picked = [[row_of(cells, 4 * q + 2 * b + c) for c in range(2)] for b in range(2)]
-        rows = cell_rows(py, pz, picked, on)
         corners = [line_m[line : line + 1], line_p[line : line + 1], jnp.zeros((14, 64), F32)]
-        out[35] = jnp.concatenate(corners + [rows], axis=0).astype(BF)
+        corners = jnp.concatenate(corners + [cell_rows(py, pz, picked, on)], axis=0)
         c0 = 3 * q
         parts = [row_of(halo, 4 * cy + c0) for cy in range(4)]
         parts += [halo_m[4 * c0 : 4 * c0 + 4], halo_p[4 * c0 : 4 * c0 + 4]]
         parts += [row_of(halo_m, 16 + c0), row_of(halo_p, 16 + c0), jnp.zeros((18, 64), F32)]
-        out[36] = jnp.concatenate(parts, axis=0).astype(BF)
+        tiles = [z_line, rym[line], ryp[line], corners, jnp.concatenate(parts, axis=0)]
+        write_message(out, face[0], tiles, py, pz, on)
 
 
 def coarse_table():
@@ -217,7 +252,16 @@
     return ref[i].astype(F32)[j : j + 1]
 
 
-def interior(info, lat, rz, rym, ryp, weight, raw, scene, columns):
+def interior(info, lat, rz_in, rym_in, ryp_in, taps, raw, scene, columns, weight, rz, rym, ryp):
+    for ref, out in ((rz_in, rz), (rym_in, rym), (ryp_in, ryp)):
+        open_message(ref, out)
+    nought = jnp.zeros((64, 64), BF)
+    for tap in range(9):
+        ox, oz = tap // 3, tap % 3
+        for a in range(4):
+            left = nought if a == 3 else taps[9 * ox + 3 * a + oz]
+            right = nought if a == 0 else taps[9 * ox + 3 * a - 3 + oz]
+            weight[256 * tap + 64 * a : 256 * tap + 64 * a + 64] = jnp.concatenate([left, right], axis=1)
     w = Window(info, rz, rym, ryp)
     y_low = keep(w.ylo, rym[w.xs, w.z0, :])
     y_high = keep(w.yhi, ryp[w.xs, w.z0, :])
@@ -255,7 +299,16 @@
         raw[(first - 1) * 128 : (first - 1 + count) * 128] = value
 
 
-def forward(info, near_low, near_high, raw, columns, rz, rym, ryp, rxm, rxp, pooled, table, weight, coarse_weight, time_bias, act, ends, patch_out, stats, shift):
+def forward(
+    info, near_low, near_high, raw, columns, rz_in, rym_in, ryp_in, rxm_in, rxp_in, pooled, weight,
+    coarse_weight, temb, time_weight, tables, act, ends, patch_out, stats,
+    shift, table, arrived, rz, rym, ryp, rxm, rxp
+):
+    px, py, pz, kz = bits(info)
+    fetch = pltpu.make_async_copy(tables.at[8 * px + 4 * py + 2 * pz + kz], table, arrived)
+    fetch.start()
+    for ref, out in ((rz_in, rz), (rym_in, rym), (ryp_in, ryp), (rxm_in, rxm), (rxp_in, rxp)):
+        open_message(ref, out)
     w = Window(info, rz, rym, ryp)
     nought = jnp.zeros((16, 64), BF)
 
@@ -313,16 +366,25 @@
         [pooled[...], rz[32, 0:16, :], rym[33], ryp[33], rxm[35, 16:32, :], rxm[36, 0:16, :], rxp[35, 16:32, :], rxp[36, 0:16, :]],
         axis=0,
     )
+    fetch.wait()
     taps = jnp.dot(table[...], source, preferred_element_type=F32)
     patch = jnp.concatenate([taps[8 * t : 8 * t + 8] for t in range(27)], axis=1)
     patch_out[...] = jnp.concatenate([patch, patch], axis=0).astype(BF)
     coarse = jnp.dot(patch_out[...], coarse_weight[...], preferred_element_type=F32)
     coarse = coarse.astype(BF).astype(F32)
     coarse = jnp.concatenate([coarse, coarse], axis=1)
+    time_bias = lax.dot_general(
+        jnp.broadcast_to(temb[...], (8, 256)),
+        time_weight[...].astype(F32),
+        (((1,), (1,)), ((), ())),
+        preferred_element_type=F32,
+        precision=lax.Precision.HIGHEST,
+    )[:1]
+    time_bias = jnp.concatenate([time_bias, time_bias], axis=1)
     z_half = lax.broadcasted_iota(jnp.int32, (16, 128), 0) < 8
     added = []
     for q in range(4):
-        added.append(jnp.where(z_half, coarse[2 * q : 2 * q + 1], coarse[2 * q + 1 : 2 * q + 2]) + time_bias[...])
+        added.append(jnp.where(z_half, coarse[2 * q : 2 * q + 1], coarse[2 * q + 1 : 2 * q + 2]) + time_bias)
 
     pieces = []
     for tap in range(9):
@@ -401,7 +463,7 @@
     count = float(voxels * GROUP)
     scale = 1.0 / (voxels * 64)
 
-    def kernel(info, act, gathered, target, gain, bias, weight, weight_t, scene, ends, patch, stats, predicted, payload, cotangent):
+    def kernel(info, act, gathered, target, gain, bias, weight, weight_t, scene, ends, patch, stats, predicted, mine, other, cotangent, payload, sent):
         kz = lax.axis_index("cz")
         _, _, mean, rstd = moments(gathered, count)
         gains = jnp.zeros((1, 128), F32)
@@ -476,8 +538,8 @@
         loss = jnp.broadcast_to(jnp.sum(lost, axis=1, keepdims=True), (64, 128))
         high = loss.astype(BF).astype(F32)
         lane = lax.broadcasted_iota(jnp.int32, (64, 128), 1)
-        mine = jnp.where(lane == 2 * kz, high, jnp.where(lane == 2 * kz + 1, loss - high, 0.0))
-        store(27, 7, mine)
+        split = jnp.where(lane == 2 * kz, high, jnp.where(lane == 2 * kz + 1, loss - high, 0.0))
+        store(27, 7, split)
         lane = lax.broadcasted_iota(jnp.int32, (1, 128), 1)
         row = jnp.where(lane < 64, gains + pltpu.roll(gains, 64, 1), biases + pltpu.roll(biases, 64, 1))
         wide = jnp.broadcast_to(row, (128, 128))
@@ -485,6 +547,11 @@
             payload.at[half][pl.ds(14, 128, stride=16), :] = wide
             slot = jnp.where(kz == half, 0, 1)
             payload.at[slot][pl.ds(15, 128, stride=16), :] = stats[128 * half : 128 * half + 128]
+        copies = [pltpu.make_async_copy(payload.at[n], ref, sent.at[n]) for n, ref in ((0, mine), (1, other))]
+        for copy in copies:
+            copy.start()
+        for copy in copies:
+            copy.wait()
 
     return kernel
 
@@ -518,17 +585,20 @@
     count = float(voxels * GROUP)
     pair_count = float(2 * 4096 * GROUP)
 
-    def kernel(info, pieces, gathered, gain, copies, act_sum, grads):
+    def kernel(info, pieces, gathered, gain, temb, copies, grad_time, gain_out, bias_out):
         _, sums, mean, rstd = moments(gathered, count)
         value = pieces[...].astype(F32)
         chips = value.shape[0]
         seen = value[:, 14] + value[:, 15]
         norms = jnp.sum(seen, axis=0, keepdims=True)
-        grads[...] = norms
         grad_gain, grad_bias = halves(norms)
+        gain_out[...] = grad_gain[:, :64]
+        bias_out[...] = grad_bias[:, :64]
         m1, m2 = slopes(norms, gain[...], count)
         centred = (sums - voxels * mean) * rstd
-        act_sum[...] = rstd * (gain[...] * grad_bias - voxels * m1 - m2 * centred)
+        act_sum = rstd * (gain[...] * grad_bias - voxels * m1 - m2 * centred)
+        column = jnp.broadcast_to(act_sum, (128, 128)).T[:64]
+        grad_time[...] = jnp.concatenate([column, column], axis=1) * temb[...]
         own1, own2 = slopes(seen, gain[...], pair_count)
         delta1, delta2 = (own1 - m1) * rstd, (own2 - m2) * rstd
         ones = gathered[0:chips] + gathered[chips : 2 * chips]
@@ -547,7 +617,7 @@
     return kernel
 
 
-def spread(info, near, far, conv, coarse, out, loss, rows):
+def spread(scale, info, near, far, conv, coarse, out, loss, rows):
     kz = lax.axis_index("cz")
     rows[pl.ds(pl.multiple_of(1024 * kz, 1024), 1024), :] = near[...].astype(F32).reshape(1024, 128)
     rows[pl.ds(pl.multiple_of(1024 * (1 - kz), 1024), 1024), :] = far[...].astype(F32).reshape(1024, 128)
@@ -561,7 +631,7 @@
             parts = tile[0:1] + rows[2048 - 512 + 7 : 2048 - 512 + 8, :]
             lane = lax.broadcasted_iota(jnp.int32, (1, 128), 1)
             whole = jnp.sum(jnp.where((lane >= 64) & (lane < 68), parts, 0.0), axis=1, keepdims=True)
-            loss[...] = jnp.broadcast_to(whole, (1, 128))
+            loss[...] = whole * scale
 
 
 def exchange(rows):
@@ -596,80 +666,85 @@
 def shards(latents, target, block_coords, timestep, conv_weight, coarse_weight, out_weight, time_weight, norm_gain, norm_bias):
     devices = lax.axis_size("bx") * lax.axis_size("by") * lax.axis_size("cz")
     voxels = devices * 4096
-    core = lax.axis_index("cz").astype(jnp.int32)
-    at = block_coords[0]
     info = block_coords
     lat = latents[0]
     lat_pairs = lat.reshape(16, 8, 2, 16, 64)
 
-    mz, pooled = call(z_message, [like((33, 32, 64), BF), like((16, 64), BF)], [info, lat])
+    mz, pooled = call(z_message, [message(Z_TILES), like((16, 64), BF)], [info, lat])
     rz = lax.ppermute(mz, "cz", [(0, 1), (1, 0)])
-    plane = like((34, 32, 64), BF)
-    down, up = call(y_messages, [plane, plane], [info, lat, lat, rz, pooled], (), [face_spec(1, 0), face_spec(1, 15)])
+    out = message(Y_TILES)
+    down, up = call(
+        y_messages, [out, out], [info, lat, lat, rz, pooled], [plane(Z_TILES)], [face_spec(1, 0), face_spec(1, 15)]
+    )
     rym, ryp = neighbours(down, up, "by")
-    plane = like((37, 32, 64), BF)
-    down, up = call(x_messages, [plane, plane], [info, lat, lat, rz, rym, ryp, pooled], (), [face_spec(0, 0), face_spec(0, 15)])
+    out = message(X_TILES)
+    planes = [plane(Z_TILES), plane(Y_TILES), plane(Y_TILES)]
+    down, up = call(
+        x_messages,
+        [out, out],
+        [info, lat, lat, rz, rym, ryp, pooled],
+        planes,
+        [face_spec(0, 0), face_spec(0, 15)],
+    )
     rxm, rxp = neighbours(down, up, "bx")
 
-    temb = time_embedding(timestep, time_weight.shape[0])
-    time_bias = jnp.sum(temb[:, None] * time_weight.astype(F32), axis=0)
-    taps = conv_weight.reshape(3, 3, 3, 64, 64).transpose(0, 2, 1, 3, 4)
-    taps = jnp.stack(
-        [jnp.pad(taps, ((0, 0), (0, 0), (b, 1 - b), (0, 0), (0, 0))) for b in range(2)], axis=4
-    ).reshape(9 * 256, 128)
-    combo = 8 * at[0] + 4 * at[1] + 2 * at[2] + core
-    table = lax.dynamic_index_in_dim(jnp.asarray(coarse_table(), BF), combo, keepdims=False)
-
-    raw, scene, columns = call(
+    temb = time_embedding(timestep, time_weight.shape[0]).reshape(1, -1)
+    raw, scene, columns, taps = call(
         interior,
-        [like((1792, 128), F32), like((3, 16, 9, 16, 128), BF), like((3, 9, 128), F32)],
-        [info, lat_pairs, rz, rym, ryp, taps],
+        [like((1792, 128), F32), like((3, 16, 9, 16, 128), BF), like((3, 9, 128), F32), like((2304, 128), BF)],
+        [info, lat_pairs, rz, rym, ryp, conv_weight],
+        planes,
     )
     pair = (3, 2, 9, 16, 128)
+    tables = jnp.asarray(coarse_table(), BF)
     act, ends, patch, stats = call(
         forward,
         [like((2048, 128), F32), like((2, 3, 9, 16, 128), BF), like((16, 1728), BF), like((devices, 128), F32)],
-        [info, scene, scene, raw, columns, rz, rym, ryp, rxm, rxp, pooled, table, taps]
-        + [coarse_weight.reshape(1728, 64), twice(time_bias)],
-        [pltpu.VMEM((2, 128, 128), F32)],
+        [info, scene, scene, raw, columns, rz, rym, ryp, rxm, rxp, pooled, taps]
+        + [coarse_weight.reshape(1728, 64), temb, time_weight.T, tables],
+        [pltpu.VMEM((2, 128, 128), F32), pltpu.VMEM((224, 160), BF), pltpu.SemaphoreType.DMA]
+        + planes
+        + [plane(X_TILES), plane(X_TILES)],
         [pl.BlockSpec(pair, lambda i: (0, 0, 0, 0, 0)), pl.BlockSpec(pair, lambda i: (0, 7, 0, 0, 0))],
+        far_args=1,
     )
     first = exchange(stats)
     gain, bias = twice(norm_gain), twice(norm_bias)
     weights = [diagonal(out_weight), diagonal(out_weight.T)]
-    predicted, payload = call(
+    predicted, mine, other = call(
         backward(voxels),
-        [like((16, 8, 2, 16, 64), BF), like((2, 2048, 128), F32)],
+        [like((16, 8, 2, 16, 64), BF), like((2048, 128), F32), like((2048, 128), F32)],
         [info, act, first, target.reshape(16, 8, 2, 16, 64), gain, bias] + weights + [scene, ends, patch, stats],
-        [pltpu.VMEM((256, 2048), BF)],
+        [pltpu.VMEM((256, 2048), BF), pltpu.VMEM((2, 2048, 128), F32), pltpu.SemaphoreType.DMA((2,))],
+        far_outs=2,
     )
     swap = [(0, 1), (1, 0)]
     chips = devices // 2
-    other = lax.ppermute(payload[1], "cz", swap)
-    (pieces,) = call(pair_add(voxels), [like((chips, 16, 128), BF)], [info, payload[0], other, first, gain])
+    other = lax.ppermute(other, "cz", swap)
+    (pieces,) = call(pair_add(voxels), [like((chips, 16, 128), BF)], [info, mine, other, first, gain])
     pieces = lax.all_to_all(pieces, CHIPS, 0, 0, tiled=True)
-    copies, act_sum, grads = call(
+    copies, grad_time, grad_gain, grad_bias = call(
         combine(voxels),
-        [like((chips, 8, 128), BF), like((1, 128), F32), like((1, 128), F32)],
-        [info, pieces, first, gain],
+        [like((chips, 8, 128), BF), like((64, 256), F32), like((1, 64), F32), like((1, 64), F32)],
+        [info, pieces, first, gain, temb],
     )
     near = lax.all_to_all(copies, CHIPS, 0, 0, tiled=True)
     far = lax.ppermute(near, "cz", swap)
     grad_conv, grad_coarse, grad_out, loss = call(
-        spread,
-        [like((27, 64, 64), F32), like((27, 64, 64), F32), like((64, 64), F32), like((1, 128), F32)],
+        functools.partial(spread, 1.0 / (voxels * 64)),
+        [like((27, 64, 64), F32), like((27, 64, 64), F32), like((64, 64), F32), like((1, 1), F32)],
         [info, near, far],
         [pltpu.VMEM((2048, 128), F32)],
     )
     return (
         predicted.reshape(latents.shape),
-        loss[0, :1] * (1.0 / (voxels * 64)),
+        loss.reshape(1),
         grad_conv,
         grad_coarse,
         grad_out,
-        temb[:, None] * act_sum[:, :64],
-        grads[0, :64],
-        grads[0, 64:],
+        grad_time.T,
+        grad_gain.reshape(64),
+        grad_bias.reshape(64),
     )
 
 

time: 157 us -> 140 us (0.89)
  blocking collectives: 26.7 us -> 45.9 us
  waiting for transfers between devices: 34 us -> 19.4 us
  local copies, waits for them, and re-layouts: 16.3 us -> 4.31 us
  starting transfers between devices: 37 us -> 31.9 us
  between operations: 5.18 us -> 1.42 us
  other arithmetic: 3.85 us -> 1.94 us
    all_to_all x0 -> x1, blocking collectives: none -> 19.2 us  [shards(): near = lax.all_to_all(copies, CHIPS, 0, 0, tiled=True)]
    all_to_all x1 -> x0, waiting for transfers between devices: 11.4 us -> none  [shards(): near = lax.all_to_all(copies, CHIPS, 0, 0, tiled=True)]
    all_to_all x1 -> x0, starting transfers between devices: 6.18 us -> none  [shards(): near = lax.all_to_all(copies, CHIPS, 0, 0, tiled=True)]
    squeeze x3 -> x0, local copies, waits for them, and re-layouts: 5.54 us -> none  [the longest x1 2.66 us: shards(): other = lax.ppermute(payload[1], 'cz', swap)]
    ppermute x2, waiting for transfers between devices: 4.8 us -> 0.08 us  [neighbours(): before = lax.ppermute(up, axis, [(i, i + 1) for i in range(ends)])]
    another operation x2 -> x0, local copies, waits for them, and re-layouts: 2.66 us -> none  [shards(): jnp.stack([jnp.pad(taps, ((0, 0), (0, 0), (b, 1 - b), (0, 0), (0, 0))) fo...]
  transfers between devices with their start and end apart: 9 -> 8, of which waited for: 5 -> 6; matrix products, arithmetic and copies ran while one was open for 8% -> 1% of each run, Pallas kernels for 3% -> 4%
where the time goes in v1:
time: 140 us; the launch traced here: 139 us
  blocking collectives  45.9 us (33%)
  Pallas kernels  34.5 us (25%)
  starting transfers between devices  31.9 us (23%)
  waiting for transfers between devices  19.4 us (14%)
  local copies, waits for them, and re-layouts  4.31 us (3%)
  other arithmetic  1.94 us (1%)
  between operations  1.42 us (1%)
    pallas_call x9, Pallas kernels, call(): pl.pallas_call(kernel, grid=(1,), out_shape=outs, in_specs=[pl.BlockSpec(...  34.5 us
    all_to_all x1, blocking collectives, shards(): pieces = lax.all_to_all(pieces, CHIPS, 0, 0, tiled=True)  26.7 us
    all_to_all x1, blocking collectives, shards(): near = lax.all_to_all(copies, CHIPS, 0, 0, tiled=True)  19.2 us
    all_to_all x1, starting transfers between devices, exchange(): lax.all_to_all(rows.reshape(rows.shape[0], 1, 128), ('cz',) + CHIPS, 0, 0...  17 us
    all_to_all x1, waiting for transfers between devices, exchange(): lax.all_to_all(rows.reshape(rows.shape[0], 1, 128), ('cz',) + CHIPS, 0, 0...  11.4 us
    ppermute x2, starting transfers between devices, neighbours(): before = lax.ppermute(up, axis, [(i, i + 1) for i in range(ends)])  4.9 us
    unnamed x25, local copies, waits for them, and re-layouts  4.31 us
    ppermute x2, waiting for transfers between devices, neighbours(): after = lax.ppermute(down, axis, [(i + 1, i) for i in range(ends)])  3.75 us
  transfers between devices with their start and end apart: 8, of which 6 were waited for; matrix products, arithmetic and copies ran while one was open for 1% of the time, Pallas kernels for 4%

profile of v1, /device:TPU:1, one launch (start us, length us, event | category | flops | bytes accessed | tf_op | source)
XLA Modules:
  0.0 139.4 jit_solution(2677661617865140019)
XLA Ops:
  0.6 2.7 %shard_map.170 = (bf16[10,16,128]{2,1,0:T(8,128)(2,1)}, bf16[16,64]{1,0:T(8,128)(2,1)}) custom-call(s32[1,3]{1,0:T(1,128)} %info.17, bf16[16,16,16,64]{3,2,1,0:T(8,128)(2,1)} %bitcast.21), custom_call_target="tpu_custom_call" | custom-call | tf_op jit(solution)/shard_map/pallas_call | solution.py:32
  3.3 3.2 %collective-permute-start = (bf16[10,16,128]{2,1,0:T(8,128)(2,1)}, bf16[10,16,128]{2,1,0:T(8,128)(2,1)S(1)}, u32[]{:S(2)}, u32[]{:S(2)}) collective-permute-start(bf16[10,16,128]{2,1,0:T(8,128)(2,1)} %get-tuple-element.33), channel_id=1, source_target_pairs={{0,1},{1,0},{2,3},{3,2},{4,5},{5,4},{6,7},{7,6},{8,9},{9,8},{10,11... | collective-permute-start | bytes 122888 | tf_op jit(solution)/shard_map/ppermute | solution.py:674
  7.6 0.6 copy-done.3
  8.2 1.7 %shard_map.171 = (bf16[11,16,128]{2,1,0:T(8,128)(2,1)}, bf16[11,16,128]{2,1,0:T(8,128)(2,1)}) custom-call(s32[1,3]{1,0:T(1,128)} %info.17, bf16[16,16,16,64]{3,2,1,0:T(8,128)(2,1)} %bitcast.22, bf16[16,16,16,64]{3,2,1,0:T(8,128)(2,1)} %bitcast.23, bf16[10,16,128]{2,1,0:T(8,128)(2,1)} %copy-done.3, bf16[16,64]{1,0:T(8,128)(2,1)} %get-tuple-element.34.pooled), custom_call_target="tpu_custom_call" | custom-call | tf_op jit(solution)/shard_map/pallas_call | solution.py:32
  9.9 1.8 %collective-permute-start.1 = (bf16[11,16,128]{2,1,0:T(8,128)(2,1)}, bf16[11,16,128]{2,1,0:T(8,128)(2,1)S(1)}, u32[]{:S(2)}, u32[]{:S(2)}) collective-permute-start(bf16[11,16,128]{2,1,0:T(8,128)(2,1)} %get-tuple-element.35), channel_id=1, source_target_pairs={{0,2},{2,4},{4,6},{6,8},{8,10},{10,12},{12,14},{1,3},{3,5},{5,7},{... | collective-permute-start | bytes 135176 | tf_op jit(solution)/shard_map/ppermute | solution.py:644
  11.7 1.3 collective-permute-start.2
  13.1 3.7 %collective-permute-done.2.ryp_in = bf16[11,16,128]{2,1,0:T(8,128)(2,1)S(1)} collective-permute-done((bf16[11,16,128]{2,1,0:T(8,128)(2,1)}, bf16[11,16,128]{2,1,0:T(8,128)(2,1)S(1)}, u32[]{:S(2)}, u32[]{:S(2)}) %collective-permute-start.2) | collective-permute-done | bytes 45088 | tf_op jit(solution)/shard_map/ppermute | solution.py:645
  16.9 0.6 copy-done.5
  17.5 1.8 %shard_map.173 = (bf16[14,16,128]{2,1,0:T(8,128)(2,1)}, bf16[14,16,128]{2,1,0:T(8,128)(2,1)}) custom-call(s32[1,3]{1,0:T(1,128)} %info.17, bf16[16,16,16,64]{3,2,1,0:T(8,128)(2,1)} %bitcast.24, bf16[16,16,16,64]{3,2,1,0:T(8,128)(2,1)} %bitcast.25, bf16[10,16,128]{2,1,0:T(8,128)(2,1)} %copy-done.3, bf16[11,16,128]{2,1,0:T(8,128)(2,1)} %copy-done.4, ...), custom_call_target="tpu_custom_call" | custom-call | tf_op jit(solution)/shard_map/pallas_call | solution.py:32
  19.3 3.1 %collective-permute-start.3 = (bf16[14,16,128]{2,1,0:T(8,128)(2,1)}, bf16[14,16,128]{2,1,0:T(8,128)(2,1)S(1)}, u32[]{:S(2)}, u32[]{:S(2)}) collective-permute-start(bf16[14,16,128]{2,1,0:T(8,128)(2,1)} %get-tuple-element.40), channel_id=1, source_target_pairs={{0,16},{16,32},{32,48},{48,64},{64,80},{80,96},{96,112},{112,128},... | collective-permute-start | bytes 172040 | tf_op jit(solution)/shard_map/ppermute | solution.py:644
  22.4 1.3 collective-permute-start.4
  23.7 0.6 pad_maximum_fusion
  24.3 5.3 %shard_map.172 = (f32[1792,128]{1,0:T(8,128)}, bf16[3,16,9,16,128]{4,3,2,1,0:T(8,128)(2,1)}, f32[3,9,128]{2,1,0:T(8,128)}, bf16[2304,128]{1,0:T(8,128)(2,1)}) custom-call(s32[1,3]{1,0:T(1,128)} %info.17, bf16[16,8,2,16,64]{4,3,2,1,0:T(8,128)(2,1)} %bitcast.26, bf16[10,16,128]{2,1,0:T(8,128)(2,1)} %copy-done.3, bf16[11,16,128]{2,1,0:T(8,128)(2,1)} %copy-done.4, ...), custom_call_target="tpu_custom_call" | custom-call | tf_op jit(solution)/shard_map/pallas_call | solution.py:32
  29.6 0.6 copy-done.8
  30.2 5.1 %shard_map.174 = (f32[2048,128]{1,0:T(8,128)}, bf16[2,3,9,16,128]{4,3,2,1,0:T(8,128)(2,1)}, bf16[16,1728]{1,0:T(8,128)(2,1)}, f32[256,128]{1,0:T(8,128)}) custom-call(s32[1,3]{1,0:T(1,128)} %info.17, bf16[3,16,9,16,128]{4,3,2,1,0:T(8,128)(2,1)} %get-tuple-element.37.near_low.near_high.scene, ...), custom_call_target="tpu_custom_call" | custom-call | tf_op jit(solution)/shard_map/pallas_call | solution.py:32
  35.3 17.0 %all-to-all-start = ((f32[256,1,128]{2,1,0:T(1,128)}), f32[256,1,128]{2,1,0:T(1,128)S(1)}, u32[]{:S(2)}, u32[]{:S(2)}) async-start(f32[256,1,128]{2,1,0:T(1,128)} %bitcast.31), calls=%async_computation | async-start | bytes 262144 | tf_op jit(solution)/shard_map/all_to_all | solution.py:638
  52.5 0.6 maximum_bitcast_fusion
  53.1 0.7 fusion.4
  53.8 11.4 %all-to-all-done = f32[256,1,128]{2,1,0:T(1,128)S(1)} async-done(((f32[256,1,128]{2,1,0:T(1,128)}), f32[256,1,128]{2,1,0:T(1,128)S(1)}, u32[]{:S(2)}, u32[]{:S(2)}) %all-to-all-start) | async-done | bytes 131104 | tf_op jit(solution)/shard_map/all_to_all | solution.py:638
  65.2 0.6 copy-done
  65.9 9.8 %shard_map.175 = (bf16[16,8,2,16,64]{4,3,2,1,0:T(8,128)(2,1)}, f32[2048,128]{1,0:T(8,128)}, f32[2048,128]{1,0:T(8,128)}) custom-call(s32[1,3]{1,0:T(1,128)} %info.17, f32[2048,128]{1,0:T(8,128)} %get-tuple-element.43.act, f32[256,128]{1,0:T(8,128)} %bitcast.27, bf16[16,8,2,16,64]{4,3,2,1,0:T(8,128)(2,1)} %bitcast.30, f32[1,128]{1,0:T(1,128)} %get-tuple-element.62.gain, ...), custom_call_target="tpu_custom_call" | custom-call | tf_op jit(solution)/shard_map/pallas_call | solution.py:32
  75.7 0.9 collective-permute-start.5
  76.6 2.5 %collective-permute-done.5.other = f32[2048,128]{1,0:T(8,128)S(1)} collective-permute-done((f32[2048,128]{1,0:T(8,128)}, f32[2048,128]{1,0:T(8,128)S(1)}, u32[]{:S(2)}, u32[]{:S(2)}) %collective-permute-start.5) | collective-permute-done | bytes 1048608 | tf_op jit(solution)/shard_map/ppermute | solution.py:723
  79.1 1.0 copy-done.1
  80.1 3.2 %shard_map.176 = bf16[128,16,128]{2,1,0:T(8,128)(2,1)} custom-call(s32[1,3]{1,0:T(1,128)} %info.17, f32[2048,128]{1,0:T(8,128)} %get-tuple-element.48.mine, f32[2048,128]{1,0:T(8,128)} %copy-done.1, f32[256,128]{1,0:T(8,128)} %bitcast.28, f32[1,128]{1,0:T(1,128)} %get-tuple-element.62.gain), custom_call_target="tpu_custom_call" | custom-call | tf_op jit(solution)/shard_map/pallas_call | solution.py:32
  83.3 26.7 %all_to_all.15.pieces = bf16[128,16,128]{2,1,0:T(8,128)(2,1)} all-to-all(bf16[128,16,128]{2,1,0:T(8,128)(2,1)} %shard_map.176), channel_id=1, replica_groups=mesh['bx'=16,'by'=8,'cz'=2] {'bx','by'}, dimensions={0} | all-to-all | bytes 1048576 | tf_op jit(solution)/shard_map/all_to_all | solution.py:725
  110.0 2.5 %shard_map.177 = (bf16[128,8,128]{2,1,0:T(8,128)(2,1)}, f32[64,256]{1,0:T(8,128)}, f32[1,64]{1,0:T(1,128)}, f32[1,64]{1,0:T(1,128)}) custom-call(s32[1,3]{1,0:T(1,128)} %info.17, bf16[128,16,128]{2,1,0:T(8,128)(2,1)} %all_to_all.15.pieces, f32[256,128]{1,0:T(8,128)} %bitcast.29, f32[1,128]{1,0:T(1,128)} %get-tuple-element.62.gain, f32[1,256]{1,0:T(1,128)} %bitcast.36), custom_call_target="tpu_custom_call" | custom-call | tf_op jit(solution)/shard_map/pallas_call | solution.py:32
  112.5 19.2 %all_to_all.16.near = bf16[128,8,128]{2,1,0:T(8,128)(2,1)S(1)} all-to-all(bf16[128,8,128]{2,1,0:T(8,128)(2,1)} %get-tuple-element.50), channel_id=1, replica_groups=mesh['bx'=16,'by'=8,'cz'=2] {'bx','by'}, dimensions={0} | all-to-all | bytes 524288 | tf_op jit(solution)/shard_map/all_to_all | solution.py:731
  131.7 3.3 %collective-permute-start.6 = (bf16[128,8,128]{2,1,0:T(8,128)(2,1)S(1)}, bf16[128,8,128]{2,1,0:T(8,128)(2,1)S(1)}, u32[]{:S(2)}, u32[]{:S(2)}) collective-permute-start(bf16[128,8,128]{2,1,0:T(8,128)(2,1)S(1)} %all_to_all.16.near), channel_id=1, source_target_pairs={{0,1},{1,0},{2,3},{3,2},{4,5},{5,4},{6,7},{7,6},{8,9},{9,8},{10,11... | collective-permute-start | bytes 786440 | tf_op jit(solution)/shard_map/ppermute | solution.py:732
  135.0 1.2 collective-permute-done.6.far
  136.1 0.7 copy-done.6
  136.8 2.5 %shard_map.178 = (f32[27,64,64]{2,1,0:T(8,128)}, f32[27,64,64]{2,1,0:T(8,128)}, f32[64,64]{1,0:T(8,128)}, f32[1,1]{1,0:T(1,128)}) custom-call(s32[1,3]{1,0:T(1,128)} %info.17, bf16[128,8,128]{2,1,0:T(8,128)(2,1)} %copy-done.2, bf16[128,8,128]{2,1,0:T(8,128)(2,1)} %copy-done.6), custom_call_target="tpu_custom_call" | custom-call | tf_op jit(solution)/shard_map/pallas_call | solution.py:32
  (24 shorter events, 0.7 us)
Async XLA Ops:
  3.3 4.3 %collective-permute-start = (bf16[10,16,128]{2,1,0:T(8,128)(2,1)}, bf16[10,16,128]{2,1,0:T(8,128)(2,1)S(1)}, u32[]{:S(2)}, u32[]{:S(2)}) collective-permute-start(bf16[10,16,128]{2,1,0:T(8,128)(2,1)} %get-tuple-element.33), channel_id=1, source_target_pairs={{0,1},{1,0},{2,3},{3,2},{4,5},{5,4},{6,7},{7,6},{8,9},{9,8},{10,11... | collective-permute-start | bytes 122888 | tf_op jit(solution)/shard_map/ppermute | solution.py:674
  7.6 0.6 copy-start.3
  9.9 3.2 %collective-permute-start.1 = (bf16[11,16,128]{2,1,0:T(8,128)(2,1)}, bf16[11,16,128]{2,1,0:T(8,128)(2,1)S(1)}, u32[]{:S(2)}, u32[]{:S(2)}) collective-permute-start(bf16[11,16,128]{2,1,0:T(8,128)(2,1)} %get-tuple-element.35), channel_id=1, source_target_pairs={{0,2},{2,4},{4,6},{6,8},{8,10},{10,12},{12,14},{1,3},{3,5},{5,7},{... | collective-permute-start | bytes 135176 | tf_op jit(solution)/shard_map/ppermute | solution.py:644
  11.7 5.2 %collective-permute-start.2 = (bf16[11,16,128]{2,1,0:T(8,128)(2,1)}, bf16[11,16,128]{2,1,0:T(8,128)(2,1)S(1)}, u32[]{:S(2)}, u32[]{:S(2)}) collective-permute-start(bf16[11,16,128]{2,1,0:T(8,128)(2,1)} %get-tuple-element.36), channel_id=1, source_target_pairs={{2,0},{4,2},{6,4},{8,6},{10,8},{12,10},{14,12},{3,1},{5,3},{7,5},{... | collective-permute-start | bytes 135176 | tf_op jit(solution)/shard_map/ppermute | solution.py:645
  13.1 3.8 %copy-start.4 = (bf16[11,16,128]{2,1,0:T(8,128)(2,1)}, bf16[11,16,128]{2,1,0:T(8,128)(2,1)S(1)}, u32[]{:S(2)}) copy-start(bf16[11,16,128]{2,1,0:T(8,128)(2,1)S(1)} %collective-permute-done.1.rym_in) | copy-start | bytes 135172
  16.9 0.6 copy-start.5
  19.3 10.3 %collective-permute-start.3 = (bf16[14,16,128]{2,1,0:T(8,128)(2,1)}, bf16[14,16,128]{2,1,0:T(8,128)(2,1)S(1)}, u32[]{:S(2)}, u32[]{:S(2)}) collective-permute-start(bf16[14,16,128]{2,1,0:T(8,128)(2,1)} %get-tuple-element.40), channel_id=1, source_target_pairs={{0,16},{16,32},{32,48},{48,64},{64,80},{80,96},{96,112},{112,128},... | collective-permute-start | bytes 172040 | tf_op jit(solution)/shard_map/ppermute | solution.py:644
  22.4 7.2 %collective-permute-start.4 = (bf16[14,16,128]{2,1,0:T(8,128)(2,1)}, bf16[14,16,128]{2,1,0:T(8,128)(2,1)S(1)}, u32[]{:S(2)}, u32[]{:S(2)}) collective-permute-start(bf16[14,16,128]{2,1,0:T(8,128)(2,1)} %get-tuple-element.41), channel_id=1, source_target_pairs={{16,0},{32,16},{48,32},{64,48},{80,64},{96,80},{112,96},{128,112},... | collective-permute-start | bytes 172040 | tf_op jit(solution)/shard_map/ppermute | solution.py:645
  29.6 0.6 copy-start.8
  29.6 0.6 copy-start.9
  30.2 22.2 %copy-start.7 = (bf16[64,64]{1,0:T(8,128)(2,1)S(1)}, bf16[64,64]{1,0:T(8,128)(2,1)}, u32[]{:S(2)}) copy-start(bf16[64,64]{1,0:T(8,128)(2,1)} %param.17) | copy-start | bytes 24580
  30.2 22.3 %copy-start.10 = (f32[64]{0:T(128)S(1)}, f32[64]{0:T(128)}, u32[]{:S(2)}) copy-start(f32[64]{0:T(128)} %param.19) | copy-start | bytes 772
  30.2 22.3 %copy-start.11 = (f32[64]{0:T(128)S(1)}, f32[64]{0:T(128)}, u32[]{:S(2)}) copy-start(f32[64]{0:T(128)} %param.20) | copy-start | bytes 772
  35.3 29.9 %all-to-all-start = ((f32[256,1,128]{2,1,0:T(1,128)}), f32[256,1,128]{2,1,0:T(1,128)S(1)}, u32[]{:S(2)}, u32[]{:S(2)}) async-start(f32[256,1,128]{2,1,0:T(1,128)} %bitcast.31), calls=%async_computation | async-start | bytes 262144 | tf_op jit(solution)/shard_map/all_to_all | solution.py:638
  65.2 0.6 copy-start
  75.7 3.4 %collective-permute-start.5 = (f32[2048,128]{1,0:T(8,128)}, f32[2048,128]{1,0:T(8,128)S(1)}, u32[]{:S(2)}, u32[]{:S(2)}) collective-permute-start(f32[2048,128]{1,0:T(8,128)} %get-tuple-element.49), channel_id=1, source_target_pairs={{0,1},{1,0},{2,3},{3,2},{4,5},{5,4},{6,7},{7,6},{8,9},{9,8},{10,11... | collective-permute-start | bytes 3145736 | tf_op jit(solution)/shard_map/ppermute | solution.py:723
  79.1 1.0 copy-start.1
  131.7 4.4 %copy-start.2 = (bf16[128,8,128]{2,1,0:T(8,128)(2,1)}, bf16[128,8,128]{2,1,0:T(8,128)(2,1)S(1)}, u32[]{:S(2)}) copy-start(bf16[128,8,128]{2,1,0:T(8,128)(2,1)S(1)} %all_to_all.16.near) | copy-start | bytes 786436
  131.7 4.4 %collective-permute-start.6 = (bf16[128,8,128]{2,1,0:T(8,128)(2,1)S(1)}, bf16[128,8,128]{2,1,0:T(8,128)(2,1)S(1)}, u32[]{:S(2)}, u32[]{:S(2)}) collective-permute-start(bf16[128,8,128]{2,1,0:T(8,128)(2,1)S(1)} %all_to_all.16.near), channel_id=1, source_target_pairs={{0,1},{1,0},{2,3},{3,2},{4,5},{5,4},{6,7},{7,6},{8,9},{9,8},{10,11... | collective-permute-start | bytes 786440 | tf_op jit(solution)/shard_map/ppermute | solution.py:732
  136.1 0.7 copy-start.6

commit v2 on v1

--- a/solution.py
+++ b/solution.py
@@ -15,7 +15,7 @@
 F32 = jnp.float32
 EPS = 1e-05
 GROUP = 2
-VMEM_LIMIT = 56 * 1024 * 1024
+VMEM_LIMIT = 40 * 1024 * 1024
 SHIFT_LANE = 65
 
 
@@ -29,6 +29,10 @@
     vmem = pl.BlockSpec(memory_space=pltpu.VMEM)
     far = pl.BlockSpec(memory_space=pl.ANY)
     specs = list(faces) + [vmem] * (len(args) - 1 - len(faces) - far_args) + [far] * far_args
+    args = [
+        pltpu.with_memory_space_constraint(arg, pltpu.VMEM) if spec is vmem else arg
+        for arg, spec in zip(args, [None] + specs)
+    ]
     return pl.pallas_call(
         kernel,
         grid=(1,),
@@ -438,6 +442,14 @@
         stats[128 * u : 128 * u + 128] = shift[u].T + row
 
 
+def turn(info, scene, ends, turned):
+    for oz in range(3):
+        for xp in range(18):
+            for dk in range(2):
+                tile = scene[oz, xp - 1, dk : dk + 8] if 1 <= xp <= 16 else ends[xp // 17, oz, dk : dk + 8]
+                turned[oz, 128 * dk : 128 * dk + 128, 128 * xp : 128 * xp + 128] = tile.reshape(128, 128).T
+
+
 def pair_sum(row):
     lane = lax.broadcasted_iota(jnp.int32, row.shape, 1)
     return row + jnp.where(lane % 2 == 0, pltpu.roll(row, 127, 1), pltpu.roll(row, 1, 1))
@@ -463,7 +475,7 @@
     count = float(voxels * GROUP)
     scale = 1.0 / (voxels * 64)
 
-    def kernel(info, act, gathered, target, gain, bias, weight, weight_t, scene, ends, patch, stats, predicted, mine, other, cotangent, payload, sent):
+    def kernel(info, act, gathered, target, gain, bias, weight, weight_t, turned, patch, stats, predicted, mine, other, cotangent, payload, sent):
         kz = lax.axis_index("cz")
         _, _, mean, rstd = moments(gathered, count)
         gains = jnp.zeros((1, 128), F32)
@@ -491,10 +503,10 @@
             lost = lost + jnp.sum(residue * residue, axis=0, keepdims=True)
             outer = outer + lax.dot_general(hidden, upstream, (((0,), (0,)), ((), ())), preferred_element_type=F32)
             value = value * (gain[...] * rstd)
+            narrow = [value.astype(BF), normalized.astype(BF)]
+            cotangent[rows, :128] = jnp.concatenate([part[:, :64] for part in narrow], axis=1)
+            cotangent[rows, 128:] = jnp.concatenate([part[:, 64:] for part in narrow], axis=1)
             for part, wide in enumerate((value, normalized)):
-                flipped = wide.T.astype(BF)
-                cotangent[64 * part : 64 * part + 64, rows] = flipped[:64]
-                cotangent[128 + 64 * part : 192 + 64 * part, rows] = flipped[64:]
                 planes = wide.reshape(2, 2, 4, 16, 128)
                 for b in range(2):
                     q = 2 * (x // 8) + b
@@ -519,17 +531,10 @@
         for t in range(27):
             store(t, 7, coarse[64 * t : 64 * t + 64])
         for ox in range(3):
+            windows = turned[:, :, 128 * ox : 128 * ox + 2048].reshape(768, 2048)
+            products = jnp.dot(windows, cotangent[...], preferred_element_type=F32)
             for oz in range(3):
-                parts = []
-                for dk in range(2):
-                    planes = [scene[oz, max(ox - 1, 0) : min(ox + 15, 16), dk : dk + 8]]
-                    if ox == 0:
-                        planes = [ends[0, oz, dk : dk + 8][None]] + planes
-                    if ox == 2:
-                        planes = planes + [ends[1, oz, dk : dk + 8][None]]
-                    parts.append(jnp.concatenate(planes, axis=0).reshape(2048, 128))
-                window = jnp.concatenate(parts, axis=1)
-                product = jnp.dot(cotangent[...], window, preferred_element_type=F32).T
+                product = products[256 * oz : 256 * oz + 256]
                 for oy in range(3):
                     value = product[64 * oy : 64 * oy + 64, :128] + product[64 * oy + 64 : 64 * oy + 128, 128:]
                     store(9 * ox + 3 * oy + oz, 0, value)
@@ -709,13 +714,14 @@
         far_args=1,
     )
     first = exchange(stats)
+    (turned,) = call(turn, [like((3, 256, 18 * 128), BF)], [info, scene, ends])
     gain, bias = twice(norm_gain), twice(norm_bias)
     weights = [diagonal(out_weight), diagonal(out_weight.T)]
     predicted, mine, other = call(
         backward(voxels),
         [like((16, 8, 2, 16, 64), BF), like((2048, 128), F32), like((2048, 128), F32)],
-        [info, act, first, target.reshape(16, 8, 2, 16, 64), gain, bias] + weights + [scene, ends, patch, stats],
-        [pltpu.VMEM((256, 2048), BF), pltpu.VMEM((2, 2048, 128), F32), pltpu.SemaphoreType.DMA((2,))],
+        [info, act, first, target.reshape(16, 8, 2, 16, 64), gain, bias] + weights + [turned, patch, stats],
+        [pltpu.VMEM((2048, 256), BF), pltpu.VMEM((2, 2048, 128), F32), pltpu.SemaphoreType.DMA((2,))],
         far_outs=2,
     )
     swap = [(0, 1), (1, 0)]

time: 140 us -> 127 us (0.907)
  Pallas kernels: 34.5 us -> 23.3 us
  local copies, waits for them, and re-layouts: 4.31 us -> 7.95 us
  waiting for transfers between devices: 19.4 us -> 16.5 us
  blocking collectives: 45.9 us -> 44 us
  other arithmetic: 1.94 us -> 0.22 us
    pallas_call x9 -> x10, Pallas kernels: 34.5 us -> 23.3 us  [call(): pl.pallas_call(kernel, grid=(1,), out_shape=outs, in_specs=[pl.BlockSpec(...]
    unnamed x25 -> x31, local copies, waits for them, and re-layouts: 4.31 us -> 7.95 us
    all_to_all x1, waiting for transfers between devices: 11.4 us -> 9.24 us  [exchange(): lax.all_to_all(rows.reshape(rows.shape[0], 1, 128), ('cz',) + CHIPS, 0, 0...]
    all_to_all x1, blocking collectives: 26.7 us -> 25 us  [shards(): pieces = lax.all_to_all(pieces, CHIPS, 0, 0, tiled=True)]
    all_to_all x1, starting transfers between devices: 17 us -> 18.6 us  [exchange(): lax.all_to_all(rows.reshape(rows.shape[0], 1, 128), ('cz',) + CHIPS, 0, 0...]
  transfers between devices with their start and end apart: 8 -> 8, of which waited for: 6 -> 6; matrix products, arithmetic and copies ran while one was open for 1% -> 0% of each run, Pallas kernels for 4% -> 4%
where the time goes in v2:
time: 127 us
  blocking collectives  44 us (35%)
  starting transfers between devices  33.3 us (26%)
  Pallas kernels  23.3 us (18%)
  waiting for transfers between devices  16.5 us (13%)
  local copies, waits for them, and re-layouts  7.95 us (6%)
  between operations  1.54 us (1%)
    all_to_all x1, blocking collectives, shards(): pieces = lax.all_to_all(pieces, CHIPS, 0, 0, tiled=True)  25 us
    pallas_call x10, Pallas kernels, call(): pl.pallas_call(kernel, grid=(1,), out_shape=outs, in_specs=[pl.BlockSpec(...  23.3 us
    all_to_all x1, blocking collectives, shards(): near = lax.all_to_all(copies, CHIPS, 0, 0, tiled=True)  19 us
    all_to_all x1, starting transfers between devices, exchange(): lax.all_to_all(rows.reshape(rows.shape[0], 1, 128), ('cz',) + CHIPS, 0, 0...  18.6 us
    all_to_all x1, waiting for transfers between devices, exchange(): lax.all_to_all(rows.reshape(rows.shape[0], 1, 128), ('cz',) + CHIPS, 0, 0...  9.24 us
    unnamed x31, local copies, waits for them, and re-layouts  7.95 us
    ppermute x2, starting transfers between devices, neighbours(): before = lax.ppermute(up, axis, [(i, i + 1) for i in range(ends)])  4.92 us
    ppermute x2, waiting for transfers between devices, neighbours(): after = lax.ppermute(down, axis, [(i + 1, i) for i in range(ends)])  3.63 us
  transfers between devices with their start and end apart: 8, of which 6 were waited for; matrix products, arithmetic and copies ran while one was open for 0% of the time, Pallas kernels for 4%

profile of v2, /device:TPU:1, one launch (start us, length us, event | category | flops | bytes accessed | tf_op | source)
XLA Modules:
  0.0 126.9 jit_solution(5508333802365322128)
XLA Ops:
  0.6 1.2 copy-done
  1.9 0.7 copy-done.9
  2.5 1.4 %shard_map.170 = (bf16[10,16,128]{2,1,0:T(8,128)(2,1)S(1)}, bf16[16,64]{1,0:T(8,128)(2,1)S(1)}) custom-call(s32[1,3]{1,0:T(1,128)S(1)} %copy-done.9, bf16[16,16,16,64]{3,2,1,0:T(8,128)(2,1)S(1)} %bitcast.21), custom_call_target="tpu_custom_call" | custom-call | tf_op jit(solution)/shard_map/pallas_call | solution.py:36
  3.9 3.3 %collective-permute-start = (bf16[10,16,128]{2,1,0:T(8,128)(2,1)S(1)}, bf16[10,16,128]{2,1,0:T(8,128)(2,1)S(1)}, u32[]{:S(2)}, u32[]{:S(2)}) collective-permute-start(bf16[10,16,128]{2,1,0:T(8,128)(2,1)S(1)} %get-tuple-element.33), channel_id=1, source_target_pairs={{0,1},{1,0},{2,3},{3,2},{4,5},{5,4},{6,7},{7,6},{8,9},{9,8},{10,11... | collective-permute-start | bytes 122888 | tf_op jit(solution)/shard_map/ppermute | solution.py:679
  7.9 0.2 collective-permute-done.rz_in
  8.1 0.7 shard_map.171
  8.8 1.8 %collective-permute-start.1 = (bf16[11,16,128]{2,1,0:T(8,128)(2,1)S(1)}, bf16[11,16,128]{2,1,0:T(8,128)(2,1)S(1)}, u32[]{:S(2)}, u32[]{:S(2)}) collective-permute-start(bf16[11,16,128]{2,1,0:T(8,128)(2,1)S(1)} %get-tuple-element.35), channel_id=1, source_target_pairs={{0,2},{2,4},{4,6},{6,8},{8,10},{10,12},{12,14},{1,3},{3,5},{5,7},{... | collective-permute-start | bytes 135176 | tf_op jit(solution)/shard_map/ppermute | solution.py:649
  10.6 1.3 %collective-permute-start.2 = (bf16[11,16,128]{2,1,0:T(8,128)(2,1)S(1)}, bf16[11,16,128]{2,1,0:T(8,128)(2,1)S(1)}, u32[]{:S(2)}, u32[]{:S(2)}) collective-permute-start(bf16[11,16,128]{2,1,0:T(8,128)(2,1)S(1)} %get-tuple-element.36), channel_id=1, source_target_pairs={{2,0},{4,2},{6,4},{8,6},{10,8},{12,10},{14,12},{3,1},{5,3},{7,5},{... | collective-permute-start | bytes 135176 | tf_op jit(solution)/shard_map/ppermute | solution.py:650
  12.0 3.6 %collective-permute-done.2.ryp_in = bf16[11,16,128]{2,1,0:T(8,128)(2,1)S(1)} collective-permute-done((bf16[11,16,128]{2,1,0:T(8,128)(2,1)S(1)}, bf16[11,16,128]{2,1,0:T(8,128)(2,1)S(1)}, u32[]{:S(2)}, u32[]{:S(2)}) %collective-permute-start.2) | collective-permute-done | bytes 45088 | tf_op jit(solution)/shard_map/ppermute | solution.py:650
  15.6 0.8 shard_map.173
  16.3 3.1 %collective-permute-start.3 = (bf16[14,16,128]{2,1,0:T(8,128)(2,1)S(1)}, bf16[14,16,128]{2,1,0:T(8,128)(2,1)S(1)}, u32[]{:S(2)}, u32[]{:S(2)}) collective-permute-start(bf16[14,16,128]{2,1,0:T(8,128)(2,1)S(1)} %get-tuple-element.40), channel_id=1, source_target_pairs={{0,16},{16,32},{32,48},{48,64},{64,80},{80,96},{96,112},{112,128},... | collective-permute-start | bytes 172040 | tf_op jit(solution)/shard_map/ppermute | solution.py:649
  19.5 1.3 %collective-permute-start.4 = (bf16[14,16,128]{2,1,0:T(8,128)(2,1)S(1)}, bf16[14,16,128]{2,1,0:T(8,128)(2,1)S(1)}, u32[]{:S(2)}, u32[]{:S(2)}) collective-permute-start(bf16[14,16,128]{2,1,0:T(8,128)(2,1)S(1)} %get-tuple-element.41), channel_id=1, source_target_pairs={{16,0},{32,16},{48,32},{64,48},{80,64},{96,80},{112,96},{128,112},... | collective-permute-start | bytes 172040 | tf_op jit(solution)/shard_map/ppermute | solution.py:650
  20.8 3.5 %shard_map.172 = (f32[1792,128]{1,0:T(8,128)S(1)}, bf16[3,16,9,16,128]{4,3,2,1,0:T(8,128)(2,1)S(1)}, f32[3,9,128]{2,1,0:T(8,128)S(1)}, bf16[2304,128]{1,0:T(8,128)(2,1)S(1)}) custom-call(s32[1,3]{1,0:T(1,128)S(1)} %copy-done.9, bf16[16,8,2,16,64]{4,3,2,1,0:T(8,128)(2,1)S(1)} %bitcast.26, bf16[10,16,128]{2,1,0:T(8,128)(2,1)S(1)} %collective-permute-done.rz_in, ...), custom_call_target="tpu_custom_call" | custom-call | tf_op jit(solution)/shard_map/pallas_call | solution.py:36
  24.4 3.0 %shard_map.174 = (f32[2048,128]{1,0:T(8,128)S(1)}, bf16[2,3,9,16,128]{4,3,2,1,0:T(8,128)(2,1)S(1)}, bf16[16,1728]{1,0:T(8,128)(2,1)S(1)}, f32[256,128]{1,0:T(8,128)}) custom-call(s32[1,3]{1,0:T(1,128)S(1)} %copy-done.9, bf16[3,16,9,16,128]{4,3,2,1,0:T(8,128)(2,1)S(1)} %get-tuple-element.37.near_low.near_high.scene, ...), custom_call_target="tpu_custom_call" | custom-call | tf_op jit(solution)/shard_map/pallas_call | solution.py:36
  27.5 1.0 copy-done.5
  28.5 18.6 %all-to-all-start = ((f32[256,1,128]{2,1,0:T(1,128)}), f32[256,1,128]{2,1,0:T(1,128)S(1)}, u32[]{:S(2)}, u32[]{:S(2)}) async-start(f32[256,1,128]{2,1,0:T(1,128)} %bitcast.7), calls=%async_computation | async-start | bytes 262144 | tf_op jit(solution)/shard_map/all_to_all | solution.py:643
  47.1 0.1 copy.21
  47.4 1.5 %shard_map.175.turned = bf16[3,256,2304]{2,1,0:T(8,128)(2,1)S(1)} custom-call(s32[1,3]{1,0:T(1,128)S(1)} %copy-done.10, bf16[3,16,9,16,128]{4,3,2,1,0:T(8,128)(2,1)S(1)} %get-tuple-element.37.near_low.near_high.scene, bf16[2,3,9,16,128]{4,3,2,1,0:T(8,128)(2,1)S(1)} %get-tuple-element.45.ends), custom_call_target="tpu_custom_call" | custom-call | tf_op jit(solution)/shard_map/pallas_call | solution.py:36
  48.9 1.7 %copy-done.1 = bf16[3,256,2304]{2,1,0:T(8,128)(2,1)} copy-done((bf16[3,256,2304]{2,1,0:T(8,128)(2,1)}, bf16[3,256,2304]{2,1,0:T(8,128)(2,1)S(1)}, u32[]{:S(2)}) %copy-start.1) | copy-done | bytes 3538968
  50.6 9.2 %all-to-all-done = f32[256,1,128]{2,1,0:T(1,128)S(1)} async-done(((f32[256,1,128]{2,1,0:T(1,128)}), f32[256,1,128]{2,1,0:T(1,128)S(1)}, u32[]{:S(2)}, u32[]{:S(2)}) %all-to-all-start) | async-done | bytes 131104 | tf_op jit(solution)/shard_map/all_to_all | solution.py:643
  59.9 2.0 %copy-done.2 = bf16[3,256,2304]{2,1,0:T(8,128)(2,1)S(1)} copy-done((bf16[3,256,2304]{2,1,0:T(8,128)(2,1)S(1)}, bf16[3,256,2304]{2,1,0:T(8,128)(2,1)}, u32[]{:S(2)}) %copy-start.2) | copy-done | bytes 3538968
  61.9 1.2 copy-done.6
  63.1 7.3 %shard_map.176 = (bf16[16,8,2,16,64]{4,3,2,1,0:T(8,128)(2,1)}, f32[2048,128]{1,0:T(8,128)S(1)}, f32[2048,128]{1,0:T(8,128)S(1)}) custom-call(s32[1,3]{1,0:T(1,128)S(1)} %copy-done.10, f32[2048,128]{1,0:T(8,128)S(1)} %copy-done.6, f32[256,128]{1,0:T(8,128)S(1)} %bitcast.27, bf16[16,8,2,16,64]{4,3,2,1,0:T(8,128)(2,1)S(1)} %bitcast.30, ...), custom_call_target="tpu_custom_call" | custom-call | tf_op jit(solution)/shard_map/pallas_call | solution.py:36
  70.3 0.7 collective-permute-start.5
  71.1 2.3 %collective-permute-done.5.other = f32[2048,128]{1,0:T(8,128)S(1)} collective-permute-done((f32[2048,128]{1,0:T(8,128)S(1)}, f32[2048,128]{1,0:T(8,128)S(1)}, u32[]{:S(2)}, u32[]{:S(2)}) %collective-permute-start.5) | collective-permute-done | bytes 1048608 | tf_op jit(solution)/shard_map/ppermute | solution.py:729
  73.4 1.4 %shard_map.177 = bf16[128,16,128]{2,1,0:T(8,128)(2,1)S(1)} custom-call(s32[1,3]{1,0:T(1,128)S(1)} %copy-done.10, f32[2048,128]{1,0:T(8,128)S(1)} %get-tuple-element.48.mine, f32[2048,128]{1,0:T(8,128)S(1)} %collective-permute-done.5.other, f32[256,128]{1,0:T(8,128)S(1)} %bitcast.28, f32[1,128]{1,0:T(1,128)S(1)} %get-tuple-element.62.gain), custom_call_target="tpu_custom_call" | custom-call | tf_op jit(solution)/shard_map/pallas_call | solution.py:36
  74.8 25.0 %all_to_all.15.pieces = bf16[128,16,128]{2,1,0:T(8,128)(2,1)S(1)} all-to-all(bf16[128,16,128]{2,1,0:T(8,128)(2,1)S(1)} %shard_map.177), channel_id=1, replica_groups=mesh['bx'=16,'by'=8,'cz'=2] {'bx','by'}, dimensions={0} | all-to-all | bytes 1048576 | tf_op jit(solution)/shard_map/all_to_all | solution.py:731
  99.8 1.7 %shard_map.178 = (bf16[128,8,128]{2,1,0:T(8,128)(2,1)S(1)}, f32[64,256]{1,0:T(8,128)}, f32[1,64]{1,0:T(1,128)}, f32[1,64]{1,0:T(1,128)}) custom-call(s32[1,3]{1,0:T(1,128)S(1)} %copy-done.10, bf16[128,16,128]{2,1,0:T(8,128)(2,1)S(1)} %all_to_all.15.pieces, f32[256,128]{1,0:T(8,128)S(1)} %bitcast.29, f32[1,128]{1,0:T(1,128)S(1)} %get-tuple-element.62.gain, ...), custom_call_target="tpu_custom_call" | custom-call | tf_op jit(solution)/shard_map/pallas_call | solution.py:36
  101.5 19.0 %all_to_all.16.near = bf16[128,8,128]{2,1,0:T(8,128)(2,1)S(1)} all-to-all(bf16[128,8,128]{2,1,0:T(8,128)(2,1)S(1)} %get-tuple-element.50), channel_id=1, replica_groups=mesh['bx'=16,'by'=8,'cz'=2] {'bx','by'}, dimensions={0} | all-to-all | bytes 524288 | tf_op jit(solution)/shard_map/all_to_all | solution.py:737
  120.5 3.2 %collective-permute-start.6 = (bf16[128,8,128]{2,1,0:T(8,128)(2,1)S(1)}, bf16[128,8,128]{2,1,0:T(8,128)(2,1)S(1)}, u32[]{:S(2)}, u32[]{:S(2)}) collective-permute-start(bf16[128,8,128]{2,1,0:T(8,128)(2,1)S(1)} %all_to_all.16.near), channel_id=1, source_target_pairs={{0,1},{1,0},{2,3},{3,2},{4,5},{5,4},{6,7},{7,6},{8,9},{9,8},{10,11... | collective-permute-start | bytes 786440 | tf_op jit(solution)/shard_map/ppermute | solution.py:738
  123.7 1.2 collective-permute-done.6.far
  124.8 2.1 %shard_map.179 = (f32[27,64,64]{2,1,0:T(8,128)}, f32[27,64,64]{2,1,0:T(8,128)}, f32[64,64]{1,0:T(8,128)}, f32[1,1]{1,0:T(1,128)}) custom-call(s32[1,3]{1,0:T(1,128)S(1)} %copy-done.10, bf16[128,8,128]{2,1,0:T(8,128)(2,1)S(1)} %all_to_all.16.near, bf16[128,8,128]{2,1,0:T(8,128)(2,1)S(1)} %collective-permute-done.6.far), custom_call_target="tpu_custom_call" | custom-call | tf_op jit(solution)/shard_map/pallas_call | solution.py:36
  (31 shorter events, 0.3 us)
Async XLA Ops:
  0.6 1.2 copy-start
  1.9 0.7 copy-start.9
  3.9 4.2 %collective-permute-start = (bf16[10,16,128]{2,1,0:T(8,128)(2,1)S(1)}, bf16[10,16,128]{2,1,0:T(8,128)(2,1)S(1)}, u32[]{:S(2)}, u32[]{:S(2)}) collective-permute-start(bf16[10,16,128]{2,1,0:T(8,128)(2,1)S(1)} %get-tuple-element.33), channel_id=1, source_target_pairs={{0,1},{1,0},{2,3},{3,2},{4,5},{5,4},{6,7},{7,6},{8,9},{9,8},{10,11... | collective-permute-start | bytes 122888 | tf_op jit(solution)/shard_map/ppermute | solution.py:679
  8.1 12.7 %copy-start.7 = (bf16[27,64,64]{2,1,0:T(8,128)(2,1)S(1)}, bf16[27,64,64]{2,1,0:T(8,128)(2,1)}, u32[]{:S(2)}) copy-start(bf16[27,64,64]{2,1,0:T(8,128)(2,1)} %taps.1) | copy-start | bytes 663556
  8.8 3.2 %collective-permute-start.1 = (bf16[11,16,128]{2,1,0:T(8,128)(2,1)S(1)}, bf16[11,16,128]{2,1,0:T(8,128)(2,1)S(1)}, u32[]{:S(2)}, u32[]{:S(2)}) collective-permute-start(bf16[11,16,128]{2,1,0:T(8,128)(2,1)S(1)} %get-tuple-element.35), channel_id=1, source_target_pairs={{0,2},{2,4},{4,6},{6,8},{8,10},{10,12},{12,14},{1,3},{3,5},{5,7},{... | collective-permute-start | bytes 135176 | tf_op jit(solution)/shard_map/ppermute | solution.py:649
  10.6 5.0 %collective-permute-start.2 = (bf16[11,16,128]{2,1,0:T(8,128)(2,1)S(1)}, bf16[11,16,128]{2,1,0:T(8,128)(2,1)S(1)}, u32[]{:S(2)}, u32[]{:S(2)}) collective-permute-start(bf16[11,16,128]{2,1,0:T(8,128)(2,1)S(1)} %get-tuple-element.36), channel_id=1, source_target_pairs={{2,0},{4,2},{6,4},{8,6},{10,8},{12,10},{14,12},{3,1},{5,3},{7,5},{... | collective-permute-start | bytes 135176 | tf_op jit(solution)/shard_map/ppermute | solution.py:650
  11.9 12.4 %copy-start.3 = (bf16[16,224,160]{2,1,0:T(8,128)(2,1)S(1)}, bf16[16,224,160]{2,1,0:T(8,128)(2,1)}, u32[]{:S(2)}) copy-start(bf16[16,224,160]{2,1,0:T(8,128)(2,1)} %constant.6.clone.tables) | copy-start | bytes 3440644
  11.9 12.4 %copy-start.8 = (bf16[27,64,64]{2,1,0:T(8,128)(2,1)S(1)}, bf16[27,64,64]{2,1,0:T(8,128)(2,1)}, u32[]{:S(2)}) copy-start(bf16[27,64,64]{2,1,0:T(8,128)(2,1)} %param.16) | copy-start | bytes 663556
  12.0 12.4 %copy-start.11 = (bf16[256,64]{0,1:T(8,128)(2,1)S(1)}, bf16[256,64]{0,1:T(8,128)(2,1)}, u32[]{:S(2)}) copy-start(bf16[256,64]{0,1:T(8,128)(2,1)} %param.18) | copy-start | bytes 98308
  16.3 8.0 %collective-permute-start.3 = (bf16[14,16,128]{2,1,0:T(8,128)(2,1)S(1)}, bf16[14,16,128]{2,1,0:T(8,128)(2,1)S(1)}, u32[]{:S(2)}, u32[]{:S(2)}) collective-permute-start(bf16[14,16,128]{2,1,0:T(8,128)(2,1)S(1)} %get-tuple-element.40), channel_id=1, source_target_pairs={{0,16},{16,32},{32,48},{48,64},{64,80},{80,96},{96,112},{112,128},... | collective-permute-start | bytes 172040 | tf_op jit(solution)/shard_map/ppermute | solution.py:649
  19.5 4.9 %collective-permute-start.4 = (bf16[14,16,128]{2,1,0:T(8,128)(2,1)S(1)}, bf16[14,16,128]{2,1,0:T(8,128)(2,1)S(1)}, u32[]{:S(2)}, u32[]{:S(2)}) collective-permute-start(bf16[14,16,128]{2,1,0:T(8,128)(2,1)S(1)} %get-tuple-element.41), channel_id=1, source_target_pairs={{16,0},{32,16},{48,32},{64,48},{80,64},{96,80},{112,96},{128,112},... | collective-permute-start | bytes 172040 | tf_op jit(solution)/shard_map/ppermute | solution.py:650
  24.4 22.7 %copy-start.12 = (bf16[64,64]{1,0:T(8,128)(2,1)S(1)}, bf16[64,64]{1,0:T(8,128)(2,1)}, u32[]{:S(2)}) copy-start(bf16[64,64]{1,0:T(8,128)(2,1)} %param.17) | copy-start | bytes 24580
  24.4 22.8 %copy-start.13 = (f32[64]{0:T(128)S(1)}, f32[64]{0:T(128)}, u32[]{:S(2)}) copy-start(f32[64]{0:T(128)} %param.19) | copy-start | bytes 772
  24.4 22.8 %copy-start.14 = (f32[64]{0:T(128)S(1)}, f32[64]{0:T(128)}, u32[]{:S(2)}) copy-start(f32[64]{0:T(128)} %param.20) | copy-start | bytes 772
  24.4 22.9 %copy-start.10 = (s32[1,3]{1,0:T(1,128)S(1)}, s32[1,3]{1,0:T(1,128)}, u32[]{:S(2)}) copy-start(s32[1,3]{1,0:T(1,128)} %info.19) | copy-start | bytes 40
  27.5 1.0 copy-start.5
  28.5 31.4 %all-to-all-start = ((f32[256,1,128]{2,1,0:T(1,128)}), f32[256,1,128]{2,1,0:T(1,128)S(1)}, u32[]{:S(2)}, u32[]{:S(2)}) async-start(f32[256,1,128]{2,1,0:T(1,128)} %bitcast.7), calls=%async_computation | async-start | bytes 262144 | tf_op jit(solution)/shard_map/all_to_all | solution.py:643
  47.3 12.5 %copy-start.4 = (bf16[1,16,16,16,64]{4,3,2,1,0:T(8,128)(2,1)S(1)}, bf16[1,16,16,16,64]{4,3,2,1,0:T(8,128)(2,1)}, u32[]{:S(2)}) copy-start(bf16[1,16,16,16,64]{4,3,2,1,0:T(8,128)(2,1)} %param.12) | copy-start | bytes 1572868
  48.9 1.8 %copy-start.1 = (bf16[3,256,2304]{2,1,0:T(8,128)(2,1)}, bf16[3,256,2304]{2,1,0:T(8,128)(2,1)S(1)}, u32[]{:S(2)}) copy-start(bf16[3,256,2304]{2,1,0:T(8,128)(2,1)S(1)} %shard_map.175.turned) | copy-start | bytes 10616836
  59.9 2.0 %copy-start.2 = (bf16[3,256,2304]{2,1,0:T(8,128)(2,1)S(1)}, bf16[3,256,2304]{2,1,0:T(8,128)(2,1)}, u32[]{:S(2)}) copy-start(bf16[3,256,2304]{2,1,0:T(8,128)(2,1)} %copy-done.1) | copy-start | bytes 10616836
  61.9 1.2 copy-start.6
  70.3 3.0 %collective-permute-start.5 = (f32[2048,128]{1,0:T(8,128)S(1)}, f32[2048,128]{1,0:T(8,128)S(1)}, u32[]{:S(2)}, u32[]{:S(2)}) collective-permute-start(f32[2048,128]{1,0:T(8,128)S(1)} %get-tuple-element.49), channel_id=1, source_target_pairs={{0,1},{1,0},{2,3},{3,2},{4,5},{5,4},{6,7},{7,6},{8,9},{9,8},{10,11... | collective-permute-start | bytes 3145736 | tf_op jit(solution)/shard_map/ppermute | solution.py:729
  120.5 4.3 %collective-permute-start.6 = (bf16[128,8,128]{2,1,0:T(8,128)(2,1)S(1)}, bf16[128,8,128]{2,1,0:T(8,128)(2,1)S(1)}, u32[]{:S(2)}, u32[]{:S(2)}) collective-permute-start(bf16[128,8,128]{2,1,0:T(8,128)(2,1)S(1)} %all_to_all.16.near), channel_id=1, source_target_pairs={{0,1},{1,0},{2,3},{3,2},{4,5},{5,4},{6,7},{7,6},{8,9},{9,8},{10,11... | collective-permute-start | bytes 786440 | tf_op jit(solution)/shard_map/ppermute | solution.py:738

commit v3 on v2

--- a/solution.py
+++ b/solution.py
@@ -111,13 +111,22 @@
         out[32 + t] = jnp.concatenate([ref[8 + t, :, :64], ref[8 + t, :, 64:]], axis=0)
 
 
-def z_message(info, lat, out, pooled):
+def z_message(info, lat_in, out, pooled, lat, fetched):
     px, py, pz, kz = bits(info)
     zsel = 15 * (1 - kz)
+
+    def chunk(n):
+        part = pl.ds(4 * n, 4)
+        return pltpu.make_async_copy(lat_in.at[:, part], lat.at[:, part], fetched.at[n])
+
+    for n in range(4):
+        chunk(n).start()
     pick = lax.broadcasted_iota(jnp.int32, (16, 16, 64), 1) == zsel
     sums = [[None, None], [None, None]]
     faces = []
     for y in range(16):
+        if y % 4 == 0:
+            chunk(y // 4).wait()
         slab = lat[:, y].astype(F32)
         faces.append(jnp.sum(jnp.where(pick, slab, 0.0), axis=1)[None])
         for a in range(2):
@@ -475,7 +484,18 @@
     count = float(voxels * GROUP)
     scale = 1.0 / (voxels * 64)
 
-    def kernel(info, act, gathered, target, gain, bias, weight, weight_t, turned, patch, stats, predicted, mine, other, cotangent, payload, sent):
+    def kernel(
+        info, gathered, target, gain, bias, weight, weight_t, patch, stats, act_in, turned_in,
+        predicted, mine, other, cotangent, payload, act, turned, fetched, sent
+    ):
+        def chunk(n):
+            rows = pl.ds(256 * n, 256)
+            return pltpu.make_async_copy(act_in.at[rows], act.at[rows], fetched.at[n])
+
+        whole = pltpu.make_async_copy(turned_in, turned, fetched.at[8])
+        for n in range(8):
+            chunk(n).start()
+        whole.start()
         kz = lax.axis_index("cz")
         _, _, mean, rstd = moments(gathered, count)
         gains = jnp.zeros((1, 128), F32)
@@ -485,6 +505,7 @@
         cells = [[None] * 4, [None] * 4]
         for x in range(0, 16, 2):
             rows = slice(x * 128, x * 128 + 256)
+            chunk(x // 2).wait()
             normalized = (act[rows] - mean) * rstd
             shifted = normalized * gain[...] + bias[...]
             sigma = jax.nn.sigmoid(shifted)
@@ -530,6 +551,7 @@
         coarse = lax.dot_general(patch[...], split, (((0,), (0,)), ((), ())), preferred_element_type=F32)
         for t in range(27):
             store(t, 7, coarse[64 * t : 64 * t + 64])
+        whole.wait()
         for ox in range(3):
             windows = turned[:, :, 128 * ox : 128 * ox + 2048].reshape(768, 2048)
             products = jnp.dot(windows, cotangent[...], preferred_element_type=F32)
@@ -671,11 +693,13 @@
 def shards(latents, target, block_coords, timestep, conv_weight, coarse_weight, out_weight, time_weight, norm_gain, norm_bias):
     devices = lax.axis_size("bx") * lax.axis_size("by") * lax.axis_size("cz")
     voxels = devices * 4096
-    info = block_coords
+    info = pltpu.with_memory_space_constraint(block_coords, pltpu.HBM)
     lat = latents[0]
+    lat_far = pltpu.with_memory_space_constraint(lat, pltpu.HBM)
     lat_pairs = lat.reshape(16, 8, 2, 16, 64)
 
-    mz, pooled = call(z_message, [message(Z_TILES), like((16, 64), BF)], [info, lat])
+    scratch = [pltpu.VMEM((16, 16, 16, 64), BF), pltpu.SemaphoreType.DMA((4,))]
+    mz, pooled = call(z_message, [message(Z_TILES), like((16, 64), BF)], [info, lat_far], scratch, far_args=1)
     rz = lax.ppermute(mz, "cz", [(0, 1), (1, 0)])
     out = message(Y_TILES)
     down, up = call(
@@ -720,8 +744,16 @@
     predicted, mine, other = call(
         backward(voxels),
         [like((16, 8, 2, 16, 64), BF), like((2048, 128), F32), like((2048, 128), F32)],
-        [info, act, first, target.reshape(16, 8, 2, 16, 64), gain, bias] + weights + [turned, patch, stats],
-        [pltpu.VMEM((2048, 256), BF), pltpu.VMEM((2, 2048, 128), F32), pltpu.SemaphoreType.DMA((2,))],
+        [info, first, target.reshape(16, 8, 2, 16, 64), gain, bias] + weights + [patch, stats, act, turned],
+        [
+            pltpu.VMEM((2048, 256), BF),
+            pltpu.VMEM((2, 2048, 128), F32),
+            pltpu.VMEM((2048, 128), F32),
+            pltpu.VMEM((3, 256, 18 * 128), BF),
+            pltpu.SemaphoreType.DMA((9,)),
+            pltpu.SemaphoreType.DMA((2,)),
+        ],
+        far_args=2,
         far_outs=2,
     )
     swap = [(0, 1), (1, 0)]

time: 127 us -> 132 us (1.039)
  Pallas kernels: 23.3 us -> 29 us
    pallas_call x10, Pallas kernels: 23.3 us -> 29 us  [call(): pl.pallas_call(kernel, grid=(1,), out_shape=outs, in_specs=[pl.BlockSpec(...]
    unnamed x31 -> x27, local copies, waits for them, and re-layouts: 7.95 us -> 7.29 us
  transfers between devices with their start and end apart: 8 -> 8, of which waited for: 6 -> 5; matrix products, arithmetic and copies ran while one was open for 0% -> 0% of each run, Pallas kernels for 4% -> 4%
where the time goes in v3:
time: 132 us
  blocking collectives  44 us (33%)
  starting transfers between devices  33.2 us (25%)
  Pallas kernels  29 us (22%)
  waiting for transfers between devices  16.3 us (12%)
  local copies, waits for them, and re-layouts  7.29 us (6%)
  between operations  1.54 us (1%)
    pallas_call x10, Pallas kernels, call(): pl.pallas_call(kernel, grid=(1,), out_shape=outs, in_specs=[pl.BlockSpec(...  29 us
    all_to_all x1, blocking collectives, shards(): pieces = lax.all_to_all(pieces, CHIPS, 0, 0, tiled=True)  25 us
    all_to_all x1, blocking collectives, shards(): near = lax.all_to_all(copies, CHIPS, 0, 0, tiled=True)  19 us
    all_to_all x1, starting transfers between devices, exchange(): lax.all_to_all(rows.reshape(rows.shape[0], 1, 128), ('cz',) + CHIPS, 0, 0...  18.5 us
    all_to_all x1, waiting for transfers between devices, exchange(): lax.all_to_all(rows.reshape(rows.shape[0], 1, 128), ('cz',) + CHIPS, 0, 0...  9 us
    unnamed x27, local copies, waits for them, and re-layouts  7.29 us
    ppermute x2, starting transfers between devices, neighbours(): before = lax.ppermute(up, axis, [(i, i + 1) for i in range(ends)])  4.92 us
    ppermute x2, waiting for transfers between devices, neighbours(): after = lax.ppermute(down, axis, [(i + 1, i) for i in range(ends)])  3.58 us
  transfers between devices with their start and end apart: 8, of which 5 were waited for; matrix products, arithmetic and copies ran while one was open for 0% of the time, Pallas kernels for 4%

profile of v3, /device:TPU:1, one launch (start us, length us, event | category | flops | bytes accessed | tf_op | source)
XLA Modules:
  0.0 131.5 jit_solution(14788559434037640294)
XLA Ops:
  0.6 2.4 %shard_map.170 = (bf16[10,16,128]{2,1,0:T(8,128)(2,1)S(1)}, bf16[16,64]{1,0:T(8,128)(2,1)S(1)}) custom-call(s32[1,3]{1,0:T(1,128)} %info.19, bf16[16,16,16,64]{3,2,1,0:T(8,128)(2,1)} %bitcast.21), custom_call_target="tpu_custom_call" | custom-call | tf_op jit(solution)/shard_map/pallas_call | solution.py:36
  3.1 3.3 %collective-permute-start = (bf16[10,16,128]{2,1,0:T(8,128)(2,1)S(1)}, bf16[10,16,128]{2,1,0:T(8,128)(2,1)S(1)}, u32[]{:S(2)}, u32[]{:S(2)}) collective-permute-start(bf16[10,16,128]{2,1,0:T(8,128)(2,1)S(1)} %get-tuple-element.33), channel_id=1, source_target_pairs={{0,1},{1,0},{2,3},{3,2},{4,5},{5,4},{6,7},{7,6},{8,9},{9,8},{10,11... | collective-permute-start | bytes 122888 | tf_op jit(solution)/shard_map/ppermute | solution.py:703
  7.0 0.2 collective-permute-done.rz_in
  7.3 1.2 copy-done
  8.5 0.9 shard_map.171
  9.4 1.8 %collective-permute-start.1 = (bf16[11,16,128]{2,1,0:T(8,128)(2,1)S(1)}, bf16[11,16,128]{2,1,0:T(8,128)(2,1)S(1)}, u32[]{:S(2)}, u32[]{:S(2)}) collective-permute-start(bf16[11,16,128]{2,1,0:T(8,128)(2,1)S(1)} %get-tuple-element.35), channel_id=1, source_target_pairs={{0,2},{2,4},{4,6},{6,8},{8,10},{10,12},{12,14},{1,3},{3,5},{5,7},{... | collective-permute-start | bytes 135176 | tf_op jit(solution)/shard_map/ppermute | solution.py:671
  11.2 1.3 collective-permute-start.2
  12.6 3.6 %collective-permute-done.2.ryp_in = bf16[11,16,128]{2,1,0:T(8,128)(2,1)S(1)} collective-permute-done((bf16[11,16,128]{2,1,0:T(8,128)(2,1)S(1)}, bf16[11,16,128]{2,1,0:T(8,128)(2,1)S(1)}, u32[]{:S(2)}, u32[]{:S(2)}) %collective-permute-start.2) | collective-permute-done | bytes 45088 | tf_op jit(solution)/shard_map/ppermute | solution.py:672
  16.2 0.9 shard_map.173
  17.1 3.1 %collective-permute-start.3 = (bf16[14,16,128]{2,1,0:T(8,128)(2,1)S(1)}, bf16[14,16,128]{2,1,0:T(8,128)(2,1)S(1)}, u32[]{:S(2)}, u32[]{:S(2)}) collective-permute-start(bf16[14,16,128]{2,1,0:T(8,128)(2,1)S(1)} %get-tuple-element.40), channel_id=1, source_target_pairs={{0,16},{16,32},{32,48},{48,64},{64,80},{80,96},{96,112},{112,128},... | collective-permute-start | bytes 172040 | tf_op jit(solution)/shard_map/ppermute | solution.py:671
  20.2 1.3 collective-permute-start.4
  21.6 3.6 %shard_map.172 = (f32[1792,128]{1,0:T(8,128)S(1)}, bf16[3,16,9,16,128]{4,3,2,1,0:T(8,128)(2,1)S(1)}, f32[3,9,128]{2,1,0:T(8,128)S(1)}, bf16[2304,128]{1,0:T(8,128)(2,1)S(1)}) custom-call(s32[1,3]{1,0:T(1,128)} %info.19, bf16[16,8,2,16,64]{4,3,2,1,0:T(8,128)(2,1)S(1)} %bitcast.26, bf16[10,16,128]{2,1,0:T(8,128)(2,1)S(1)} %collective-permute-done.rz_in, ...), custom_call_target="tpu_custom_call" | custom-call | tf_op jit(solution)/shard_map/pallas_call | solution.py:36
  25.3 3.2 %shard_map.174 = (f32[2048,128]{1,0:T(8,128)S(1)}, bf16[2,3,9,16,128]{4,3,2,1,0:T(8,128)(2,1)S(1)}, bf16[16,1728]{1,0:T(8,128)(2,1)S(1)}, f32[256,128]{1,0:T(8,128)}) custom-call(s32[1,3]{1,0:T(1,128)} %info.19, bf16[3,16,9,16,128]{4,3,2,1,0:T(8,128)(2,1)S(1)} %get-tuple-element.37.near_low.near_high.scene, ...), custom_call_target="tpu_custom_call" | custom-call | tf_op jit(solution)/shard_map/pallas_call | solution.py:36
  28.5 1.0 copy-done.5
  29.5 18.5 %all-to-all-start = ((f32[256,1,128]{2,1,0:T(1,128)}), f32[256,1,128]{2,1,0:T(1,128)S(1)}, u32[]{:S(2)}, u32[]{:S(2)}) async-start(f32[256,1,128]{2,1,0:T(1,128)} %bitcast.7), calls=%async_computation | async-start | bytes 262144 | tf_op jit(solution)/shard_map/all_to_all | solution.py:665
  48.0 0.1 copy.21
  48.2 0.1 fusion.4
  48.2 1.8 %shard_map.175.turned_in = bf16[3,256,2304]{2,1,0:T(8,128)(2,1)S(1)} custom-call(s32[1,3]{1,0:T(1,128)} %info.19, bf16[3,16,9,16,128]{4,3,2,1,0:T(8,128)(2,1)S(1)} %get-tuple-element.37.near_low.near_high.scene, bf16[2,3,9,16,128]{4,3,2,1,0:T(8,128)(2,1)S(1)} %get-tuple-element.46.ends), custom_call_target="tpu_custom_call" | custom-call | tf_op jit(solution)/shard_map/pallas_call | solution.py:36
  50.0 1.7 %copy-done.1 = bf16[3,256,2304]{2,1,0:T(8,128)(2,1)} copy-done((bf16[3,256,2304]{2,1,0:T(8,128)(2,1)}, bf16[3,256,2304]{2,1,0:T(8,128)(2,1)S(1)}, u32[]{:S(2)}) %copy-start.1) | copy-done | bytes 3538968
  51.8 9.0 %all-to-all-done = f32[256,1,128]{2,1,0:T(1,128)S(1)} async-done(((f32[256,1,128]{2,1,0:T(1,128)}), f32[256,1,128]{2,1,0:T(1,128)S(1)}, u32[]{:S(2)}, u32[]{:S(2)}) %all-to-all-start) | async-done | bytes 131104 | tf_op jit(solution)/shard_map/all_to_all | solution.py:665
  60.8 2.0 %copy-done.2 = bf16[3,256,2304]{2,1,0:T(8,128)(2,1)S(1)} copy-done((bf16[3,256,2304]{2,1,0:T(8,128)(2,1)S(1)}, bf16[3,256,2304]{2,1,0:T(8,128)(2,1)}, u32[]{:S(2)}) %copy-start.2) | copy-done | bytes 3538968
  62.8 1.2 copy-done.6
  64.0 10.6 %shard_map.176 = (bf16[16,8,2,16,64]{4,3,2,1,0:T(8,128)(2,1)}, f32[2048,128]{1,0:T(8,128)S(1)}, f32[2048,128]{1,0:T(8,128)S(1)}) custom-call(s32[1,3]{1,0:T(1,128)} %info.19, f32[256,128]{1,0:T(8,128)S(1)} %bitcast.27, bf16[16,8,2,16,64]{4,3,2,1,0:T(8,128)(2,1)S(1)} %bitcast.30, f32[1,128]{1,0:T(1,128)S(1)} %get-tuple-element.62.gain, ...), custom_call_target="tpu_custom_call" | custom-call | tf_op jit(solution)/shard_map/pallas_call | solution.py:36
  74.6 0.7 collective-permute-start.5
  75.4 2.3 %collective-permute-done.5.other = f32[2048,128]{1,0:T(8,128)S(1)} collective-permute-done((f32[2048,128]{1,0:T(8,128)S(1)}, f32[2048,128]{1,0:T(8,128)S(1)}, u32[]{:S(2)}, u32[]{:S(2)}) %collective-permute-start.5) | collective-permute-done | bytes 1048608 | tf_op jit(solution)/shard_map/ppermute | solution.py:761
  77.7 1.5 %shard_map.177 = bf16[128,16,128]{2,1,0:T(8,128)(2,1)S(1)} custom-call(s32[1,3]{1,0:T(1,128)} %info.19, f32[2048,128]{1,0:T(8,128)S(1)} %get-tuple-element.48.mine, f32[2048,128]{1,0:T(8,128)S(1)} %collective-permute-done.5.other, f32[256,128]{1,0:T(8,128)S(1)} %bitcast.28, f32[1,128]{1,0:T(1,128)S(1)} %get-tuple-element.62.gain), custom_call_target="tpu_custom_call" | custom-call | tf_op jit(solution)/shard_map/pallas_call | solution.py:36
  79.2 25.0 %all_to_all.15.pieces = bf16[128,16,128]{2,1,0:T(8,128)(2,1)S(1)} all-to-all(bf16[128,16,128]{2,1,0:T(8,128)(2,1)S(1)} %shard_map.177), channel_id=1, replica_groups=mesh['bx'=16,'by'=8,'cz'=2] {'bx','by'}, dimensions={0} | all-to-all | bytes 1048576 | tf_op jit(solution)/shard_map/all_to_all | solution.py:763
  104.2 1.8 %shard_map.178 = (bf16[128,8,128]{2,1,0:T(8,128)(2,1)S(1)}, f32[64,256]{1,0:T(8,128)}, f32[1,64]{1,0:T(1,128)}, f32[1,64]{1,0:T(1,128)}) custom-call(s32[1,3]{1,0:T(1,128)} %info.19, bf16[128,16,128]{2,1,0:T(8,128)(2,1)S(1)} %all_to_all.15.pieces, f32[256,128]{1,0:T(8,128)S(1)} %bitcast.29, f32[1,128]{1,0:T(1,128)S(1)} %get-tuple-element.62.gain, ...), custom_call_target="tpu_custom_call" | custom-call | tf_op jit(solution)/shard_map/pallas_call | solution.py:36
  106.0 19.0 %all_to_all.16.near = bf16[128,8,128]{2,1,0:T(8,128)(2,1)S(1)} all-to-all(bf16[128,8,128]{2,1,0:T(8,128)(2,1)S(1)} %get-tuple-element.50), channel_id=1, replica_groups=mesh['bx'=16,'by'=8,'cz'=2] {'bx','by'}, dimensions={0} | all-to-all | bytes 524288 | tf_op jit(solution)/shard_map/all_to_all | solution.py:769
  125.0 3.2 %collective-permute-start.6 = (bf16[128,8,128]{2,1,0:T(8,128)(2,1)S(1)}, bf16[128,8,128]{2,1,0:T(8,128)(2,1)S(1)}, u32[]{:S(2)}, u32[]{:S(2)}) collective-permute-start(bf16[128,8,128]{2,1,0:T(8,128)(2,1)S(1)} %all_to_all.16.near), channel_id=1, source_target_pairs={{0,1},{1,0},{2,3},{3,2},{4,5},{5,4},{6,7},{7,6},{8,9},{9,8},{10,11... | collective-permute-start | bytes 786440 | tf_op jit(solution)/shard_map/ppermute | solution.py:770
  128.2 1.2 collective-permute-done.6.far
  129.4 2.2 %shard_map.179 = (f32[27,64,64]{2,1,0:T(8,128)}, f32[27,64,64]{2,1,0:T(8,128)}, f32[64,64]{1,0:T(8,128)}, f32[1,1]{1,0:T(1,128)}) custom-call(s32[1,3]{1,0:T(1,128)} %info.19, bf16[128,8,128]{2,1,0:T(8,128)(2,1)S(1)} %all_to_all.16.near, bf16[128,8,128]{2,1,0:T(8,128)(2,1)S(1)} %collective-permute-done.6.far), custom_call_target="tpu_custom_call" | custom-call | tf_op jit(solution)/shard_map/pallas_call | solution.py:36
  (27 shorter events, 0.2 us)
Async XLA Ops:
  3.1 4.2 %collective-permute-start = (bf16[10,16,128]{2,1,0:T(8,128)(2,1)S(1)}, bf16[10,16,128]{2,1,0:T(8,128)(2,1)S(1)}, u32[]{:S(2)}, u32[]{:S(2)}) collective-permute-start(bf16[10,16,128]{2,1,0:T(8,128)(2,1)S(1)} %get-tuple-element.33), channel_id=1, source_target_pairs={{0,1},{1,0},{2,3},{3,2},{4,5},{5,4},{6,7},{7,6},{8,9},{9,8},{10,11... | collective-permute-start | bytes 122888 | tf_op jit(solution)/shard_map/ppermute | solution.py:703
  7.3 1.2 copy-start
  8.5 13.1 %copy-start.7 = (bf16[27,64,64]{2,1,0:T(8,128)(2,1)S(1)}, bf16[27,64,64]{2,1,0:T(8,128)(2,1)}, u32[]{:S(2)}) copy-start(bf16[27,64,64]{2,1,0:T(8,128)(2,1)} %taps.1) | copy-start | bytes 663556
  9.4 3.2 %collective-permute-start.1 = (bf16[11,16,128]{2,1,0:T(8,128)(2,1)S(1)}, bf16[11,16,128]{2,1,0:T(8,128)(2,1)S(1)}, u32[]{:S(2)}, u32[]{:S(2)}) collective-permute-start(bf16[11,16,128]{2,1,0:T(8,128)(2,1)S(1)} %get-tuple-element.35), channel_id=1, source_target_pairs={{0,2},{2,4},{4,6},{6,8},{8,10},{10,12},{12,14},{1,3},{3,5},{5,7},{... | collective-permute-start | bytes 135176 | tf_op jit(solution)/shard_map/ppermute | solution.py:671
  11.2 5.0 %collective-permute-start.2 = (bf16[11,16,128]{2,1,0:T(8,128)(2,1)S(1)}, bf16[11,16,128]{2,1,0:T(8,128)(2,1)S(1)}, u32[]{:S(2)}, u32[]{:S(2)}) collective-permute-start(bf16[11,16,128]{2,1,0:T(8,128)(2,1)S(1)} %get-tuple-element.36), channel_id=1, source_target_pairs={{2,0},{4,2},{6,4},{8,6},{10,8},{12,10},{14,12},{3,1},{5,3},{7,5},{... | collective-permute-start | bytes 135176 | tf_op jit(solution)/shard_map/ppermute | solution.py:672
  12.6 12.6 %copy-start.3 = (bf16[16,224,160]{2,1,0:T(8,128)(2,1)S(1)}, bf16[16,224,160]{2,1,0:T(8,128)(2,1)}, u32[]{:S(2)}) copy-start(bf16[16,224,160]{2,1,0:T(8,128)(2,1)} %constant.6.clone.tables) | copy-start | bytes 3440644
  12.6 12.6 %copy-start.8 = (bf16[27,64,64]{2,1,0:T(8,128)(2,1)S(1)}, bf16[27,64,64]{2,1,0:T(8,128)(2,1)}, u32[]{:S(2)}) copy-start(bf16[27,64,64]{2,1,0:T(8,128)(2,1)} %param.16) | copy-start | bytes 663556
  12.6 12.6 %copy-start.9 = (bf16[256,64]{0,1:T(8,128)(2,1)S(1)}, bf16[256,64]{0,1:T(8,128)(2,1)}, u32[]{:S(2)}) copy-start(bf16[256,64]{0,1:T(8,128)(2,1)} %param.18) | copy-start | bytes 98308
  17.1 8.1 %collective-permute-start.3 = (bf16[14,16,128]{2,1,0:T(8,128)(2,1)S(1)}, bf16[14,16,128]{2,1,0:T(8,128)(2,1)S(1)}, u32[]{:S(2)}, u32[]{:S(2)}) collective-permute-start(bf16[14,16,128]{2,1,0:T(8,128)(2,1)S(1)} %get-tuple-element.40), channel_id=1, source_target_pairs={{0,16},{16,32},{32,48},{48,64},{64,80},{80,96},{96,112},{112,128},... | collective-permute-start | bytes 172040 | tf_op jit(solution)/shard_map/ppermute | solution.py:671
  20.2 5.0 %collective-permute-start.4 = (bf16[14,16,128]{2,1,0:T(8,128)(2,1)S(1)}, bf16[14,16,128]{2,1,0:T(8,128)(2,1)S(1)}, u32[]{:S(2)}, u32[]{:S(2)}) collective-permute-start(bf16[14,16,128]{2,1,0:T(8,128)(2,1)S(1)} %get-tuple-element.41), channel_id=1, source_target_pairs={{16,0},{32,16},{48,32},{64,48},{80,64},{96,80},{112,96},{128,112},... | collective-permute-start | bytes 172040 | tf_op jit(solution)/shard_map/ppermute | solution.py:672
  25.3 22.7 %copy-start.10 = (bf16[64,64]{1,0:T(8,128)(2,1)S(1)}, bf16[64,64]{1,0:T(8,128)(2,1)}, u32[]{:S(2)}) copy-start(bf16[64,64]{1,0:T(8,128)(2,1)} %param.17) | copy-start | bytes 24580
  25.3 22.8 %copy-start.11 = (f32[64]{0:T(128)S(1)}, f32[64]{0:T(128)}, u32[]{:S(2)}) copy-start(f32[64]{0:T(128)} %param.19) | copy-start | bytes 772
  25.3 22.8 %copy-start.12 = (f32[64]{0:T(128)S(1)}, f32[64]{0:T(128)}, u32[]{:S(2)}) copy-start(f32[64]{0:T(128)} %param.20) | copy-start | bytes 772
  28.5 1.0 copy-start.5
  29.5 31.3 %all-to-all-start = ((f32[256,1,128]{2,1,0:T(1,128)}), f32[256,1,128]{2,1,0:T(1,128)S(1)}, u32[]{:S(2)}, u32[]{:S(2)}) async-start(f32[256,1,128]{2,1,0:T(1,128)} %bitcast.7), calls=%async_computation | async-start | bytes 262144 | tf_op jit(solution)/shard_map/all_to_all | solution.py:665
  48.2 12.5 %copy-start.4 = (bf16[1,16,16,16,64]{4,3,2,1,0:T(8,128)(2,1)S(1)}, bf16[1,16,16,16,64]{4,3,2,1,0:T(8,128)(2,1)}, u32[]{:S(2)}) copy-start(bf16[1,16,16,16,64]{4,3,2,1,0:T(8,128)(2,1)} %param.12) | copy-start | bytes 1572868
  50.0 1.7 %copy-start.1 = (bf16[3,256,2304]{2,1,0:T(8,128)(2,1)}, bf16[3,256,2304]{2,1,0:T(8,128)(2,1)S(1)}, u32[]{:S(2)}) copy-start(bf16[3,256,2304]{2,1,0:T(8,128)(2,1)S(1)} %shard_map.175.turned_in) | copy-start | bytes 10616836
  60.8 2.0 %copy-start.2 = (bf16[3,256,2304]{2,1,0:T(8,128)(2,1)S(1)}, bf16[3,256,2304]{2,1,0:T(8,128)(2,1)}, u32[]{:S(2)}) copy-start(bf16[3,256,2304]{2,1,0:T(8,128)(2,1)} %copy-done.1) | copy-start | bytes 10616836
  62.8 1.2 copy-start.6
  74.6 3.0 %collective-permute-start.5 = (f32[2048,128]{1,0:T(8,128)S(1)}, f32[2048,128]{1,0:T(8,128)S(1)}, u32[]{:S(2)}, u32[]{:S(2)}) collective-permute-start(f32[2048,128]{1,0:T(8,128)S(1)} %get-tuple-element.49), channel_id=1, source_target_pairs={{0,1},{1,0},{2,3},{3,2},{4,5},{5,4},{6,7},{7,6},{8,9},{9,8},{10,11... | collective-permute-start | bytes 3145736 | tf_op jit(solution)/shard_map/ppermute | solution.py:761
  125.0 4.3 %collective-permute-start.6 = (bf16[128,8,128]{2,1,0:T(8,128)(2,1)S(1)}, bf16[128,8,128]{2,1,0:T(8,128)(2,1)S(1)}, u32[]{:S(2)}, u32[]{:S(2)}) collective-permute-start(bf16[128,8,128]{2,1,0:T(8,128)(2,1)S(1)} %all_to_all.16.near), channel_id=1, source_target_pairs={{0,1},{1,0},{2,3},{3,2},{4,5},{5,4},{6,7},{7,6},{8,9},{9,8},{10,11... | collective-permute-start | bytes 786440 | tf_op jit(solution)/shard_map/ppermute | solution.py:770

commit v4 on v3

--- a/solution.py
+++ b/solution.py
@@ -44,6 +44,10 @@
     )(*args)
 
 
+def in_hbm(array):
+    return pltpu.with_memory_space_constraint(array, pltpu.HBM)
+
+
 def like(shape, dtype):
     return jax.ShapeDtypeStruct(shape, dtype)
 
@@ -111,22 +115,13 @@
         out[32 + t] = jnp.concatenate([ref[8 + t, :, :64], ref[8 + t, :, 64:]], axis=0)
 
 
-def z_message(info, lat_in, out, pooled, lat, fetched):
+def z_message(info, lat, out, pooled):
     px, py, pz, kz = bits(info)
     zsel = 15 * (1 - kz)
-
-    def chunk(n):
-        part = pl.ds(4 * n, 4)
-        return pltpu.make_async_copy(lat_in.at[:, part], lat.at[:, part], fetched.at[n])
-
-    for n in range(4):
-        chunk(n).start()
     pick = lax.broadcasted_iota(jnp.int32, (16, 16, 64), 1) == zsel
     sums = [[None, None], [None, None]]
     faces = []
     for y in range(16):
-        if y % 4 == 0:
-            chunk(y // 4).wait()
         slab = lat[:, y].astype(F32)
         faces.append(jnp.sum(jnp.where(pick, slab, 0.0), axis=1)[None])
         for a in range(2):
@@ -486,7 +481,7 @@
 
     def kernel(
         info, gathered, target, gain, bias, weight, weight_t, patch, stats, act_in, turned_in,
-        predicted, mine, other, cotangent, payload, act, turned, fetched, sent
+        predicted, payload, other, cotangent, act, turned, fetched, sent
     ):
         def chunk(n):
             rows = pl.ds(256 * n, 256)
@@ -574,11 +569,9 @@
             payload.at[half][pl.ds(14, 128, stride=16), :] = wide
             slot = jnp.where(kz == half, 0, 1)
             payload.at[slot][pl.ds(15, 128, stride=16), :] = stats[128 * half : 128 * half + 128]
-        copies = [pltpu.make_async_copy(payload.at[n], ref, sent.at[n]) for n, ref in ((0, mine), (1, other))]
-        for copy in copies:
-            copy.start()
-        for copy in copies:
-            copy.wait()
+        copy = pltpu.make_async_copy(payload.at[1], other, sent)
+        copy.start()
+        copy.wait()
 
     return kernel
 
@@ -594,7 +587,7 @@
 
     def kernel(info, mine, other, gathered, gain, out):
         _, _, _, rstd = moments(gathered, total_count)
-        total = (mine[...] + other[...]).reshape(-1, 16, 128)
+        total = (mine[0] + other[...]).reshape(-1, 16, 128)
         m1, m2 = slopes(total[0, 14:15], gain[...], count)
         row = lax.broadcasted_iota(jnp.int32, total.shape, 1)
         lane = lax.broadcasted_iota(jnp.int32, total.shape, 2)
@@ -693,13 +686,11 @@
 def shards(latents, target, block_coords, timestep, conv_weight, coarse_weight, out_weight, time_weight, norm_gain, norm_bias):
     devices = lax.axis_size("bx") * lax.axis_size("by") * lax.axis_size("cz")
     voxels = devices * 4096
-    info = pltpu.with_memory_space_constraint(block_coords, pltpu.HBM)
+    info = block_coords
     lat = latents[0]
-    lat_far = pltpu.with_memory_space_constraint(lat, pltpu.HBM)
     lat_pairs = lat.reshape(16, 8, 2, 16, 64)
 
-    scratch = [pltpu.VMEM((16, 16, 16, 64), BF), pltpu.SemaphoreType.DMA((4,))]
-    mz, pooled = call(z_message, [message(Z_TILES), like((16, 64), BF)], [info, lat_far], scratch, far_args=1)
+    mz, pooled = call(z_message, [message(Z_TILES), like((16, 64), BF)], [in_hbm(info), lat])
     rz = lax.ppermute(mz, "cz", [(0, 1), (1, 0)])
     out = message(Y_TILES)
     down, up = call(
@@ -728,7 +719,7 @@
     tables = jnp.asarray(coarse_table(), BF)
     act, ends, patch, stats = call(
         forward,
-        [like((2048, 128), F32), like((2, 3, 9, 16, 128), BF), like((16, 1728), BF), like((devices, 128), F32)],
+        [pltpu.HBM((2048, 128), F32), like((2, 3, 9, 16, 128), BF), like((16, 1728), BF), like((devices, 128), F32)],
         [info, scene, scene, raw, columns, rz, rym, ryp, rxm, rxp, pooled, taps]
         + [coarse_weight.reshape(1728, 64), temb, time_weight.T, tables],
         [pltpu.VMEM((2, 128, 128), F32), pltpu.VMEM((224, 160), BF), pltpu.SemaphoreType.DMA]
@@ -738,28 +729,27 @@
         far_args=1,
     )
     first = exchange(stats)
-    (turned,) = call(turn, [like((3, 256, 18 * 128), BF)], [info, scene, ends])
+    (turned,) = call(turn, [pltpu.HBM((3, 256, 18 * 128), BF)], [info, scene, ends])
     gain, bias = twice(norm_gain), twice(norm_bias)
     weights = [diagonal(out_weight), diagonal(out_weight.T)]
-    predicted, mine, other = call(
+    predicted, payload, other = call(
         backward(voxels),
-        [like((16, 8, 2, 16, 64), BF), like((2048, 128), F32), like((2048, 128), F32)],
-        [info, first, target.reshape(16, 8, 2, 16, 64), gain, bias] + weights + [patch, stats, act, turned],
+        [like((16, 8, 2, 16, 64), BF), like((2, 2048, 128), F32), like((2048, 128), F32)],
+        [info, first, target.reshape(16, 8, 2, 16, 64), gain, bias] + weights + [patch, stats, in_hbm(act), in_hbm(turned)],
         [
             pltpu.VMEM((2048, 256), BF),
-            pltpu.VMEM((2, 2048, 128), F32),
             pltpu.VMEM((2048, 128), F32),
             pltpu.VMEM((3, 256, 18 * 128), BF),
             pltpu.SemaphoreType.DMA((9,)),
-            pltpu.SemaphoreType.DMA((2,)),
+            pltpu.SemaphoreType.DMA,
         ],
         far_args=2,
-        far_outs=2,
+        far_outs=1,
     )
     swap = [(0, 1), (1, 0)]
     chips = devices // 2
     other = lax.ppermute(other, "cz", swap)
-    (pieces,) = call(pair_add(voxels), [like((chips, 16, 128), BF)], [info, mine, other, first, gain])
+    (pieces,) = call(pair_add(voxels), [like((chips, 16, 128), BF)], [info, payload, other, first, gain])
     pieces = lax.all_to_all(pieces, CHIPS, 0, 0, tiled=True)
     copies, grad_time, grad_gain, grad_bias = call(
         combine(voxels),

time: 132 us -> 127 us (0.962)
  local copies, waits for them, and re-layouts: 7.29 us -> 3.23 us
  Pallas kernels: 29 us -> 27.6 us
    unnamed x27 -> x25, local copies, waits for them, and re-layouts: 7.29 us -> 3.23 us
    pallas_call x10, Pallas kernels: 29 us -> 27.6 us  [call(): pl.pallas_call(kernel, grid=(1,), out_shape=outs, in_specs=[pl.BlockSpec(...]
  transfers between devices with their start and end apart: 8 -> 8, of which waited for: 5 -> 6; matrix products, arithmetic and copies ran while one was open for 0% -> 0% of each run, Pallas kernels for 4% -> 5%
where the time goes in v4:
time: 127 us
  blocking collectives  44 us (35%)
  starting transfers between devices  33.5 us (26%)
  Pallas kernels  27.6 us (22%)
  waiting for transfers between devices  16.6 us (13%)
  local copies, waits for them, and re-layouts  3.23 us (3%)
  between operations  1.49 us (1%)
    pallas_call x10, Pallas kernels, call(): pl.pallas_call(kernel, grid=(1,), out_shape=outs, in_specs=[pl.BlockSpec(...  27.6 us
    all_to_all x1, blocking collectives, shards(): pieces = lax.all_to_all(pieces, CHIPS, 0, 0, tiled=True)  25 us
    all_to_all x1, blocking collectives, shards(): near = lax.all_to_all(copies, CHIPS, 0, 0, tiled=True)  19 us
    all_to_all x1, starting transfers between devices, exchange(): lax.all_to_all(rows.reshape(rows.shape[0], 1, 128), ('cz',) + CHIPS, 0, 0...  18.6 us
    all_to_all x1, waiting for transfers between devices, exchange(): lax.all_to_all(rows.reshape(rows.shape[0], 1, 128), ('cz',) + CHIPS, 0, 0...  9.25 us
    ppermute x2, starting transfers between devices, neighbours(): before = lax.ppermute(up, axis, [(i, i + 1) for i in range(ends)])  5.06 us
    ppermute x2, waiting for transfers between devices, neighbours(): after = lax.ppermute(down, axis, [(i + 1, i) for i in range(ends)])  3.66 us
    ppermute x1, starting transfers between devices, shards(): rz = lax.ppermute(mz, 'cz', [(0, 1), (1, 0)])  3.33 us
  transfers between devices with their start and end apart: 8, of which 6 were waited for; matrix products, arithmetic and copies ran while one was open for 0% of the time, Pallas kernels for 5%

profile of v4, /device:TPU:1, one launch (start us, length us, event | category | flops | bytes accessed | tf_op | source)
XLA Modules:
  0.0 126.6 jit_solution(6765491019176032067)
XLA Ops:
  0.6 1.2 copy-done
  1.9 1.5 %shard_map.170 = (bf16[10,16,128]{2,1,0:T(8,128)(2,1)S(1)}, bf16[16,64]{1,0:T(8,128)(2,1)S(1)}) custom-call(s32[1,3]{1,0:T(1,128)} %info.19, bf16[16,16,16,64]{3,2,1,0:T(8,128)(2,1)S(1)} %bitcast.21), custom_call_target="tpu_custom_call" | custom-call | tf_op jit(solution)/shard_map/pallas_call | solution.py:36
  3.3 3.3 %collective-permute-start = (bf16[10,16,128]{2,1,0:T(8,128)(2,1)S(1)}, bf16[10,16,128]{2,1,0:T(8,128)(2,1)S(1)}, u32[]{:S(2)}, u32[]{:S(2)}) collective-permute-start(bf16[10,16,128]{2,1,0:T(8,128)(2,1)S(1)} %get-tuple-element.33), channel_id=1, source_target_pairs={{0,1},{1,0},{2,3},{3,2},{4,5},{5,4},{6,7},{7,6},{8,9},{9,8},{10,11... | collective-permute-start | bytes 122888 | tf_op jit(solution)/shard_map/ppermute | solution.py:694
  7.3 0.2 collective-permute-done.rz_in
  7.5 1.2 copy-done.1
  8.8 0.7 copy-done.6
  9.4 0.7 shard_map.171
  10.1 1.9 %collective-permute-start.1 = (bf16[11,16,128]{2,1,0:T(8,128)(2,1)S(1)}, bf16[11,16,128]{2,1,0:T(8,128)(2,1)S(1)}, u32[]{:S(2)}, u32[]{:S(2)}) collective-permute-start(bf16[11,16,128]{2,1,0:T(8,128)(2,1)S(1)} %get-tuple-element.35), channel_id=1, source_target_pairs={{0,2},{2,4},{4,6},{6,8},{8,10},{10,12},{12,14},{1,3},{3,5},{5,7},{... | collective-permute-start | bytes 135176 | tf_op jit(solution)/shard_map/ppermute | solution.py:664
  12.1 1.3 %collective-permute-start.2 = (bf16[11,16,128]{2,1,0:T(8,128)(2,1)S(1)}, bf16[11,16,128]{2,1,0:T(8,128)(2,1)S(1)}, u32[]{:S(2)}, u32[]{:S(2)}) collective-permute-start(bf16[11,16,128]{2,1,0:T(8,128)(2,1)S(1)} %get-tuple-element.36), channel_id=1, source_target_pairs={{2,0},{4,2},{6,4},{8,6},{10,8},{12,10},{14,12},{3,1},{5,3},{7,5},{... | collective-permute-start | bytes 135176 | tf_op jit(solution)/shard_map/ppermute | solution.py:665
  13.4 3.6 %collective-permute-done.2.ryp_in = bf16[11,16,128]{2,1,0:T(8,128)(2,1)S(1)} collective-permute-done((bf16[11,16,128]{2,1,0:T(8,128)(2,1)S(1)}, bf16[11,16,128]{2,1,0:T(8,128)(2,1)S(1)}, u32[]{:S(2)}, u32[]{:S(2)}) %collective-permute-start.2) | collective-permute-done | bytes 45088 | tf_op jit(solution)/shard_map/ppermute | solution.py:665
  17.0 0.8 shard_map.173
  17.8 3.1 %collective-permute-start.3 = (bf16[14,16,128]{2,1,0:T(8,128)(2,1)S(1)}, bf16[14,16,128]{2,1,0:T(8,128)(2,1)S(1)}, u32[]{:S(2)}, u32[]{:S(2)}) collective-permute-start(bf16[14,16,128]{2,1,0:T(8,128)(2,1)S(1)} %get-tuple-element.40), channel_id=1, source_target_pairs={{0,16},{16,32},{32,48},{48,64},{64,80},{80,96},{96,112},{112,128},... | collective-permute-start | bytes 172040 | tf_op jit(solution)/shard_map/ppermute | solution.py:664
  20.9 1.3 %collective-permute-start.4 = (bf16[14,16,128]{2,1,0:T(8,128)(2,1)S(1)}, bf16[14,16,128]{2,1,0:T(8,128)(2,1)S(1)}, u32[]{:S(2)}, u32[]{:S(2)}) collective-permute-start(bf16[14,16,128]{2,1,0:T(8,128)(2,1)S(1)} %get-tuple-element.41), channel_id=1, source_target_pairs={{16,0},{32,16},{48,32},{64,48},{80,64},{96,80},{112,96},{128,112},... | collective-permute-start | bytes 172040 | tf_op jit(solution)/shard_map/ppermute | solution.py:665
  22.3 3.5 %shard_map.172 = (f32[1792,128]{1,0:T(8,128)S(1)}, bf16[3,16,9,16,128]{4,3,2,1,0:T(8,128)(2,1)S(1)}, f32[3,9,128]{2,1,0:T(8,128)S(1)}, bf16[2304,128]{1,0:T(8,128)(2,1)S(1)}) custom-call(s32[1,3]{1,0:T(1,128)S(1)} %copy-done.6, bf16[16,8,2,16,64]{4,3,2,1,0:T(8,128)(2,1)S(1)} %bitcast.26, bf16[10,16,128]{2,1,0:T(8,128)(2,1)S(1)} %collective-permute-done.rz_in, ...), custom_call_target="tpu_custom_call" | custom-call | tf_op jit(solution)/shard_map/pallas_call | solution.py:36
  25.8 0.1 collective-permute-done.4.rxp_in
  25.9 3.2 %shard_map.174 = (f32[2048,128]{1,0:T(8,128)}, bf16[2,3,9,16,128]{4,3,2,1,0:T(8,128)(2,1)S(1)}, bf16[16,1728]{1,0:T(8,128)(2,1)S(1)}, f32[256,128]{1,0:T(8,128)}) custom-call(s32[1,3]{1,0:T(1,128)S(1)} %copy-done.6, bf16[3,16,9,16,128]{4,3,2,1,0:T(8,128)(2,1)S(1)} %get-tuple-element.37.near_low.near_high.scene, ...), custom_call_target="tpu_custom_call" | custom-call | tf_op jit(solution)/shard_map/pallas_call | solution.py:36
  29.1 18.6 %all-to-all-start = ((f32[256,1,128]{2,1,0:T(1,128)}), f32[256,1,128]{2,1,0:T(1,128)S(1)}, u32[]{:S(2)}, u32[]{:S(2)}) async-start(f32[256,1,128]{2,1,0:T(1,128)} %bitcast.7), calls=%async_computation | async-start | bytes 262144 | tf_op jit(solution)/shard_map/all_to_all | solution.py:658
  47.7 0.1 copy.21
  47.9 0.1 maximum_bitcast_fusion
  47.9 0.1 fusion.4
  48.0 3.3 %shard_map.175.turned_in = bf16[3,256,2304]{2,1,0:T(8,128)(2,1)} custom-call(s32[1,3]{1,0:T(1,128)S(1)} %copy-done.7, bf16[3,16,9,16,128]{4,3,2,1,0:T(8,128)(2,1)S(1)} %get-tuple-element.37.near_low.near_high.scene, bf16[2,3,9,16,128]{4,3,2,1,0:T(8,128)(2,1)S(1)} %get-tuple-element.46.ends), custom_call_target="tpu_custom_call" | custom-call | tf_op jit(solution)/shard_map/pallas_call | solution.py:36
  51.3 9.2 %all-to-all-done = f32[256,1,128]{2,1,0:T(1,128)S(1)} async-done(((f32[256,1,128]{2,1,0:T(1,128)}), f32[256,1,128]{2,1,0:T(1,128)S(1)}, u32[]{:S(2)}, u32[]{:S(2)}) %all-to-all-start) | async-done | bytes 131104 | tf_op jit(solution)/shard_map/all_to_all | solution.py:658
  60.5 9.5 %shard_map.176 = (bf16[16,8,2,16,64]{4,3,2,1,0:T(8,128)(2,1)}, f32[2,2048,128]{2,1,0:T(8,128)S(1)}, f32[2048,128]{1,0:T(8,128)S(1)}) custom-call(s32[1,3]{1,0:T(1,128)S(1)} %copy-done.7, f32[256,128]{1,0:T(8,128)S(1)} %bitcast.27, bf16[16,8,2,16,64]{4,3,2,1,0:T(8,128)(2,1)S(1)} %bitcast.30, f32[1,128]{1,0:T(1,128)S(1)} %get-tuple-element.62.gain, ...), custom_call_target="tpu_custom_call" | custom-call | tf_op jit(solution)/shard_map/pallas_call | solution.py:36
  70.1 0.7 collective-permute-start.5
  70.8 2.3 %collective-permute-done.5.other = f32[2048,128]{1,0:T(8,128)S(1)} collective-permute-done((f32[2048,128]{1,0:T(8,128)S(1)}, f32[2048,128]{1,0:T(8,128)S(1)}, u32[]{:S(2)}, u32[]{:S(2)}) %collective-permute-start.5) | collective-permute-done | bytes 1048608 | tf_op jit(solution)/shard_map/ppermute | solution.py:751
  73.1 1.4 %shard_map.177 = bf16[128,16,128]{2,1,0:T(8,128)(2,1)S(1)} custom-call(s32[1,3]{1,0:T(1,128)S(1)} %copy-done.7, f32[2,2048,128]{2,1,0:T(8,128)S(1)} %get-tuple-element.48.mine, f32[2048,128]{1,0:T(8,128)S(1)} %collective-permute-done.5.other, f32[256,128]{1,0:T(8,128)S(1)} %bitcast.28, f32[1,128]{1,0:T(1,128)S(1)} %get-tuple-element.62.gain), custom_call_target="tpu_custom_call" | custom-call | tf_op jit(solution)/shard_map/pallas_call | solution.py:36
  74.5 25.0 %all_to_all.15.pieces = bf16[128,16,128]{2,1,0:T(8,128)(2,1)S(1)} all-to-all(bf16[128,16,128]{2,1,0:T(8,128)(2,1)S(1)} %shard_map.177), channel_id=1, replica_groups=mesh['bx'=16,'by'=8,'cz'=2] {'bx','by'}, dimensions={0} | all-to-all | bytes 1048576 | tf_op jit(solution)/shard_map/all_to_all | solution.py:753
  99.5 1.7 %shard_map.178 = (bf16[128,8,128]{2,1,0:T(8,128)(2,1)S(1)}, f32[64,256]{1,0:T(8,128)}, f32[1,64]{1,0:T(1,128)}, f32[1,64]{1,0:T(1,128)}) custom-call(s32[1,3]{1,0:T(1,128)S(1)} %copy-done.7, bf16[128,16,128]{2,1,0:T(8,128)(2,1)S(1)} %all_to_all.15.pieces, f32[256,128]{1,0:T(8,128)S(1)} %bitcast.29, f32[1,128]{1,0:T(1,128)S(1)} %get-tuple-element.62.gain, ...), custom_call_target="tpu_custom_call" | custom-call | tf_op jit(solution)/shard_map/pallas_call | solution.py:36
  101.2 19.0 %all_to_all.16.near = bf16[128,8,128]{2,1,0:T(8,128)(2,1)S(1)} all-to-all(bf16[128,8,128]{2,1,0:T(8,128)(2,1)S(1)} %get-tuple-element.50), channel_id=1, replica_groups=mesh['bx'=16,'by'=8,'cz'=2] {'bx','by'}, dimensions={0} | all-to-all | bytes 524288 | tf_op jit(solution)/shard_map/all_to_all | solution.py:759
  120.2 3.2 %collective-permute-start.6 = (bf16[128,8,128]{2,1,0:T(8,128)(2,1)S(1)}, bf16[128,8,128]{2,1,0:T(8,128)(2,1)S(1)}, u32[]{:S(2)}, u32[]{:S(2)}) collective-permute-start(bf16[128,8,128]{2,1,0:T(8,128)(2,1)S(1)} %all_to_all.16.near), channel_id=1, source_target_pairs={{0,1},{1,0},{2,3},{3,2},{4,5},{5,4},{6,7},{7,6},{8,9},{9,8},{10,11... | collective-permute-start | bytes 786440 | tf_op jit(solution)/shard_map/ppermute | solution.py:760
  123.4 1.2 collective-permute-done.6.far
  124.6 2.1 %shard_map.179 = (f32[27,64,64]{2,1,0:T(8,128)}, f32[27,64,64]{2,1,0:T(8,128)}, f32[64,64]{1,0:T(8,128)}, f32[1,1]{1,0:T(1,128)}) custom-call(s32[1,3]{1,0:T(1,128)S(1)} %copy-done.7, bf16[128,8,128]{2,1,0:T(8,128)(2,1)S(1)} %all_to_all.16.near, bf16[128,8,128]{2,1,0:T(8,128)(2,1)S(1)} %collective-permute-done.6.far), custom_call_target="tpu_custom_call" | custom-call | tf_op jit(solution)/shard_map/pallas_call | solution.py:36
  (25 shorter events, 0.1 us)
Async XLA Ops:
  0.6 1.2 copy-start
  3.3 4.2 %collective-permute-start = (bf16[10,16,128]{2,1,0:T(8,128)(2,1)S(1)}, bf16[10,16,128]{2,1,0:T(8,128)(2,1)S(1)}, u32[]{:S(2)}, u32[]{:S(2)}) collective-permute-start(bf16[10,16,128]{2,1,0:T(8,128)(2,1)S(1)} %get-tuple-element.33), channel_id=1, source_target_pairs={{0,1},{1,0},{2,3},{3,2},{4,5},{5,4},{6,7},{7,6},{8,9},{9,8},{10,11... | collective-permute-start | bytes 122888 | tf_op jit(solution)/shard_map/ppermute | solution.py:694
  7.5 1.2 copy-start.1
  8.8 0.7 copy-start.6
  9.4 12.8 %copy-start.4 = (bf16[27,64,64]{2,1,0:T(8,128)(2,1)S(1)}, bf16[27,64,64]{2,1,0:T(8,128)(2,1)}, u32[]{:S(2)}) copy-start(bf16[27,64,64]{2,1,0:T(8,128)(2,1)} %taps.1) | copy-start | bytes 663556
  10.1 15.8 %copy-start.2 = (bf16[16,224,160]{2,1,0:T(8,128)(2,1)S(1)}, bf16[16,224,160]{2,1,0:T(8,128)(2,1)}, u32[]{:S(2)}) copy-start(bf16[16,224,160]{2,1,0:T(8,128)(2,1)} %constant.6.clone.tables) | copy-start | bytes 3440644
  10.1 15.8 %copy-start.5 = (bf16[27,64,64]{2,1,0:T(8,128)(2,1)S(1)}, bf16[27,64,64]{2,1,0:T(8,128)(2,1)}, u32[]{:S(2)}) copy-start(bf16[27,64,64]{2,1,0:T(8,128)(2,1)} %param.16) | copy-start | bytes 663556
  10.1 15.8 %copy-start.8 = (bf16[256,64]{0,1:T(8,128)(2,1)S(1)}, bf16[256,64]{0,1:T(8,128)(2,1)}, u32[]{:S(2)}) copy-start(bf16[256,64]{0,1:T(8,128)(2,1)} %param.18) | copy-start | bytes 98308
  10.1 3.3 %collective-permute-start.1 = (bf16[11,16,128]{2,1,0:T(8,128)(2,1)S(1)}, bf16[11,16,128]{2,1,0:T(8,128)(2,1)S(1)}, u32[]{:S(2)}, u32[]{:S(2)}) collective-permute-start(bf16[11,16,128]{2,1,0:T(8,128)(2,1)S(1)} %get-tuple-element.35), channel_id=1, source_target_pairs={{0,2},{2,4},{4,6},{6,8},{8,10},{10,12},{12,14},{1,3},{3,5},{5,7},{... | collective-permute-start | bytes 135176 | tf_op jit(solution)/shard_map/ppermute | solution.py:664
  12.1 5.0 %collective-permute-start.2 = (bf16[11,16,128]{2,1,0:T(8,128)(2,1)S(1)}, bf16[11,16,128]{2,1,0:T(8,128)(2,1)S(1)}, u32[]{:S(2)}, u32[]{:S(2)}) collective-permute-start(bf16[11,16,128]{2,1,0:T(8,128)(2,1)S(1)} %get-tuple-element.36), channel_id=1, source_target_pairs={{2,0},{4,2},{6,4},{8,6},{10,8},{12,10},{14,12},{3,1},{5,3},{7,5},{... | collective-permute-start | bytes 135176 | tf_op jit(solution)/shard_map/ppermute | solution.py:665
  17.8 8.0 %collective-permute-start.3 = (bf16[14,16,128]{2,1,0:T(8,128)(2,1)S(1)}, bf16[14,16,128]{2,1,0:T(8,128)(2,1)S(1)}, u32[]{:S(2)}, u32[]{:S(2)}) collective-permute-start(bf16[14,16,128]{2,1,0:T(8,128)(2,1)S(1)} %get-tuple-element.40), channel_id=1, source_target_pairs={{0,16},{16,32},{32,48},{48,64},{64,80},{80,96},{96,112},{112,128},... | collective-permute-start | bytes 172040 | tf_op jit(solution)/shard_map/ppermute | solution.py:664
  20.9 4.9 %collective-permute-start.4 = (bf16[14,16,128]{2,1,0:T(8,128)(2,1)S(1)}, bf16[14,16,128]{2,1,0:T(8,128)(2,1)S(1)}, u32[]{:S(2)}, u32[]{:S(2)}) collective-permute-start(bf16[14,16,128]{2,1,0:T(8,128)(2,1)S(1)} %get-tuple-element.41), channel_id=1, source_target_pairs={{16,0},{32,16},{48,32},{64,48},{80,64},{96,80},{112,96},{128,112},... | collective-permute-start | bytes 172040 | tf_op jit(solution)/shard_map/ppermute | solution.py:665
  25.9 21.9 %copy-start.9 = (bf16[64,64]{1,0:T(8,128)(2,1)S(1)}, bf16[64,64]{1,0:T(8,128)(2,1)}, u32[]{:S(2)}) copy-start(bf16[64,64]{1,0:T(8,128)(2,1)} %param.17) | copy-start | bytes 24580
  25.9 21.9 %copy-start.10 = (f32[64]{0:T(128)S(1)}, f32[64]{0:T(128)}, u32[]{:S(2)}) copy-start(f32[64]{0:T(128)} %param.19) | copy-start | bytes 772
  25.9 21.9 %copy-start.11 = (f32[64]{0:T(128)S(1)}, f32[64]{0:T(128)}, u32[]{:S(2)}) copy-start(f32[64]{0:T(128)} %param.20) | copy-start | bytes 772
  25.9 22.1 %copy-start.7 = (s32[1,3]{1,0:T(1,128)S(1)}, s32[1,3]{1,0:T(1,128)}, u32[]{:S(2)}) copy-start(s32[1,3]{1,0:T(1,128)} %info.19) | copy-start | bytes 40
  29.1 31.4 %all-to-all-start = ((f32[256,1,128]{2,1,0:T(1,128)}), f32[256,1,128]{2,1,0:T(1,128)S(1)}, u32[]{:S(2)}, u32[]{:S(2)}) async-start(f32[256,1,128]{2,1,0:T(1,128)} %bitcast.7), calls=%async_computation | async-start | bytes 262144 | tf_op jit(solution)/shard_map/all_to_all | solution.py:658
  48.0 12.5 %copy-start.3 = (bf16[1,16,16,16,64]{4,3,2,1,0:T(8,128)(2,1)S(1)}, bf16[1,16,16,16,64]{4,3,2,1,0:T(8,128)(2,1)}, u32[]{:S(2)}) copy-start(bf16[1,16,16,16,64]{4,3,2,1,0:T(8,128)(2,1)} %param.12) | copy-start | bytes 1572868
  70.1 3.0 %collective-permute-start.5 = (f32[2048,128]{1,0:T(8,128)S(1)}, f32[2048,128]{1,0:T(8,128)S(1)}, u32[]{:S(2)}, u32[]{:S(2)}) collective-permute-start(f32[2048,128]{1,0:T(8,128)S(1)} %get-tuple-element.49), channel_id=1, source_target_pairs={{0,1},{1,0},{2,3},{3,2},{4,5},{5,4},{6,7},{7,6},{8,9},{9,8},{10,11... | collective-permute-start | bytes 3145736 | tf_op jit(solution)/shard_map/ppermute | solution.py:751
  120.2 4.3 %collective-permute-start.6 = (bf16[128,8,128]{2,1,0:T(8,128)(2,1)S(1)}, bf16[128,8,128]{2,1,0:T(8,128)(2,1)S(1)}, u32[]{:S(2)}, u32[]{:S(2)}) collective-permute-start(bf16[128,8,128]{2,1,0:T(8,128)(2,1)S(1)} %all_to_all.16.near), channel_id=1, source_target_pairs={{0,1},{1,0},{2,3},{3,2},{4,5},{5,4},{6,7},{7,6},{8,9},{9,8},{10,11... | collective-permute-start | bytes 786440 | tf_op jit(solution)/shard_map/ppermute | solution.py:760

commit v5 on v4

--- a/solution.py
+++ b/solution.py
@@ -309,8 +309,8 @@
 
 def forward(
     info, near_low, near_high, raw, columns, rz_in, rym_in, ryp_in, rxm_in, rxp_in, pooled, weight,
-    coarse_weight, temb, time_weight, tables, act, ends, patch_out, stats,
-    shift, table, arrived, rz, rym, ryp, rxm, rxp
+    coarse_weight, temb, time_weight, tables, ends, patch_out, stats, act_out,
+    act, sent, shift, table, arrived, rz, rym, ryp, rxm, rxp
 ):
     px, py, pz, kz = bits(info)
     fetch = pltpu.make_async_copy(tables.at[8 * px + 4 * py + 2 * pz + kz], table, arrived)
@@ -403,6 +403,10 @@
             pieces.append(jnp.concatenate([low[dk : dk + 8], high[dk : dk + 8]], axis=0).reshape(256, 128))
     edges = jnp.dot(jnp.concatenate(pieces, axis=1), weight[...], preferred_element_type=F32)
 
+    def leave(n):
+        rows = pl.ds(512 * n, 512)
+        return pltpu.make_async_copy(act.at[rows], act_out.at[rows], sent.at[n])
+
     total = jnp.zeros((1, 128), F32)
     squares = jnp.zeros((1, 128), F32)
     for x in range(16):
@@ -416,6 +420,8 @@
         a = x // 8
         value = jnp.concatenate([(value[b] + added[2 * a + b][None])[None] for b in range(2)], axis=0).reshape(128, 128)
         act[x * 128 : x * 128 + 128] = value
+        if x % 4 == 3:
+            leave(x // 4).start()
         total = total + jnp.sum(value, axis=0, keepdims=True)
         squares = squares + jnp.sum(value * value, axis=0, keepdims=True)
     shift[...] = jnp.zeros(shift.shape, F32)
@@ -444,14 +450,19 @@
     row = jnp.where(lane < 64, total + pltpu.roll(total, 64, 1), jnp.where(lane % 2 == 0, pairs, 0.0))
     for u in range(2):
         stats[128 * u : 128 * u + 128] = shift[u].T + row
-
-
-def turn(info, scene, ends, turned):
+    for n in range(4):
+        leave(n).wait()
+
+
+def turn(info, scene, ends, turned_out, turned, sent):
     for oz in range(3):
         for xp in range(18):
             for dk in range(2):
                 tile = scene[oz, xp - 1, dk : dk + 8] if 1 <= xp <= 16 else ends[xp // 17, oz, dk : dk + 8]
                 turned[oz, 128 * dk : 128 * dk + 128, 128 * xp : 128 * xp + 128] = tile.reshape(128, 128).T
+        pltpu.make_async_copy(turned.at[oz], turned_out.at[oz], sent.at[oz]).start()
+    for oz in range(3):
+        pltpu.make_async_copy(turned.at[oz], turned_out.at[oz], sent.at[oz]).wait()
 
 
 def pair_sum(row):
@@ -481,16 +492,19 @@
 
     def kernel(
         info, gathered, target, gain, bias, weight, weight_t, patch, stats, act_in, turned_in,
-        predicted, payload, other, cotangent, act, turned, fetched, sent
+        payload, other, predicted_out, cotangent, act, turned, predicted, fetched, sent, shown_sent
     ):
         def chunk(n):
             rows = pl.ds(256 * n, 256)
             return pltpu.make_async_copy(act_in.at[rows], act.at[rows], fetched.at[n])
 
+        def show(x):
+            part = pl.ds(x, 2)
+            return pltpu.make_async_copy(predicted.at[part], predicted_out.at[part], shown_sent.at[x // 2])
+
         whole = pltpu.make_async_copy(turned_in, turned, fetched.at[8])
         for n in range(8):
             chunk(n).start()
-        whole.start()
         kz = lax.axis_index("cz")
         _, _, mean, rstd = moments(gathered, count)
         gains = jnp.zeros((1, 128), F32)
@@ -501,6 +515,8 @@
         for x in range(0, 16, 2):
             rows = slice(x * 128, x * 128 + 256)
             chunk(x // 2).wait()
+            if x == 4:
+                whole.start()
             normalized = (act[rows] - mean) * rstd
             shifted = normalized * gain[...] + bias[...]
             sigma = jax.nn.sigmoid(shifted)
@@ -511,6 +527,7 @@
             shown = output.astype(BF).reshape(2, 8, 16, 128)
             predicted[x : x + 2, :, 0] = shown[..., :64]
             predicted[x : x + 2, :, 1] = shown[..., 64:]
+            show(x).start()
             upstream = (2.0 * scale * residue).astype(BF)
             back = jnp.dot(upstream, weight_t[...], preferred_element_type=F32)
             value = back * sigma * (1.0 + shifted * (1.0 - sigma))
@@ -571,6 +588,8 @@
             payload.at[slot][pl.ds(15, 128, stride=16), :] = stats[128 * half : 128 * half + 128]
         copy = pltpu.make_async_copy(payload.at[1], other, sent)
         copy.start()
+        for x in range(0, 16, 2):
+            show(x).wait()
         copy.wait()
 
     return kernel
@@ -690,7 +709,7 @@
     lat = latents[0]
     lat_pairs = lat.reshape(16, 8, 2, 16, 64)
 
-    mz, pooled = call(z_message, [message(Z_TILES), like((16, 64), BF)], [in_hbm(info), lat])
+    mz, pooled = call(z_message, [message(Z_TILES), like((16, 64), BF)], [info, lat])
     rz = lax.ppermute(mz, "cz", [(0, 1), (1, 0)])
     out = message(Y_TILES)
     down, up = call(
@@ -717,34 +736,44 @@
     )
     pair = (3, 2, 9, 16, 128)
     tables = jnp.asarray(coarse_table(), BF)
-    act, ends, patch, stats = call(
+    ends, patch, stats, act = call(
         forward,
-        [pltpu.HBM((2048, 128), F32), like((2, 3, 9, 16, 128), BF), like((16, 1728), BF), like((devices, 128), F32)],
+        [like((2, 3, 9, 16, 128), BF), like((16, 1728), BF), like((devices, 128), F32), pltpu.HBM((2048, 128), F32)],
         [info, scene, scene, raw, columns, rz, rym, ryp, rxm, rxp, pooled, taps]
         + [coarse_weight.reshape(1728, 64), temb, time_weight.T, tables],
-        [pltpu.VMEM((2, 128, 128), F32), pltpu.VMEM((224, 160), BF), pltpu.SemaphoreType.DMA]
+        [pltpu.VMEM((2048, 128), F32), pltpu.SemaphoreType.DMA((4,))]
+        + [pltpu.VMEM((2, 128, 128), F32), pltpu.VMEM((224, 160), BF), pltpu.SemaphoreType.DMA]
         + planes
         + [plane(X_TILES), plane(X_TILES)],
         [pl.BlockSpec(pair, lambda i: (0, 0, 0, 0, 0)), pl.BlockSpec(pair, lambda i: (0, 7, 0, 0, 0))],
         far_args=1,
+        far_outs=1,
     )
     first = exchange(stats)
-    (turned,) = call(turn, [pltpu.HBM((3, 256, 18 * 128), BF)], [info, scene, ends])
+    (turned,) = call(
+        turn,
+        [pltpu.HBM((3, 256, 18 * 128), BF)],
+        [info, scene, ends],
+        [pltpu.VMEM((3, 256, 18 * 128), BF), pltpu.SemaphoreType.DMA((3,))],
+        far_outs=1,
+    )
     gain, bias = twice(norm_gain), twice(norm_bias)
     weights = [diagonal(out_weight), diagonal(out_weight.T)]
-    predicted, payload, other = call(
+    payload, other, predicted = call(
         backward(voxels),
-        [like((16, 8, 2, 16, 64), BF), like((2, 2048, 128), F32), like((2048, 128), F32)],
+        [like((2, 2048, 128), F32), like((2048, 128), F32), pltpu.HBM((16, 8, 2, 16, 64), BF)],
         [info, first, target.reshape(16, 8, 2, 16, 64), gain, bias] + weights + [patch, stats, in_hbm(act), in_hbm(turned)],
         [
             pltpu.VMEM((2048, 256), BF),
             pltpu.VMEM((2048, 128), F32),
             pltpu.VMEM((3, 256, 18 * 128), BF),
+            pltpu.VMEM((16, 8, 2, 16, 64), BF),
             pltpu.SemaphoreType.DMA((9,)),
             pltpu.SemaphoreType.DMA,
+            pltpu.SemaphoreType.DMA((8,)),
         ],
         far_args=2,
-        far_outs=1,
+        far_outs=2,
     )
     swap = [(0, 1), (1, 0)]
     chips = devices // 2

time: 127 us -> 125 us (0.984)
    unnamed x25 -> x23, local copies, waits for them, and re-layouts: 3.23 us -> 2.01 us
where the time goes in v5:
time: 125 us
  blocking collectives  44 us (35%)
  starting transfers between devices  33.5 us (27%)
  Pallas kernels  26.6 us (21%)
  waiting for transfers between devices  17.2 us (14%)
  local copies, waits for them, and re-layouts  2.01 us (2%)
  between operations  1.5 us (1%)
    pallas_call x10, Pallas kernels, call(): pl.pallas_call(kernel, grid=(1,), out_shape=outs, in_specs=[pl.BlockSpec(...  26.6 us
    all_to_all x1, blocking collectives, shards(): pieces = lax.all_to_all(pieces, CHIPS, 0, 0, tiled=True)  25.1 us
    all_to_all x1, blocking collectives, shards(): near = lax.all_to_all(copies, CHIPS, 0, 0, tiled=True)  19 us
    all_to_all x1, starting transfers between devices, exchange(): lax.all_to_all(rows.reshape(rows.shape[0], 1, 128), ('cz',) + CHIPS, 0, 0...  18.6 us
    all_to_all x1, waiting for transfers between devices, exchange(): lax.all_to_all(rows.reshape(rows.shape[0], 1, 128), ('cz',) + CHIPS, 0, 0...  9.81 us
    ppermute x2, starting transfers between devices, neighbours(): before = lax.ppermute(up, axis, [(i, i + 1) for i in range(ends)])  5.06 us
    ppermute x2, waiting for transfers between devices, neighbours(): after = lax.ppermute(down, axis, [(i + 1, i) for i in range(ends)])  3.67 us
    ppermute x1, starting transfers between devices, shards(): rz = lax.ppermute(mz, 'cz', [(0, 1), (1, 0)])  3.33 us
  transfers between devices with their start and end apart: 8, of which 6 were waited for; matrix products, arithmetic and copies ran while one was open for 0% of the time, Pallas kernels for 5%

profile of v5, /device:TPU:1, one launch (start us, length us, event | category | flops | bytes accessed | tf_op | source)
XLA Modules:
  0.0 125.0 jit_solution(9308983824892390357)
XLA Ops:
  0.6 1.2 copy-done
  1.9 0.7 copy-done.5
  2.5 1.4 %shard_map.170 = (bf16[10,16,128]{2,1,0:T(8,128)(2,1)S(1)}, bf16[16,64]{1,0:T(8,128)(2,1)S(1)}) custom-call(s32[1,3]{1,0:T(1,128)S(1)} %copy-done.5, bf16[16,16,16,64]{3,2,1,0:T(8,128)(2,1)S(1)} %bitcast.21), custom_call_target="tpu_custom_call" | custom-call | tf_op jit(solution)/shard_map/pallas_call | solution.py:36
  3.9 3.3 %collective-permute-start = (bf16[10,16,128]{2,1,0:T(8,128)(2,1)S(1)}, bf16[10,16,128]{2,1,0:T(8,128)(2,1)S(1)}, u32[]{:S(2)}, u32[]{:S(2)}) collective-permute-start(bf16[10,16,128]{2,1,0:T(8,128)(2,1)S(1)} %get-tuple-element.33), channel_id=1, source_target_pairs={{0,1},{1,0},{2,3},{3,2},{4,5},{5,4},{6,7},{7,6},{8,9},{9,8},{10,11... | collective-permute-start | bytes 122888 | tf_op jit(solution)/shard_map/ppermute | solution.py:713
  7.9 0.2 collective-permute-done.rz_in
  8.1 0.7 shard_map.171
  8.8 1.9 %collective-permute-start.1 = (bf16[11,16,128]{2,1,0:T(8,128)(2,1)S(1)}, bf16[11,16,128]{2,1,0:T(8,128)(2,1)S(1)}, u32[]{:S(2)}, u32[]{:S(2)}) collective-permute-start(bf16[11,16,128]{2,1,0:T(8,128)(2,1)S(1)} %get-tuple-element.35), channel_id=1, source_target_pairs={{0,2},{2,4},{4,6},{6,8},{8,10},{10,12},{12,14},{1,3},{3,5},{5,7},{... | collective-permute-start | bytes 135176 | tf_op jit(solution)/shard_map/ppermute | solution.py:683
  10.7 1.3 %collective-permute-start.2 = (bf16[11,16,128]{2,1,0:T(8,128)(2,1)S(1)}, bf16[11,16,128]{2,1,0:T(8,128)(2,1)S(1)}, u32[]{:S(2)}, u32[]{:S(2)}) collective-permute-start(bf16[11,16,128]{2,1,0:T(8,128)(2,1)S(1)} %get-tuple-element.36), channel_id=1, source_target_pairs={{2,0},{4,2},{6,4},{8,6},{10,8},{12,10},{14,12},{3,1},{5,3},{7,5},{... | collective-permute-start | bytes 135176 | tf_op jit(solution)/shard_map/ppermute | solution.py:684
  12.1 3.6 %collective-permute-done.2.ryp_in = bf16[11,16,128]{2,1,0:T(8,128)(2,1)S(1)} collective-permute-done((bf16[11,16,128]{2,1,0:T(8,128)(2,1)S(1)}, bf16[11,16,128]{2,1,0:T(8,128)(2,1)S(1)}, u32[]{:S(2)}, u32[]{:S(2)}) %collective-permute-start.2) | collective-permute-done | bytes 45088 | tf_op jit(solution)/shard_map/ppermute | solution.py:684
  15.7 0.8 shard_map.173
  16.5 3.1 %collective-permute-start.3 = (bf16[14,16,128]{2,1,0:T(8,128)(2,1)S(1)}, bf16[14,16,128]{2,1,0:T(8,128)(2,1)S(1)}, u32[]{:S(2)}, u32[]{:S(2)}) collective-permute-start(bf16[14,16,128]{2,1,0:T(8,128)(2,1)S(1)} %get-tuple-element.40), channel_id=1, source_target_pairs={{0,16},{16,32},{32,48},{48,64},{64,80},{80,96},{96,112},{112,128},... | collective-permute-start | bytes 172040 | tf_op jit(solution)/shard_map/ppermute | solution.py:683
  19.6 1.3 %collective-permute-start.4 = (bf16[14,16,128]{2,1,0:T(8,128)(2,1)S(1)}, bf16[14,16,128]{2,1,0:T(8,128)(2,1)S(1)}, u32[]{:S(2)}, u32[]{:S(2)}) collective-permute-start(bf16[14,16,128]{2,1,0:T(8,128)(2,1)S(1)} %get-tuple-element.41), channel_id=1, source_target_pairs={{16,0},{32,16},{48,32},{64,48},{80,64},{96,80},{112,96},{128,112},... | collective-permute-start | bytes 172040 | tf_op jit(solution)/shard_map/ppermute | solution.py:684
  20.9 3.5 %shard_map.172 = (f32[1792,128]{1,0:T(8,128)S(1)}, bf16[3,16,9,16,128]{4,3,2,1,0:T(8,128)(2,1)S(1)}, f32[3,9,128]{2,1,0:T(8,128)S(1)}, bf16[2304,128]{1,0:T(8,128)(2,1)S(1)}) custom-call(s32[1,3]{1,0:T(1,128)S(1)} %copy-done.5, bf16[16,8,2,16,64]{4,3,2,1,0:T(8,128)(2,1)S(1)} %bitcast.26, bf16[10,16,128]{2,1,0:T(8,128)(2,1)S(1)} %collective-permute-done.rz_in, ...), custom_call_target="tpu_custom_call" | custom-call | tf_op jit(solution)/shard_map/pallas_call | solution.py:36
  24.5 0.1 collective-permute-done.4.rxp_in
  24.5 0.0 copy-start.9
  24.6 3.8 %shard_map.174 = (bf16[2,3,9,16,128]{4,3,2,1,0:T(8,128)(2,1)S(1)}, bf16[16,1728]{1,0:T(8,128)(2,1)S(1)}, f32[256,128]{1,0:T(8,128)}, f32[2048,128]{1,0:T(8,128)}) custom-call(s32[1,3]{1,0:T(1,128)S(1)} %copy-done.5, bf16[3,16,9,16,128]{4,3,2,1,0:T(8,128)(2,1)S(1)} %get-tuple-element.37.near_low.near_high.scene, ...), custom_call_target="tpu_custom_call" | custom-call | tf_op jit(solution)/shard_map/pallas_call | solution.py:36
  28.4 18.6 %all-to-all-start = ((f32[256,1,128]{2,1,0:T(1,128)}), f32[256,1,128]{2,1,0:T(1,128)S(1)}, u32[]{:S(2)}, u32[]{:S(2)}) async-start(f32[256,1,128]{2,1,0:T(1,128)} %bitcast.7), calls=%async_computation | async-start | bytes 262144 | tf_op jit(solution)/shard_map/all_to_all | solution.py:677
  47.0 0.1 copy.21
  47.1 0.1 maximum_bitcast_fusion
  47.2 0.1 fusion.4
  47.3 2.7 %shard_map.175.turned_in = bf16[3,256,2304]{2,1,0:T(8,128)(2,1)} custom-call(s32[1,3]{1,0:T(1,128)S(1)} %copy-done.6, bf16[3,16,9,16,128]{4,3,2,1,0:T(8,128)(2,1)S(1)} %get-tuple-element.37.near_low.near_high.scene, bf16[2,3,9,16,128]{4,3,2,1,0:T(8,128)(2,1)S(1)} %get-tuple-element.46.ends), custom_call_target="tpu_custom_call" | custom-call | tf_op jit(solution)/shard_map/pallas_call | solution.py:36
  50.0 9.8 %all-to-all-done = f32[256,1,128]{2,1,0:T(1,128)S(1)} async-done(((f32[256,1,128]{2,1,0:T(1,128)}), f32[256,1,128]{2,1,0:T(1,128)S(1)}, u32[]{:S(2)}, u32[]{:S(2)}) %all-to-all-start) | async-done | bytes 131104 | tf_op jit(solution)/shard_map/all_to_all | solution.py:677
  59.8 8.7 %shard_map.176 = (f32[2,2048,128]{2,1,0:T(8,128)S(1)}, f32[2048,128]{1,0:T(8,128)S(1)}, bf16[16,8,2,16,64]{4,3,2,1,0:T(8,128)(2,1)}) custom-call(s32[1,3]{1,0:T(1,128)S(1)} %copy-done.6, f32[256,128]{1,0:T(8,128)S(1)} %bitcast.27, bf16[16,8,2,16,64]{4,3,2,1,0:T(8,128)(2,1)S(1)} %bitcast.30, f32[1,128]{1,0:T(1,128)S(1)} %get-tuple-element.62.gain, ...), custom_call_target="tpu_custom_call" | custom-call | tf_op jit(solution)/shard_map/pallas_call | solution.py:36
  68.4 0.7 collective-permute-start.5
  69.2 2.3 %collective-permute-done.5.other = f32[2048,128]{1,0:T(8,128)S(1)} collective-permute-done((f32[2048,128]{1,0:T(8,128)S(1)}, f32[2048,128]{1,0:T(8,128)S(1)}, u32[]{:S(2)}, u32[]{:S(2)}) %collective-permute-start.5) | collective-permute-done | bytes 1048608 | tf_op jit(solution)/shard_map/ppermute | solution.py:780
  71.4 1.4 %shard_map.177 = bf16[128,16,128]{2,1,0:T(8,128)(2,1)S(1)} custom-call(s32[1,3]{1,0:T(1,128)S(1)} %copy-done.6, f32[2,2048,128]{2,1,0:T(8,128)S(1)} %get-tuple-element.48.mine, f32[2048,128]{1,0:T(8,128)S(1)} %collective-permute-done.5.other, f32[256,128]{1,0:T(8,128)S(1)} %bitcast.28, f32[1,128]{1,0:T(1,128)S(1)} %get-tuple-element.62.gain), custom_call_target="tpu_custom_call" | custom-call | tf_op jit(solution)/shard_map/pallas_call | solution.py:36
  72.8 25.1 %all_to_all.15.pieces = bf16[128,16,128]{2,1,0:T(8,128)(2,1)S(1)} all-to-all(bf16[128,16,128]{2,1,0:T(8,128)(2,1)S(1)} %shard_map.177), channel_id=1, replica_groups=mesh['bx'=16,'by'=8,'cz'=2] {'bx','by'}, dimensions={0} | all-to-all | bytes 1048576 | tf_op jit(solution)/shard_map/all_to_all | solution.py:782
  97.9 1.7 %shard_map.178 = (bf16[128,8,128]{2,1,0:T(8,128)(2,1)S(1)}, f32[64,256]{1,0:T(8,128)}, f32[1,64]{1,0:T(1,128)}, f32[1,64]{1,0:T(1,128)}) custom-call(s32[1,3]{1,0:T(1,128)S(1)} %copy-done.6, bf16[128,16,128]{2,1,0:T(8,128)(2,1)S(1)} %all_to_all.15.pieces, f32[256,128]{1,0:T(8,128)S(1)} %bitcast.29, f32[1,128]{1,0:T(1,128)S(1)} %get-tuple-element.62.gain, ...), custom_call_target="tpu_custom_call" | custom-call | tf_op jit(solution)/shard_map/pallas_call | solution.py:36
  99.6 19.0 %all_to_all.16.near = bf16[128,8,128]{2,1,0:T(8,128)(2,1)S(1)} all-to-all(bf16[128,8,128]{2,1,0:T(8,128)(2,1)S(1)} %get-tuple-element.50), channel_id=1, replica_groups=mesh['bx'=16,'by'=8,'cz'=2] {'bx','by'}, dimensions={0} | all-to-all | bytes 524288 | tf_op jit(solution)/shard_map/all_to_all | solution.py:788
  118.6 3.2 %collective-permute-start.6 = (bf16[128,8,128]{2,1,0:T(8,128)(2,1)S(1)}, bf16[128,8,128]{2,1,0:T(8,128)(2,1)S(1)}, u32[]{:S(2)}, u32[]{:S(2)}) collective-permute-start(bf16[128,8,128]{2,1,0:T(8,128)(2,1)S(1)} %all_to_all.16.near), channel_id=1, source_target_pairs={{0,1},{1,0},{2,3},{3,2},{4,5},{5,4},{6,7},{7,6},{8,9},{9,8},{10,11... | collective-permute-start | bytes 786440 | tf_op jit(solution)/shard_map/ppermute | solution.py:789
  121.8 1.2 collective-permute-done.6.far
  122.9 2.1 %shard_map.179 = (f32[27,64,64]{2,1,0:T(8,128)}, f32[27,64,64]{2,1,0:T(8,128)}, f32[64,64]{1,0:T(8,128)}, f32[1,1]{1,0:T(1,128)}) custom-call(s32[1,3]{1,0:T(1,128)S(1)} %copy-done.6, bf16[128,8,128]{2,1,0:T(8,128)(2,1)S(1)} %all_to_all.16.near, bf16[128,8,128]{2,1,0:T(8,128)(2,1)S(1)} %collective-permute-done.6.far), custom_call_target="tpu_custom_call" | custom-call | tf_op jit(solution)/shard_map/pallas_call | solution.py:36
  (23 shorter events, 0.1 us)
Async XLA Ops:
  0.6 1.2 copy-start
  1.9 0.7 copy-start.5
  3.9 4.2 %collective-permute-start = (bf16[10,16,128]{2,1,0:T(8,128)(2,1)S(1)}, bf16[10,16,128]{2,1,0:T(8,128)(2,1)S(1)}, u32[]{:S(2)}, u32[]{:S(2)}) collective-permute-start(bf16[10,16,128]{2,1,0:T(8,128)(2,1)S(1)} %get-tuple-element.33), channel_id=1, source_target_pairs={{0,1},{1,0},{2,3},{3,2},{4,5},{5,4},{6,7},{7,6},{8,9},{9,8},{10,11... | collective-permute-start | bytes 122888 | tf_op jit(solution)/shard_map/ppermute | solution.py:713
  8.1 12.8 %copy-start.3 = (bf16[27,64,64]{2,1,0:T(8,128)(2,1)S(1)}, bf16[27,64,64]{2,1,0:T(8,128)(2,1)}, u32[]{:S(2)}) copy-start(bf16[27,64,64]{2,1,0:T(8,128)(2,1)} %taps.1) | copy-start | bytes 663556
  8.8 15.8 %copy-start.1 = (bf16[16,224,160]{2,1,0:T(8,128)(2,1)S(1)}, bf16[16,224,160]{2,1,0:T(8,128)(2,1)}, u32[]{:S(2)}) copy-start(bf16[16,224,160]{2,1,0:T(8,128)(2,1)} %constant.6.clone.tables) | copy-start | bytes 3440644
  8.8 15.8 %copy-start.4 = (bf16[27,64,64]{2,1,0:T(8,128)(2,1)S(1)}, bf16[27,64,64]{2,1,0:T(8,128)(2,1)}, u32[]{:S(2)}) copy-start(bf16[27,64,64]{2,1,0:T(8,128)(2,1)} %param.16) | copy-start | bytes 663556
  8.8 15.8 %copy-start.7 = (bf16[256,64]{0,1:T(8,128)(2,1)S(1)}, bf16[256,64]{0,1:T(8,128)(2,1)}, u32[]{:S(2)}) copy-start(bf16[256,64]{0,1:T(8,128)(2,1)} %param.18) | copy-start | bytes 98308
  8.8 3.3 %collective-permute-start.1 = (bf16[11,16,128]{2,1,0:T(8,128)(2,1)S(1)}, bf16[11,16,128]{2,1,0:T(8,128)(2,1)S(1)}, u32[]{:S(2)}, u32[]{:S(2)}) collective-permute-start(bf16[11,16,128]{2,1,0:T(8,128)(2,1)S(1)} %get-tuple-element.35), channel_id=1, source_target_pairs={{0,2},{2,4},{4,6},{6,8},{8,10},{10,12},{12,14},{1,3},{3,5},{5,7},{... | collective-permute-start | bytes 135176 | tf_op jit(solution)/shard_map/ppermute | solution.py:683
  10.7 5.0 %collective-permute-start.2 = (bf16[11,16,128]{2,1,0:T(8,128)(2,1)S(1)}, bf16[11,16,128]{2,1,0:T(8,128)(2,1)S(1)}, u32[]{:S(2)}, u32[]{:S(2)}) collective-permute-start(bf16[11,16,128]{2,1,0:T(8,128)(2,1)S(1)} %get-tuple-element.36), channel_id=1, source_target_pairs={{2,0},{4,2},{6,4},{8,6},{10,8},{12,10},{14,12},{3,1},{5,3},{7,5},{... | collective-permute-start | bytes 135176 | tf_op jit(solution)/shard_map/ppermute | solution.py:684
  16.5 8.0 %collective-permute-start.3 = (bf16[14,16,128]{2,1,0:T(8,128)(2,1)S(1)}, bf16[14,16,128]{2,1,0:T(8,128)(2,1)S(1)}, u32[]{:S(2)}, u32[]{:S(2)}) collective-permute-start(bf16[14,16,128]{2,1,0:T(8,128)(2,1)S(1)} %get-tuple-element.40), channel_id=1, source_target_pairs={{0,16},{16,32},{32,48},{48,64},{64,80},{80,96},{96,112},{112,128},... | collective-permute-start | bytes 172040 | tf_op jit(solution)/shard_map/ppermute | solution.py:683
  19.6 4.9 %collective-permute-start.4 = (bf16[14,16,128]{2,1,0:T(8,128)(2,1)S(1)}, bf16[14,16,128]{2,1,0:T(8,128)(2,1)S(1)}, u32[]{:S(2)}, u32[]{:S(2)}) collective-permute-start(bf16[14,16,128]{2,1,0:T(8,128)(2,1)S(1)} %get-tuple-element.41), channel_id=1, source_target_pairs={{16,0},{32,16},{48,32},{64,48},{80,64},{96,80},{112,96},{128,112},... | collective-permute-start | bytes 172040 | tf_op jit(solution)/shard_map/ppermute | solution.py:684
  24.5 22.4 %copy-start.8 = (bf16[64,64]{1,0:T(8,128)(2,1)S(1)}, bf16[64,64]{1,0:T(8,128)(2,1)}, u32[]{:S(2)}) copy-start(bf16[64,64]{1,0:T(8,128)(2,1)} %param.17) | copy-start | bytes 24580
  24.5 22.5 %copy-start.9 = (f32[64]{0:T(128)S(1)}, f32[64]{0:T(128)}, u32[]{:S(2)}) copy-start(f32[64]{0:T(128)} %param.19) | copy-start | bytes 772
  24.6 22.5 %copy-start.10 = (f32[64]{0:T(128)S(1)}, f32[64]{0:T(128)}, u32[]{:S(2)}) copy-start(f32[64]{0:T(128)} %param.20) | copy-start | bytes 772
  24.6 22.7 %copy-start.6 = (s32[1,3]{1,0:T(1,128)S(1)}, s32[1,3]{1,0:T(1,128)}, u32[]{:S(2)}) copy-start(s32[1,3]{1,0:T(1,128)} %info.19) | copy-start | bytes 40
  28.4 31.4 %all-to-all-start = ((f32[256,1,128]{2,1,0:T(1,128)}), f32[256,1,128]{2,1,0:T(1,128)S(1)}, u32[]{:S(2)}, u32[]{:S(2)}) async-start(f32[256,1,128]{2,1,0:T(1,128)} %bitcast.7), calls=%async_computation | async-start | bytes 262144 | tf_op jit(solution)/shard_map/all_to_all | solution.py:677
  47.3 12.5 %copy-start.2 = (bf16[1,16,16,16,64]{4,3,2,1,0:T(8,128)(2,1)S(1)}, bf16[1,16,16,16,64]{4,3,2,1,0:T(8,128)(2,1)}, u32[]{:S(2)}) copy-start(bf16[1,16,16,16,64]{4,3,2,1,0:T(8,128)(2,1)} %param.12) | copy-start | bytes 1572868
  68.4 3.0 %collective-permute-start.5 = (f32[2048,128]{1,0:T(8,128)S(1)}, f32[2048,128]{1,0:T(8,128)S(1)}, u32[]{:S(2)}, u32[]{:S(2)}) collective-permute-start(f32[2048,128]{1,0:T(8,128)S(1)} %get-tuple-element.49), channel_id=1, source_target_pairs={{0,1},{1,0},{2,3},{3,2},{4,5},{5,4},{6,7},{7,6},{8,9},{9,8},{10,11... | collective-permute-start | bytes 3145736 | tf_op jit(solution)/shard_map/ppermute | solution.py:780
  118.6 4.3 %collective-permute-start.6 = (bf16[128,8,128]{2,1,0:T(8,128)(2,1)S(1)}, bf16[128,8,128]{2,1,0:T(8,128)(2,1)S(1)}, u32[]{:S(2)}, u32[]{:S(2)}) collective-permute-start(bf16[128,8,128]{2,1,0:T(8,128)(2,1)S(1)} %all_to_all.16.near), channel_id=1, source_target_pairs={{0,1},{1,0},{2,3},{3,2},{4,5},{5,4},{6,7},{7,6},{8,9},{9,8},{10,11... | collective-permute-start | bytes 786440 | tf_op jit(solution)/shard_map/ppermute | solution.py:789

commit v6 on v4

--- a/solution.py
+++ b/solution.py
@@ -446,12 +446,15 @@
         stats[128 * u : 128 * u + 128] = shift[u].T + row
 
 
-def turn(info, scene, ends, turned):
+def turn(info, scene, ends, turned_out, turned, sent):
     for oz in range(3):
         for xp in range(18):
             for dk in range(2):
                 tile = scene[oz, xp - 1, dk : dk + 8] if 1 <= xp <= 16 else ends[xp // 17, oz, dk : dk + 8]
                 turned[oz, 128 * dk : 128 * dk + 128, 128 * xp : 128 * xp + 128] = tile.reshape(128, 128).T
+        pltpu.make_async_copy(turned.at[oz], turned_out.at[oz], sent.at[oz]).start()
+    for oz in range(3):
+        pltpu.make_async_copy(turned.at[oz], turned_out.at[oz], sent.at[oz]).wait()
 
 
 def pair_sum(row):
@@ -481,16 +484,19 @@
 
     def kernel(
         info, gathered, target, gain, bias, weight, weight_t, patch, stats, act_in, turned_in,
-        predicted, payload, other, cotangent, act, turned, fetched, sent
+        payload, other, predicted_out, cotangent, act, turned, predicted, fetched, sent, shown_sent
     ):
         def chunk(n):
-            rows = pl.ds(256 * n, 256)
+            rows = (pl.ds(0, 512), pl.ds(512, 1536))[n]
             return pltpu.make_async_copy(act_in.at[rows], act.at[rows], fetched.at[n])
 
-        whole = pltpu.make_async_copy(turned_in, turned, fetched.at[8])
-        for n in range(8):
+        def show(n):
+            part = (pl.ds(0, 4), pl.ds(4, 12))[n]
+            return pltpu.make_async_copy(predicted.at[part], predicted_out.at[part], shown_sent.at[n])
+
+        whole = pltpu.make_async_copy(turned_in, turned, fetched.at[2])
+        for n in range(2):
             chunk(n).start()
-        whole.start()
         kz = lax.axis_index("cz")
         _, _, mean, rstd = moments(gathered, count)
         gains = jnp.zeros((1, 128), F32)
@@ -500,7 +506,12 @@
         cells = [[None] * 4, [None] * 4]
         for x in range(0, 16, 2):
             rows = slice(x * 128, x * 128 + 256)
-            chunk(x // 2).wait()
+            if x == 0:
+                chunk(0).wait()
+                whole.start()
+            if x == 4:
+                show(0).start()
+                chunk(1).wait()
             normalized = (act[rows] - mean) * rstd
             shifted = normalized * gain[...] + bias[...]
             sigma = jax.nn.sigmoid(shifted)
@@ -546,6 +557,7 @@
         coarse = lax.dot_general(patch[...], split, (((0,), (0,)), ((), ())), preferred_element_type=F32)
         for t in range(27):
             store(t, 7, coarse[64 * t : 64 * t + 64])
+        show(1).start()
         whole.wait()
         for ox in range(3):
             windows = turned[:, :, 128 * ox : 128 * ox + 2048].reshape(768, 2048)
@@ -571,6 +583,8 @@
             payload.at[slot][pl.ds(15, 128, stride=16), :] = stats[128 * half : 128 * half + 128]
         copy = pltpu.make_async_copy(payload.at[1], other, sent)
         copy.start()
+        for n in range(2):
+            show(n).wait()
         copy.wait()
 
     return kernel
@@ -690,7 +704,7 @@
     lat = latents[0]
     lat_pairs = lat.reshape(16, 8, 2, 16, 64)
 
-    mz, pooled = call(z_message, [message(Z_TILES), like((16, 64), BF)], [in_hbm(info), lat])
+    mz, pooled = call(z_message, [message(Z_TILES), like((16, 64), BF)], [info, lat])
     rz = lax.ppermute(mz, "cz", [(0, 1), (1, 0)])
     out = message(Y_TILES)
     down, up = call(
@@ -729,22 +743,30 @@
         far_args=1,
     )
     first = exchange(stats)
-    (turned,) = call(turn, [pltpu.HBM((3, 256, 18 * 128), BF)], [info, scene, ends])
+    (turned,) = call(
+        turn,
+        [pltpu.HBM((3, 256, 18 * 128), BF)],
+        [info, scene, ends],
+        [pltpu.VMEM((3, 256, 18 * 128), BF), pltpu.SemaphoreType.DMA((3,))],
+        far_outs=1,
+    )
     gain, bias = twice(norm_gain), twice(norm_bias)
     weights = [diagonal(out_weight), diagonal(out_weight.T)]
-    predicted, payload, other = call(
+    payload, other, predicted = call(
         backward(voxels),
-        [like((16, 8, 2, 16, 64), BF), like((2, 2048, 128), F32), like((2048, 128), F32)],
+        [like((2, 2048, 128), F32), like((2048, 128), F32), pltpu.HBM((16, 8, 2, 16, 64), BF)],
         [info, first, target.reshape(16, 8, 2, 16, 64), gain, bias] + weights + [patch, stats, in_hbm(act), in_hbm(turned)],
         [
             pltpu.VMEM((2048, 256), BF),
             pltpu.VMEM((2048, 128), F32),
             pltpu.VMEM((3, 256, 18 * 128), BF),
-            pltpu.SemaphoreType.DMA((9,)),
+            pltpu.VMEM((16, 8, 2, 16, 64), BF),
+            pltpu.SemaphoreType.DMA((3,)),
             pltpu.SemaphoreType.DMA,
+            pltpu.SemaphoreType.DMA((2,)),
         ],
         far_args=2,
-        far_outs=1,
+        far_outs=2,
     )
     swap = [(0, 1), (1, 0)]
     chips = devices // 2

time: 127 us -> 123 us (0.969)
  Pallas kernels: 27.6 us -> 24.7 us
    pallas_call x10, Pallas kernels: 27.6 us -> 24.7 us  [call(): pl.pallas_call(kernel, grid=(1,), out_shape=outs, in_specs=[pl.BlockSpec(...]
    unnamed x25 -> x23, local copies, waits for them, and re-layouts: 3.23 us -> 2.01 us
where the time goes in v6:
time: 123 us
  blocking collectives  44.1 us (36%)
  starting transfers between devices  33.5 us (27%)
  Pallas kernels  24.7 us (20%)
  waiting for transfers between devices  17.2 us (14%)
  local copies, waits for them, and re-layouts  2.01 us (2%)
  between operations  1.5 us (1%)
    all_to_all x1, blocking collectives, shards(): pieces = lax.all_to_all(pieces, CHIPS, 0, 0, tiled=True)  25.1 us
    pallas_call x10, Pallas kernels, call(): pl.pallas_call(kernel, grid=(1,), out_shape=outs, in_specs=[pl.BlockSpec(...  24.7 us
    all_to_all x1, blocking collectives, shards(): near = lax.all_to_all(copies, CHIPS, 0, 0, tiled=True)  19 us
    all_to_all x1, starting transfers between devices, exchange(): lax.all_to_all(rows.reshape(rows.shape[0], 1, 128), ('cz',) + CHIPS, 0, 0...  18.6 us
    all_to_all x1, waiting for transfers between devices, exchange(): lax.all_to_all(rows.reshape(rows.shape[0], 1, 128), ('cz',) + CHIPS, 0, 0...  9.81 us
    ppermute x2, starting transfers between devices, neighbours(): before = lax.ppermute(up, axis, [(i, i + 1) for i in range(ends)])  5.06 us
    ppermute x2, waiting for transfers between devices, neighbours(): after = lax.ppermute(down, axis, [(i + 1, i) for i in range(ends)])  3.67 us
    ppermute x1, starting transfers between devices, shards(): rz = lax.ppermute(mz, 'cz', [(0, 1), (1, 0)])  3.33 us
  transfers between devices with their start and end apart: 8, of which 6 were waited for; matrix products, arithmetic and copies ran while one was open for 0% of the time, Pallas kernels for 5%

profile of v6, /device:TPU:1, one launch (start us, length us, event | category | flops | bytes accessed | tf_op | source)
XLA Modules:
  0.0 123.1 jit_solution(13171872762312736184)
XLA Ops:
  0.6 1.2 copy-done
  1.9 0.7 copy-done.5
  2.5 1.4 %shard_map.170 = (bf16[10,16,128]{2,1,0:T(8,128)(2,1)S(1)}, bf16[16,64]{1,0:T(8,128)(2,1)S(1)}) custom-call(s32[1,3]{1,0:T(1,128)S(1)} %copy-done.5, bf16[16,16,16,64]{3,2,1,0:T(8,128)(2,1)S(1)} %bitcast.21), custom_call_target="tpu_custom_call" | custom-call | tf_op jit(solution)/shard_map/pallas_call | solution.py:36
  3.9 3.3 %collective-permute-start = (bf16[10,16,128]{2,1,0:T(8,128)(2,1)S(1)}, bf16[10,16,128]{2,1,0:T(8,128)(2,1)S(1)}, u32[]{:S(2)}, u32[]{:S(2)}) collective-permute-start(bf16[10,16,128]{2,1,0:T(8,128)(2,1)S(1)} %get-tuple-element.33), channel_id=1, source_target_pairs={{0,1},{1,0},{2,3},{3,2},{4,5},{5,4},{6,7},{7,6},{8,9},{9,8},{10,11... | collective-permute-start | bytes 122888 | tf_op jit(solution)/shard_map/ppermute | solution.py:708
  7.9 0.2 collective-permute-done.rz_in
  8.1 0.7 shard_map.171
  8.8 1.9 %collective-permute-start.1 = (bf16[11,16,128]{2,1,0:T(8,128)(2,1)S(1)}, bf16[11,16,128]{2,1,0:T(8,128)(2,1)S(1)}, u32[]{:S(2)}, u32[]{:S(2)}) collective-permute-start(bf16[11,16,128]{2,1,0:T(8,128)(2,1)S(1)} %get-tuple-element.35), channel_id=1, source_target_pairs={{0,2},{2,4},{4,6},{6,8},{8,10},{10,12},{12,14},{1,3},{3,5},{5,7},{... | collective-permute-start | bytes 135176 | tf_op jit(solution)/shard_map/ppermute | solution.py:678
  10.7 1.3 %collective-permute-start.2 = (bf16[11,16,128]{2,1,0:T(8,128)(2,1)S(1)}, bf16[11,16,128]{2,1,0:T(8,128)(2,1)S(1)}, u32[]{:S(2)}, u32[]{:S(2)}) collective-permute-start(bf16[11,16,128]{2,1,0:T(8,128)(2,1)S(1)} %get-tuple-element.36), channel_id=1, source_target_pairs={{2,0},{4,2},{6,4},{8,6},{10,8},{12,10},{14,12},{3,1},{5,3},{7,5},{... | collective-permute-start | bytes 135176 | tf_op jit(solution)/shard_map/ppermute | solution.py:679
  12.1 3.6 %collective-permute-done.2.ryp_in = bf16[11,16,128]{2,1,0:T(8,128)(2,1)S(1)} collective-permute-done((bf16[11,16,128]{2,1,0:T(8,128)(2,1)S(1)}, bf16[11,16,128]{2,1,0:T(8,128)(2,1)S(1)}, u32[]{:S(2)}, u32[]{:S(2)}) %collective-permute-start.2) | collective-permute-done | bytes 45088 | tf_op jit(solution)/shard_map/ppermute | solution.py:679
  15.7 0.8 shard_map.173
  16.5 3.1 %collective-permute-start.3 = (bf16[14,16,128]{2,1,0:T(8,128)(2,1)S(1)}, bf16[14,16,128]{2,1,0:T(8,128)(2,1)S(1)}, u32[]{:S(2)}, u32[]{:S(2)}) collective-permute-start(bf16[14,16,128]{2,1,0:T(8,128)(2,1)S(1)} %get-tuple-element.40), channel_id=1, source_target_pairs={{0,16},{16,32},{32,48},{48,64},{64,80},{80,96},{96,112},{112,128},... | collective-permute-start | bytes 172040 | tf_op jit(solution)/shard_map/ppermute | solution.py:678
  19.6 1.3 %collective-permute-start.4 = (bf16[14,16,128]{2,1,0:T(8,128)(2,1)S(1)}, bf16[14,16,128]{2,1,0:T(8,128)(2,1)S(1)}, u32[]{:S(2)}, u32[]{:S(2)}) collective-permute-start(bf16[14,16,128]{2,1,0:T(8,128)(2,1)S(1)} %get-tuple-element.41), channel_id=1, source_target_pairs={{16,0},{32,16},{48,32},{64,48},{80,64},{96,80},{112,96},{128,112},... | collective-permute-start | bytes 172040 | tf_op jit(solution)/shard_map/ppermute | solution.py:679
  20.9 3.5 %shard_map.172 = (f32[1792,128]{1,0:T(8,128)S(1)}, bf16[3,16,9,16,128]{4,3,2,1,0:T(8,128)(2,1)S(1)}, f32[3,9,128]{2,1,0:T(8,128)S(1)}, bf16[2304,128]{1,0:T(8,128)(2,1)S(1)}) custom-call(s32[1,3]{1,0:T(1,128)S(1)} %copy-done.5, bf16[16,8,2,16,64]{4,3,2,1,0:T(8,128)(2,1)S(1)} %bitcast.26, bf16[10,16,128]{2,1,0:T(8,128)(2,1)S(1)} %collective-permute-done.rz_in, ...), custom_call_target="tpu_custom_call" | custom-call | tf_op jit(solution)/shard_map/pallas_call | solution.py:36
  24.5 0.1 collective-permute-done.4.rxp_in
  24.5 0.0 copy-start.9
  24.6 3.2 %shard_map.174 = (f32[2048,128]{1,0:T(8,128)}, bf16[2,3,9,16,128]{4,3,2,1,0:T(8,128)(2,1)S(1)}, bf16[16,1728]{1,0:T(8,128)(2,1)S(1)}, f32[256,128]{1,0:T(8,128)}) custom-call(s32[1,3]{1,0:T(1,128)S(1)} %copy-done.5, bf16[3,16,9,16,128]{4,3,2,1,0:T(8,128)(2,1)S(1)} %get-tuple-element.37.near_low.near_high.scene, ...), custom_call_target="tpu_custom_call" | custom-call | tf_op jit(solution)/shard_map/pallas_call | solution.py:36
  27.8 18.6 %all-to-all-start = ((f32[256,1,128]{2,1,0:T(1,128)}), f32[256,1,128]{2,1,0:T(1,128)S(1)}, u32[]{:S(2)}, u32[]{:S(2)}) async-start(f32[256,1,128]{2,1,0:T(1,128)} %bitcast.7), calls=%async_computation | async-start | bytes 262144 | tf_op jit(solution)/shard_map/all_to_all | solution.py:672
  46.4 0.1 copy.21
  46.5 0.1 maximum_bitcast_fusion
  46.6 0.1 fusion.4
  46.7 2.7 %shard_map.175.turned_in = bf16[3,256,2304]{2,1,0:T(8,128)(2,1)} custom-call(s32[1,3]{1,0:T(1,128)S(1)} %copy-done.6, bf16[3,16,9,16,128]{4,3,2,1,0:T(8,128)(2,1)S(1)} %get-tuple-element.37.near_low.near_high.scene, bf16[2,3,9,16,128]{4,3,2,1,0:T(8,128)(2,1)S(1)} %get-tuple-element.46.ends), custom_call_target="tpu_custom_call" | custom-call | tf_op jit(solution)/shard_map/pallas_call | solution.py:36
  49.4 9.8 %all-to-all-done = f32[256,1,128]{2,1,0:T(1,128)S(1)} async-done(((f32[256,1,128]{2,1,0:T(1,128)}), f32[256,1,128]{2,1,0:T(1,128)S(1)}, u32[]{:S(2)}, u32[]{:S(2)}) %all-to-all-start) | async-done | bytes 131104 | tf_op jit(solution)/shard_map/all_to_all | solution.py:672
  59.2 7.3 %shard_map.176 = (f32[2,2048,128]{2,1,0:T(8,128)S(1)}, f32[2048,128]{1,0:T(8,128)S(1)}, bf16[16,8,2,16,64]{4,3,2,1,0:T(8,128)(2,1)}) custom-call(s32[1,3]{1,0:T(1,128)S(1)} %copy-done.6, f32[256,128]{1,0:T(8,128)S(1)} %bitcast.27, bf16[16,8,2,16,64]{4,3,2,1,0:T(8,128)(2,1)S(1)} %bitcast.30, f32[1,128]{1,0:T(1,128)S(1)} %get-tuple-element.62.gain, ...), custom_call_target="tpu_custom_call" | custom-call | tf_op jit(solution)/shard_map/pallas_call | solution.py:36
  66.5 0.7 collective-permute-start.5
  67.3 2.3 %collective-permute-done.5.other = f32[2048,128]{1,0:T(8,128)S(1)} collective-permute-done((f32[2048,128]{1,0:T(8,128)S(1)}, f32[2048,128]{1,0:T(8,128)S(1)}, u32[]{:S(2)}, u32[]{:S(2)}) %collective-permute-start.5) | collective-permute-done | bytes 1048608 | tf_op jit(solution)/shard_map/ppermute | solution.py:773
  69.6 1.4 %shard_map.177 = bf16[128,16,128]{2,1,0:T(8,128)(2,1)S(1)} custom-call(s32[1,3]{1,0:T(1,128)S(1)} %copy-done.6, f32[2,2048,128]{2,1,0:T(8,128)S(1)} %get-tuple-element.48.mine, f32[2048,128]{1,0:T(8,128)S(1)} %collective-permute-done.5.other, f32[256,128]{1,0:T(8,128)S(1)} %bitcast.28, f32[1,128]{1,0:T(1,128)S(1)} %get-tuple-element.62.gain), custom_call_target="tpu_custom_call" | custom-call | tf_op jit(solution)/shard_map/pallas_call | solution.py:36
  71.0 25.1 %all_to_all.15.pieces = bf16[128,16,128]{2,1,0:T(8,128)(2,1)S(1)} all-to-all(bf16[128,16,128]{2,1,0:T(8,128)(2,1)S(1)} %shard_map.177), channel_id=1, replica_groups=mesh['bx'=16,'by'=8,'cz'=2] {'bx','by'}, dimensions={0} | all-to-all | bytes 1048576 | tf_op jit(solution)/shard_map/all_to_all | solution.py:775
  96.0 1.7 %shard_map.178 = (bf16[128,8,128]{2,1,0:T(8,128)(2,1)S(1)}, f32[64,256]{1,0:T(8,128)}, f32[1,64]{1,0:T(1,128)}, f32[1,64]{1,0:T(1,128)}) custom-call(s32[1,3]{1,0:T(1,128)S(1)} %copy-done.6, bf16[128,16,128]{2,1,0:T(8,128)(2,1)S(1)} %all_to_all.15.pieces, f32[256,128]{1,0:T(8,128)S(1)} %bitcast.29, f32[1,128]{1,0:T(1,128)S(1)} %get-tuple-element.62.gain, ...), custom_call_target="tpu_custom_call" | custom-call | tf_op jit(solution)/shard_map/pallas_call | solution.py:36
  97.7 19.0 %all_to_all.16.near = bf16[128,8,128]{2,1,0:T(8,128)(2,1)S(1)} all-to-all(bf16[128,8,128]{2,1,0:T(8,128)(2,1)S(1)} %get-tuple-element.50), channel_id=1, replica_groups=mesh['bx'=16,'by'=8,'cz'=2] {'bx','by'}, dimensions={0} | all-to-all | bytes 524288 | tf_op jit(solution)/shard_map/all_to_all | solution.py:781
  116.7 3.2 %collective-permute-start.6 = (bf16[128,8,128]{2,1,0:T(8,128)(2,1)S(1)}, bf16[128,8,128]{2,1,0:T(8,128)(2,1)S(1)}, u32[]{:S(2)}, u32[]{:S(2)}) collective-permute-start(bf16[128,8,128]{2,1,0:T(8,128)(2,1)S(1)} %all_to_all.16.near), channel_id=1, source_target_pairs={{0,1},{1,0},{2,3},{3,2},{4,5},{5,4},{6,7},{7,6},{8,9},{9,8},{10,11... | collective-permute-start | bytes 786440 | tf_op jit(solution)/shard_map/ppermute | solution.py:782
  119.9 1.2 collective-permute-done.6.far
  121.0 2.1 %shard_map.179 = (f32[27,64,64]{2,1,0:T(8,128)}, f32[27,64,64]{2,1,0:T(8,128)}, f32[64,64]{1,0:T(8,128)}, f32[1,1]{1,0:T(1,128)}) custom-call(s32[1,3]{1,0:T(1,128)S(1)} %copy-done.6, bf16[128,8,128]{2,1,0:T(8,128)(2,1)S(1)} %all_to_all.16.near, bf16[128,8,128]{2,1,0:T(8,128)(2,1)S(1)} %collective-permute-done.6.far), custom_call_target="tpu_custom_call" | custom-call | tf_op jit(solution)/shard_map/pallas_call | solution.py:36
  (23 shorter events, 0.1 us)
Async XLA Ops:
  0.6 1.2 copy-start
  1.9 0.7 copy-start.5
  3.9 4.2 %collective-permute-start = (bf16[10,16,128]{2,1,0:T(8,128)(2,1)S(1)}, bf16[10,16,128]{2,1,0:T(8,128)(2,1)S(1)}, u32[]{:S(2)}, u32[]{:S(2)}) collective-permute-start(bf16[10,16,128]{2,1,0:T(8,128)(2,1)S(1)} %get-tuple-element.33), channel_id=1, source_target_pairs={{0,1},{1,0},{2,3},{3,2},{4,5},{5,4},{6,7},{7,6},{8,9},{9,8},{10,11... | collective-permute-start | bytes 122888 | tf_op jit(solution)/shard_map/ppermute | solution.py:708
  8.1 12.8 %copy-start.3 = (bf16[27,64,64]{2,1,0:T(8,128)(2,1)S(1)}, bf16[27,64,64]{2,1,0:T(8,128)(2,1)}, u32[]{:S(2)}) copy-start(bf16[27,64,64]{2,1,0:T(8,128)(2,1)} %taps.1) | copy-start | bytes 663556
  8.8 15.8 %copy-start.1 = (bf16[16,224,160]{2,1,0:T(8,128)(2,1)S(1)}, bf16[16,224,160]{2,1,0:T(8,128)(2,1)}, u32[]{:S(2)}) copy-start(bf16[16,224,160]{2,1,0:T(8,128)(2,1)} %constant.6.clone.tables) | copy-start | bytes 3440644
  8.8 15.8 %copy-start.4 = (bf16[27,64,64]{2,1,0:T(8,128)(2,1)S(1)}, bf16[27,64,64]{2,1,0:T(8,128)(2,1)}, u32[]{:S(2)}) copy-start(bf16[27,64,64]{2,1,0:T(8,128)(2,1)} %param.16) | copy-start | bytes 663556
  8.8 15.8 %copy-start.7 = (bf16[256,64]{0,1:T(8,128)(2,1)S(1)}, bf16[256,64]{0,1:T(8,128)(2,1)}, u32[]{:S(2)}) copy-start(bf16[256,64]{0,1:T(8,128)(2,1)} %param.18) | copy-start | bytes 98308
  8.8 3.3 %collective-permute-start.1 = (bf16[11,16,128]{2,1,0:T(8,128)(2,1)S(1)}, bf16[11,16,128]{2,1,0:T(8,128)(2,1)S(1)}, u32[]{:S(2)}, u32[]{:S(2)}) collective-permute-start(bf16[11,16,128]{2,1,0:T(8,128)(2,1)S(1)} %get-tuple-element.35), channel_id=1, source_target_pairs={{0,2},{2,4},{4,6},{6,8},{8,10},{10,12},{12,14},{1,3},{3,5},{5,7},{... | collective-permute-start | bytes 135176 | tf_op jit(solution)/shard_map/ppermute | solution.py:678
  10.7 5.0 %collective-permute-start.2 = (bf16[11,16,128]{2,1,0:T(8,128)(2,1)S(1)}, bf16[11,16,128]{2,1,0:T(8,128)(2,1)S(1)}, u32[]{:S(2)}, u32[]{:S(2)}) collective-permute-start(bf16[11,16,128]{2,1,0:T(8,128)(2,1)S(1)} %get-tuple-element.36), channel_id=1, source_target_pairs={{2,0},{4,2},{6,4},{8,6},{10,8},{12,10},{14,12},{3,1},{5,3},{7,5},{... | collective-permute-start | bytes 135176 | tf_op jit(solution)/shard_map/ppermute | solution.py:679
  16.5 8.0 %collective-permute-start.3 = (bf16[14,16,128]{2,1,0:T(8,128)(2,1)S(1)}, bf16[14,16,128]{2,1,0:T(8,128)(2,1)S(1)}, u32[]{:S(2)}, u32[]{:S(2)}) collective-permute-start(bf16[14,16,128]{2,1,0:T(8,128)(2,1)S(1)} %get-tuple-element.40), channel_id=1, source_target_pairs={{0,16},{16,32},{32,48},{48,64},{64,80},{80,96},{96,112},{112,128},... | collective-permute-start | bytes 172040 | tf_op jit(solution)/shard_map/ppermute | solution.py:678
  19.6 4.9 %collective-permute-start.4 = (bf16[14,16,128]{2,1,0:T(8,128)(2,1)S(1)}, bf16[14,16,128]{2,1,0:T(8,128)(2,1)S(1)}, u32[]{:S(2)}, u32[]{:S(2)}) collective-permute-start(bf16[14,16,128]{2,1,0:T(8,128)(2,1)S(1)} %get-tuple-element.41), channel_id=1, source_target_pairs={{16,0},{32,16},{48,32},{64,48},{80,64},{96,80},{112,96},{128,112},... | collective-permute-start | bytes 172040 | tf_op jit(solution)/shard_map/ppermute | solution.py:679
  24.5 21.9 %copy-start.8 = (bf16[64,64]{1,0:T(8,128)(2,1)S(1)}, bf16[64,64]{1,0:T(8,128)(2,1)}, u32[]{:S(2)}) copy-start(bf16[64,64]{1,0:T(8,128)(2,1)} %param.17) | copy-start | bytes 24580
  24.5 22.0 %copy-start.9 = (f32[64]{0:T(128)S(1)}, f32[64]{0:T(128)}, u32[]{:S(2)}) copy-start(f32[64]{0:T(128)} %param.19) | copy-start | bytes 772
  24.6 21.9 %copy-start.10 = (f32[64]{0:T(128)S(1)}, f32[64]{0:T(128)}, u32[]{:S(2)}) copy-start(f32[64]{0:T(128)} %param.20) | copy-start | bytes 772
  24.6 22.1 %copy-start.6 = (s32[1,3]{1,0:T(1,128)S(1)}, s32[1,3]{1,0:T(1,128)}, u32[]{:S(2)}) copy-start(s32[1,3]{1,0:T(1,128)} %info.19) | copy-start | bytes 40
  27.8 31.4 %all-to-all-start = ((f32[256,1,128]{2,1,0:T(1,128)}), f32[256,1,128]{2,1,0:T(1,128)S(1)}, u32[]{:S(2)}, u32[]{:S(2)}) async-start(f32[256,1,128]{2,1,0:T(1,128)} %bitcast.7), calls=%async_computation | async-start | bytes 262144 | tf_op jit(solution)/shard_map/all_to_all | solution.py:672
  46.7 12.5 %copy-start.2 = (bf16[1,16,16,16,64]{4,3,2,1,0:T(8,128)(2,1)S(1)}, bf16[1,16,16,16,64]{4,3,2,1,0:T(8,128)(2,1)}, u32[]{:S(2)}) copy-start(bf16[1,16,16,16,64]{4,3,2,1,0:T(8,128)(2,1)} %param.12) | copy-start | bytes 1572868
  66.5 3.0 %collective-permute-start.5 = (f32[2048,128]{1,0:T(8,128)S(1)}, f32[2048,128]{1,0:T(8,128)S(1)}, u32[]{:S(2)}, u32[]{:S(2)}) collective-permute-start(f32[2048,128]{1,0:T(8,128)S(1)} %get-tuple-element.49), channel_id=1, source_target_pairs={{0,1},{1,0},{2,3},{3,2},{4,5},{5,4},{6,7},{7,6},{8,9},{9,8},{10,11... | collective-permute-start | bytes 3145736 | tf_op jit(solution)/shard_map/ppermute | solution.py:773
  116.7 4.3 %collective-permute-start.6 = (bf16[128,8,128]{2,1,0:T(8,128)(2,1)S(1)}, bf16[128,8,128]{2,1,0:T(8,128)(2,1)S(1)}, u32[]{:S(2)}, u32[]{:S(2)}) collective-permute-start(bf16[128,8,128]{2,1,0:T(8,128)(2,1)S(1)} %all_to_all.16.near), channel_id=1, source_target_pairs={{0,1},{1,0},{2,3},{3,2},{4,5},{5,4},{6,7},{7,6},{8,9},{9,8},{10,11... | collective-permute-start | bytes 786440 | tf_op jit(solution)/shard_map/ppermute | solution.py:782

commit v7 on v6

--- a/solution.py
+++ b/solution.py
@@ -581,7 +581,7 @@
             payload.at[half][pl.ds(14, 128, stride=16), :] = wide
             slot = jnp.where(kz == half, 0, 1)
             payload.at[slot][pl.ds(15, 128, stride=16), :] = stats[128 * half : 128 * half + 128]
-        copy = pltpu.make_async_copy(payload.at[1], other, sent)
+        copy = pltpu.make_async_copy(payload.at[1, pl.ds(0, 2048)], other, sent)
         copy.start()
         for n in range(2):
             show(n).wait()
@@ -601,7 +601,7 @@
 
     def kernel(info, mine, other, gathered, gain, out):
         _, _, _, rstd = moments(gathered, total_count)
-        total = (mine[0] + other[...]).reshape(-1, 16, 128)
+        total = (mine[0, 0:2048] + other[...]).reshape(-1, 16, 128)
         m1, m2 = slopes(total[0, 14:15], gain[...], count)
         row = lax.broadcasted_iota(jnp.int32, total.shape, 1)
         lane = lax.broadcasted_iota(jnp.int32, total.shape, 2)
@@ -754,7 +754,7 @@
     weights = [diagonal(out_weight), diagonal(out_weight.T)]
     payload, other, predicted = call(
         backward(voxels),
-        [like((2, 2048, 128), F32), like((2048, 128), F32), pltpu.HBM((16, 8, 2, 16, 64), BF)],
+        [like((2, 2064, 128), F32), like((2048, 128), F32), pltpu.HBM((16, 8, 2, 16, 64), BF)],
         [info, first, target.reshape(16, 8, 2, 16, 64), gain, bias] + weights + [patch, stats, in_hbm(act), in_hbm(turned)],
         [
             pltpu.VMEM((2048, 256), BF),
@@ -784,7 +784,7 @@
         functools.partial(spread, 1.0 / (voxels * 64)),
         [like((27, 64, 64), F32), like((27, 64, 64), F32), like((64, 64), F32), like((1, 1), F32)],
         [info, near, far],
-        [pltpu.VMEM((2048, 128), F32)],
+        [pltpu.VMEM((2056, 128), F32)],
     )
     return (
         predicted.reshape(latents.shape),

time: 123 us -> 123 us (level)
  no operation moved by 1% of the time
where the time goes in v7:
time: 123 us
  blocking collectives  44.1 us (36%)
  starting transfers between devices  33.5 us (27%)
  Pallas kernels  24.7 us (20%)
  waiting for transfers between devices  17.2 us (14%)
  local copies, waits for them, and re-layouts  2.01 us (2%)
  between operations  1.5 us (1%)
    all_to_all x1, blocking collectives, shards(): pieces = lax.all_to_all(pieces, CHIPS, 0, 0, tiled=True)  25.1 us
    pallas_call x10, Pallas kernels, call(): pl.pallas_call(kernel, grid=(1,), out_shape=outs, in_specs=[pl.BlockSpec(...  24.7 us
    all_to_all x1, blocking collectives, shards(): near = lax.all_to_all(copies, CHIPS, 0, 0, tiled=True)  19 us
    all_to_all x1, starting transfers between devices, exchange(): lax.all_to_all(rows.reshape(rows.shape[0], 1, 128), ('cz',) + CHIPS, 0, 0...  18.6 us
    all_to_all x1, waiting for transfers between devices, exchange(): lax.all_to_all(rows.reshape(rows.shape[0], 1, 128), ('cz',) + CHIPS, 0, 0...  9.81 us
    ppermute x2, starting transfers between devices, neighbours(): before = lax.ppermute(up, axis, [(i, i + 1) for i in range(ends)])  5.06 us
    ppermute x2, waiting for transfers between devices, neighbours(): after = lax.ppermute(down, axis, [(i + 1, i) for i in range(ends)])  3.67 us
    ppermute x1, starting transfers between devices, shards(): rz = lax.ppermute(mz, 'cz', [(0, 1), (1, 0)])  3.33 us
  transfers between devices with their start and end apart: 8, of which 6 were waited for; matrix products, arithmetic and copies ran while one was open for 0% of the time, Pallas kernels for 5%

profile of v7, /device:TPU:1, one launch (start us, length us, event | category | flops | bytes accessed | tf_op | source)
XLA Modules:
  0.0 123.1 jit_solution(11273003630865742293)
XLA Ops:
  0.6 1.2 copy-done
  1.9 0.7 copy-done.5
  2.5 1.4 %shard_map.170 = (bf16[10,16,128]{2,1,0:T(8,128)(2,1)S(1)}, bf16[16,64]{1,0:T(8,128)(2,1)S(1)}) custom-call(s32[1,3]{1,0:T(1,128)S(1)} %copy-done.5, bf16[16,16,16,64]{3,2,1,0:T(8,128)(2,1)S(1)} %bitcast.21), custom_call_target="tpu_custom_call" | custom-call | tf_op jit(solution)/shard_map/pallas_call | solution.py:36
  3.9 3.3 %collective-permute-start = (bf16[10,16,128]{2,1,0:T(8,128)(2,1)S(1)}, bf16[10,16,128]{2,1,0:T(8,128)(2,1)S(1)}, u32[]{:S(2)}, u32[]{:S(2)}) collective-permute-start(bf16[10,16,128]{2,1,0:T(8,128)(2,1)S(1)} %get-tuple-element.33), channel_id=1, source_target_pairs={{0,1},{1,0},{2,3},{3,2},{4,5},{5,4},{6,7},{7,6},{8,9},{9,8},{10,11... | collective-permute-start | bytes 122888 | tf_op jit(solution)/shard_map/ppermute | solution.py:708
  7.9 0.2 collective-permute-done.rz_in
  8.1 0.7 shard_map.171
  8.8 1.9 %collective-permute-start.1 = (bf16[11,16,128]{2,1,0:T(8,128)(2,1)S(1)}, bf16[11,16,128]{2,1,0:T(8,128)(2,1)S(1)}, u32[]{:S(2)}, u32[]{:S(2)}) collective-permute-start(bf16[11,16,128]{2,1,0:T(8,128)(2,1)S(1)} %get-tuple-element.35), channel_id=1, source_target_pairs={{0,2},{2,4},{4,6},{6,8},{8,10},{10,12},{12,14},{1,3},{3,5},{5,7},{... | collective-permute-start | bytes 135176 | tf_op jit(solution)/shard_map/ppermute | solution.py:678
  10.7 1.3 %collective-permute-start.2 = (bf16[11,16,128]{2,1,0:T(8,128)(2,1)S(1)}, bf16[11,16,128]{2,1,0:T(8,128)(2,1)S(1)}, u32[]{:S(2)}, u32[]{:S(2)}) collective-permute-start(bf16[11,16,128]{2,1,0:T(8,128)(2,1)S(1)} %get-tuple-element.36), channel_id=1, source_target_pairs={{2,0},{4,2},{6,4},{8,6},{10,8},{12,10},{14,12},{3,1},{5,3},{7,5},{... | collective-permute-start | bytes 135176 | tf_op jit(solution)/shard_map/ppermute | solution.py:679
  12.1 3.6 %collective-permute-done.2.ryp_in = bf16[11,16,128]{2,1,0:T(8,128)(2,1)S(1)} collective-permute-done((bf16[11,16,128]{2,1,0:T(8,128)(2,1)S(1)}, bf16[11,16,128]{2,1,0:T(8,128)(2,1)S(1)}, u32[]{:S(2)}, u32[]{:S(2)}) %collective-permute-start.2) | collective-permute-done | bytes 45088 | tf_op jit(solution)/shard_map/ppermute | solution.py:679
  15.7 0.8 shard_map.173
  16.5 3.1 %collective-permute-start.3 = (bf16[14,16,128]{2,1,0:T(8,128)(2,1)S(1)}, bf16[14,16,128]{2,1,0:T(8,128)(2,1)S(1)}, u32[]{:S(2)}, u32[]{:S(2)}) collective-permute-start(bf16[14,16,128]{2,1,0:T(8,128)(2,1)S(1)} %get-tuple-element.40), channel_id=1, source_target_pairs={{0,16},{16,32},{32,48},{48,64},{64,80},{80,96},{96,112},{112,128},... | collective-permute-start | bytes 172040 | tf_op jit(solution)/shard_map/ppermute | solution.py:678
  19.6 1.3 %collective-permute-start.4 = (bf16[14,16,128]{2,1,0:T(8,128)(2,1)S(1)}, bf16[14,16,128]{2,1,0:T(8,128)(2,1)S(1)}, u32[]{:S(2)}, u32[]{:S(2)}) collective-permute-start(bf16[14,16,128]{2,1,0:T(8,128)(2,1)S(1)} %get-tuple-element.41), channel_id=1, source_target_pairs={{16,0},{32,16},{48,32},{64,48},{80,64},{96,80},{112,96},{128,112},... | collective-permute-start | bytes 172040 | tf_op jit(solution)/shard_map/ppermute | solution.py:679
  20.9 3.5 %shard_map.172 = (f32[1792,128]{1,0:T(8,128)S(1)}, bf16[3,16,9,16,128]{4,3,2,1,0:T(8,128)(2,1)S(1)}, f32[3,9,128]{2,1,0:T(8,128)S(1)}, bf16[2304,128]{1,0:T(8,128)(2,1)S(1)}) custom-call(s32[1,3]{1,0:T(1,128)S(1)} %copy-done.5, bf16[16,8,2,16,64]{4,3,2,1,0:T(8,128)(2,1)S(1)} %bitcast.26, bf16[10,16,128]{2,1,0:T(8,128)(2,1)S(1)} %collective-permute-done.rz_in, ...), custom_call_target="tpu_custom_call" | custom-call | tf_op jit(solution)/shard_map/pallas_call | solution.py:36
  24.5 0.1 collective-permute-done.4.rxp_in
  24.5 0.0 copy-start.9
  24.6 3.2 %shard_map.174 = (f32[2048,128]{1,0:T(8,128)}, bf16[2,3,9,16,128]{4,3,2,1,0:T(8,128)(2,1)S(1)}, bf16[16,1728]{1,0:T(8,128)(2,1)S(1)}, f32[256,128]{1,0:T(8,128)}) custom-call(s32[1,3]{1,0:T(1,128)S(1)} %copy-done.5, bf16[3,16,9,16,128]{4,3,2,1,0:T(8,128)(2,1)S(1)} %get-tuple-element.37.near_low.near_high.scene, ...), custom_call_target="tpu_custom_call" | custom-call | tf_op jit(solution)/shard_map/pallas_call | solution.py:36
  27.8 18.6 %all-to-all-start = ((f32[256,1,128]{2,1,0:T(1,128)}), f32[256,1,128]{2,1,0:T(1,128)S(1)}, u32[]{:S(2)}, u32[]{:S(2)}) async-start(f32[256,1,128]{2,1,0:T(1,128)} %bitcast.7), calls=%async_computation | async-start | bytes 262144 | tf_op jit(solution)/shard_map/all_to_all | solution.py:672
  46.4 0.1 copy.21
  46.5 0.1 maximum_bitcast_fusion
  46.6 0.1 fusion.4
  46.7 2.7 %shard_map.175.turned_in = bf16[3,256,2304]{2,1,0:T(8,128)(2,1)} custom-call(s32[1,3]{1,0:T(1,128)S(1)} %copy-done.6, bf16[3,16,9,16,128]{4,3,2,1,0:T(8,128)(2,1)S(1)} %get-tuple-element.37.near_low.near_high.scene, bf16[2,3,9,16,128]{4,3,2,1,0:T(8,128)(2,1)S(1)} %get-tuple-element.46.ends), custom_call_target="tpu_custom_call" | custom-call | tf_op jit(solution)/shard_map/pallas_call | solution.py:36
  49.4 9.8 %all-to-all-done = f32[256,1,128]{2,1,0:T(1,128)S(1)} async-done(((f32[256,1,128]{2,1,0:T(1,128)}), f32[256,1,128]{2,1,0:T(1,128)S(1)}, u32[]{:S(2)}, u32[]{:S(2)}) %all-to-all-start) | async-done | bytes 131104 | tf_op jit(solution)/shard_map/all_to_all | solution.py:672
  59.2 7.3 %shard_map.176 = (f32[2,2064,128]{2,1,0:T(8,128)S(1)}, f32[2048,128]{1,0:T(8,128)S(1)}, bf16[16,8,2,16,64]{4,3,2,1,0:T(8,128)(2,1)}) custom-call(s32[1,3]{1,0:T(1,128)S(1)} %copy-done.6, f32[256,128]{1,0:T(8,128)S(1)} %bitcast.27, bf16[16,8,2,16,64]{4,3,2,1,0:T(8,128)(2,1)S(1)} %bitcast.30, f32[1,128]{1,0:T(1,128)S(1)} %get-tuple-element.62.gain, ...), custom_call_target="tpu_custom_call" | custom-call | tf_op jit(solution)/shard_map/pallas_call | solution.py:36
  66.5 0.7 collective-permute-start.5
  67.3 2.3 %collective-permute-done.5.other = f32[2048,128]{1,0:T(8,128)S(1)} collective-permute-done((f32[2048,128]{1,0:T(8,128)S(1)}, f32[2048,128]{1,0:T(8,128)S(1)}, u32[]{:S(2)}, u32[]{:S(2)}) %collective-permute-start.5) | collective-permute-done | bytes 1048608 | tf_op jit(solution)/shard_map/ppermute | solution.py:773
  69.6 1.4 %shard_map.177 = bf16[128,16,128]{2,1,0:T(8,128)(2,1)S(1)} custom-call(s32[1,3]{1,0:T(1,128)S(1)} %copy-done.6, f32[2,2064,128]{2,1,0:T(8,128)S(1)} %get-tuple-element.48.mine, f32[2048,128]{1,0:T(8,128)S(1)} %collective-permute-done.5.other, f32[256,128]{1,0:T(8,128)S(1)} %bitcast.28, f32[1,128]{1,0:T(1,128)S(1)} %get-tuple-element.62.gain), custom_call_target="tpu_custom_call" | custom-call | tf_op jit(solution)/shard_map/pallas_call | solution.py:36
  71.0 25.1 %all_to_all.15.pieces = bf16[128,16,128]{2,1,0:T(8,128)(2,1)S(1)} all-to-all(bf16[128,16,128]{2,1,0:T(8,128)(2,1)S(1)} %shard_map.177), channel_id=1, replica_groups=mesh['bx'=16,'by'=8,'cz'=2] {'bx','by'}, dimensions={0} | all-to-all | bytes 1048576 | tf_op jit(solution)/shard_map/all_to_all | solution.py:775
  96.0 1.7 %shard_map.178 = (bf16[128,8,128]{2,1,0:T(8,128)(2,1)S(1)}, f32[64,256]{1,0:T(8,128)}, f32[1,64]{1,0:T(1,128)}, f32[1,64]{1,0:T(1,128)}) custom-call(s32[1,3]{1,0:T(1,128)S(1)} %copy-done.6, bf16[128,16,128]{2,1,0:T(8,128)(2,1)S(1)} %all_to_all.15.pieces, f32[256,128]{1,0:T(8,128)S(1)} %bitcast.29, f32[1,128]{1,0:T(1,128)S(1)} %get-tuple-element.62.gain, ...), custom_call_target="tpu_custom_call" | custom-call | tf_op jit(solution)/shard_map/pallas_call | solution.py:36
  97.7 19.0 %all_to_all.16.near = bf16[128,8,128]{2,1,0:T(8,128)(2,1)S(1)} all-to-all(bf16[128,8,128]{2,1,0:T(8,128)(2,1)S(1)} %get-tuple-element.50), channel_id=1, replica_groups=mesh['bx'=16,'by'=8,'cz'=2] {'bx','by'}, dimensions={0} | all-to-all | bytes 524288 | tf_op jit(solution)/shard_map/all_to_all | solution.py:781
  116.7 3.2 %collective-permute-start.6 = (bf16[128,8,128]{2,1,0:T(8,128)(2,1)S(1)}, bf16[128,8,128]{2,1,0:T(8,128)(2,1)S(1)}, u32[]{:S(2)}, u32[]{:S(2)}) collective-permute-start(bf16[128,8,128]{2,1,0:T(8,128)(2,1)S(1)} %all_to_all.16.near), channel_id=1, source_target_pairs={{0,1},{1,0},{2,3},{3,2},{4,5},{5,4},{6,7},{7,6},{8,9},{9,8},{10,11... | collective-permute-start | bytes 786440 | tf_op jit(solution)/shard_map/ppermute | solution.py:782
  119.9 1.2 collective-permute-done.6.far
  121.0 2.1 %shard_map.179 = (f32[27,64,64]{2,1,0:T(8,128)}, f32[27,64,64]{2,1,0:T(8,128)}, f32[64,64]{1,0:T(8,128)}, f32[1,1]{1,0:T(1,128)}) custom-call(s32[1,3]{1,0:T(1,128)S(1)} %copy-done.6, bf16[128,8,128]{2,1,0:T(8,128)(2,1)S(1)} %all_to_all.16.near, bf16[128,8,128]{2,1,0:T(8,128)(2,1)S(1)} %collective-permute-done.6.far), custom_call_target="tpu_custom_call" | custom-call | tf_op jit(solution)/shard_map/pallas_call | solution.py:36
  (23 shorter events, 0.1 us)
Async XLA Ops:
  0.6 1.2 copy-start
  1.9 0.7 copy-start.5
  3.9 4.2 %collective-permute-start = (bf16[10,16,128]{2,1,0:T(8,128)(2,1)S(1)}, bf16[10,16,128]{2,1,0:T(8,128)(2,1)S(1)}, u32[]{:S(2)}, u32[]{:S(2)}) collective-permute-start(bf16[10,16,128]{2,1,0:T(8,128)(2,1)S(1)} %get-tuple-element.33), channel_id=1, source_target_pairs={{0,1},{1,0},{2,3},{3,2},{4,5},{5,4},{6,7},{7,6},{8,9},{9,8},{10,11... | collective-permute-start | bytes 122888 | tf_op jit(solution)/shard_map/ppermute | solution.py:708
  8.1 12.8 %copy-start.3 = (bf16[27,64,64]{2,1,0:T(8,128)(2,1)S(1)}, bf16[27,64,64]{2,1,0:T(8,128)(2,1)}, u32[]{:S(2)}) copy-start(bf16[27,64,64]{2,1,0:T(8,128)(2,1)} %taps.1) | copy-start | bytes 663556
  8.8 15.8 %copy-start.1 = (bf16[16,224,160]{2,1,0:T(8,128)(2,1)S(1)}, bf16[16,224,160]{2,1,0:T(8,128)(2,1)}, u32[]{:S(2)}) copy-start(bf16[16,224,160]{2,1,0:T(8,128)(2,1)} %constant.6.clone.tables) | copy-start | bytes 3440644
  8.8 15.8 %copy-start.4 = (bf16[27,64,64]{2,1,0:T(8,128)(2,1)S(1)}, bf16[27,64,64]{2,1,0:T(8,128)(2,1)}, u32[]{:S(2)}) copy-start(bf16[27,64,64]{2,1,0:T(8,128)(2,1)} %param.16) | copy-start | bytes 663556
  8.8 15.8 %copy-start.7 = (bf16[256,64]{0,1:T(8,128)(2,1)S(1)}, bf16[256,64]{0,1:T(8,128)(2,1)}, u32[]{:S(2)}) copy-start(bf16[256,64]{0,1:T(8,128)(2,1)} %param.18) | copy-start | bytes 98308
  8.8 3.3 %collective-permute-start.1 = (bf16[11,16,128]{2,1,0:T(8,128)(2,1)S(1)}, bf16[11,16,128]{2,1,0:T(8,128)(2,1)S(1)}, u32[]{:S(2)}, u32[]{:S(2)}) collective-permute-start(bf16[11,16,128]{2,1,0:T(8,128)(2,1)S(1)} %get-tuple-element.35), channel_id=1, source_target_pairs={{0,2},{2,4},{4,6},{6,8},{8,10},{10,12},{12,14},{1,3},{3,5},{5,7},{... | collective-permute-start | bytes 135176 | tf_op jit(solution)/shard_map/ppermute | solution.py:678
  10.7 5.0 %collective-permute-start.2 = (bf16[11,16,128]{2,1,0:T(8,128)(2,1)S(1)}, bf16[11,16,128]{2,1,0:T(8,128)(2,1)S(1)}, u32[]{:S(2)}, u32[]{:S(2)}) collective-permute-start(bf16[11,16,128]{2,1,0:T(8,128)(2,1)S(1)} %get-tuple-element.36), channel_id=1, source_target_pairs={{2,0},{4,2},{6,4},{8,6},{10,8},{12,10},{14,12},{3,1},{5,3},{7,5},{... | collective-permute-start | bytes 135176 | tf_op jit(solution)/shard_map/ppermute | solution.py:679
  16.5 8.0 %collective-permute-start.3 = (bf16[14,16,128]{2,1,0:T(8,128)(2,1)S(1)}, bf16[14,16,128]{2,1,0:T(8,128)(2,1)S(1)}, u32[]{:S(2)}, u32[]{:S(2)}) collective-permute-start(bf16[14,16,128]{2,1,0:T(8,128)(2,1)S(1)} %get-tuple-element.40), channel_id=1, source_target_pairs={{0,16},{16,32},{32,48},{48,64},{64,80},{80,96},{96,112},{112,128},... | collective-permute-start | bytes 172040 | tf_op jit(solution)/shard_map/ppermute | solution.py:678
  19.6 4.9 %collective-permute-start.4 = (bf16[14,16,128]{2,1,0:T(8,128)(2,1)S(1)}, bf16[14,16,128]{2,1,0:T(8,128)(2,1)S(1)}, u32[]{:S(2)}, u32[]{:S(2)}) collective-permute-start(bf16[14,16,128]{2,1,0:T(8,128)(2,1)S(1)} %get-tuple-element.41), channel_id=1, source_target_pairs={{16,0},{32,16},{48,32},{64,48},{80,64},{96,80},{112,96},{128,112},... | collective-permute-start | bytes 172040 | tf_op jit(solution)/shard_map/ppermute | solution.py:679
  24.5 21.9 %copy-start.8 = (bf16[64,64]{1,0:T(8,128)(2,1)S(1)}, bf16[64,64]{1,0:T(8,128)(2,1)}, u32[]{:S(2)}) copy-start(bf16[64,64]{1,0:T(8,128)(2,1)} %param.17) | copy-start | bytes 24580
  24.5 22.0 %copy-start.9 = (f32[64]{0:T(128)S(1)}, f32[64]{0:T(128)}, u32[]{:S(2)}) copy-start(f32[64]{0:T(128)} %param.19) | copy-start | bytes 772
  24.6 21.9 %copy-start.10 = (f32[64]{0:T(128)S(1)}, f32[64]{0:T(128)}, u32[]{:S(2)}) copy-start(f32[64]{0:T(128)} %param.20) | copy-start | bytes 772
  24.6 22.1 %copy-start.6 = (s32[1,3]{1,0:T(1,128)S(1)}, s32[1,3]{1,0:T(1,128)}, u32[]{:S(2)}) copy-start(s32[1,3]{1,0:T(1,128)} %info.19) | copy-start | bytes 40
  27.8 31.4 %all-to-all-start = ((f32[256,1,128]{2,1,0:T(1,128)}), f32[256,1,128]{2,1,0:T(1,128)S(1)}, u32[]{:S(2)}, u32[]{:S(2)}) async-start(f32[256,1,128]{2,1,0:T(1,128)} %bitcast.7), calls=%async_computation | async-start | bytes 262144 | tf_op jit(solution)/shard_map/all_to_all | solution.py:672
  46.7 12.5 %copy-start.2 = (bf16[1,16,16,16,64]{4,3,2,1,0:T(8,128)(2,1)S(1)}, bf16[1,16,16,16,64]{4,3,2,1,0:T(8,128)(2,1)}, u32[]{:S(2)}) copy-start(bf16[1,16,16,16,64]{4,3,2,1,0:T(8,128)(2,1)} %param.12) | copy-start | bytes 1572868
  66.5 3.0 %collective-permute-start.5 = (f32[2048,128]{1,0:T(8,128)S(1)}, f32[2048,128]{1,0:T(8,128)S(1)}, u32[]{:S(2)}, u32[]{:S(2)}) collective-permute-start(f32[2048,128]{1,0:T(8,128)S(1)} %get-tuple-element.49), channel_id=1, source_target_pairs={{0,1},{1,0},{2,3},{3,2},{4,5},{5,4},{6,7},{7,6},{8,9},{9,8},{10,11... | collective-permute-start | bytes 3145736 | tf_op jit(solution)/shard_map/ppermute | solution.py:773
  116.7 4.3 %collective-permute-start.6 = (bf16[128,8,128]{2,1,0:T(8,128)(2,1)S(1)}, bf16[128,8,128]{2,1,0:T(8,128)(2,1)S(1)}, u32[]{:S(2)}, u32[]{:S(2)}) collective-permute-start(bf16[128,8,128]{2,1,0:T(8,128)(2,1)S(1)} %all_to_all.16.near), channel_id=1, source_target_pairs={{0,1},{1,0},{2,3},{3,2},{4,5},{5,4},{6,7},{7,6},{8,9},{9,8},{10,11... | collective-permute-start | bytes 786440 | tf_op jit(solution)/shard_map/ppermute | solution.py:782

commit v8 on v7

--- a/solution.py
+++ b/solution.py
@@ -19,16 +19,11 @@
 SHIFT_LANE = 65
 
 
-def face_spec(dim, index):
-    shape = tuple(1 if d == dim else 16 for d in range(3)) + (64,)
-    where = tuple(index if d == dim else 0 for d in range(4))
-    return pl.BlockSpec(shape, lambda i: where)
-
-
-def call(kernel, outs, args, scratch=(), faces=(), far_args=0, far_outs=0):
+def call(kernel, outs, args, scratch=(), far_args=0, far_outs=0, smem_outs=0):
     vmem = pl.BlockSpec(memory_space=pltpu.VMEM)
     far = pl.BlockSpec(memory_space=pl.ANY)
-    specs = list(faces) + [vmem] * (len(args) - 1 - len(faces) - far_args) + [far] * far_args
+    smem = pl.BlockSpec(memory_space=pltpu.SMEM)
+    specs = [vmem] * (len(args) - 1 - far_args) + [far] * far_args
     args = [
         pltpu.with_memory_space_constraint(arg, pltpu.VMEM) if spec is vmem else arg
         for arg, spec in zip(args, [None] + specs)
@@ -37,8 +32,8 @@
         kernel,
         grid=(1,),
         out_shape=outs,
-        in_specs=[pl.BlockSpec(memory_space=pltpu.SMEM)] + specs,
-        out_specs=[vmem] * (len(outs) - far_outs) + [far] * far_outs,
+        in_specs=[smem] + specs,
+        out_specs=[vmem] * (len(outs) - far_outs - smem_outs) + [far] * far_outs + [smem] * smem_outs,
         scratch_shapes=list(scratch),
         compiler_params=pltpu.CompilerParams(vmem_limit_bytes=VMEM_LIMIT),
     )(*args)
@@ -115,19 +110,32 @@
         out[32 + t] = jnp.concatenate([ref[8 + t, :, :64], ref[8 + t, :, 64:]], axis=0)
 
 
-def z_message(info, lat, out, pooled):
+def z_message(info, lat_in, out, pooled, y_low, y_high, x_low, x_high, info_out, lat, fetched):
     px, py, pz, kz = bits(info)
     zsel = 15 * (1 - kz)
+    for d in range(3):
+        info_out[0, d] = info[0, d]
+
+    def chunk(n):
+        part = pl.ds(4 * n, 4)
+        return pltpu.make_async_copy(lat_in.at[:, part], lat.at[:, part], fetched.at[n])
+
+    for n in range(4):
+        chunk(n).start()
     pick = lax.broadcasted_iota(jnp.int32, (16, 16, 64), 1) == zsel
     sums = [[None, None], [None, None]]
     faces = []
     for y in range(16):
+        if y % 4 == 0:
+            chunk(y // 4).wait()
         slab = lat[:, y].astype(F32)
         faces.append(jnp.sum(jnp.where(pick, slab, 0.0), axis=1)[None])
         for a in range(2):
             part = jnp.sum(slab[8 * a : 8 * a + 8], axis=0)
             old = sums[a][y // 8]
             sums[a][y // 8] = part if old is None else old + part
+    y_low[...], y_high[...] = lat[:, 0], lat[:, 15]
+    x_low[...], x_high[...] = lat[0], lat[15]
     cells = []
     for a in range(2):
         for b in range(2):
@@ -155,7 +163,7 @@
         picked = [[row_of(cells, 4 * a + 2 * q + c) for c in range(2)] for a in range(2)]
         tail = halo[12:16] if q else halo[0:4]
         rows = jnp.concatenate([cell_rows(px, pz, picked, on), tail, jnp.zeros((12, 64), F32)], axis=0)
-        write_message(out, face[:, 0], [rz[line], rows], px, pz, on)
+        write_message(out, face[...], [rz[line], rows], px, pz, on)
 
 
 def x_messages(info, low, high, rz_in, rym_in, ryp_in, pooled, down, up, rz, rym, ryp):
@@ -181,7 +189,7 @@
         parts += [halo_m[4 * c0 : 4 * c0 + 4], halo_p[4 * c0 : 4 * c0 + 4]]
         parts += [row_of(halo_m, 16 + c0), row_of(halo_p, 16 + c0), jnp.zeros((18, 64), F32)]
         tiles = [z_line, rym[line], ryp[line], corners, jnp.concatenate(parts, axis=0)]
-        write_message(out, face[0], tiles, py, pz, on)
+        write_message(out, face[...], tiles, py, pz, on)
 
 
 def coarse_table():
@@ -260,7 +268,7 @@
     return ref[i].astype(F32)[j : j + 1]
 
 
-def interior(info, lat, rz_in, rym_in, ryp_in, taps, raw, scene, columns, weight, rz, rym, ryp):
+def interior(info, lat, rz_in, rym_in, ryp_in, taps, raw, scene, columns, weight, near_low, near_high, rz, rym, ryp):
     for ref, out in ((rz_in, rz), (rym_in, rym), (ryp_in, ryp)):
         open_message(ref, out)
     nought = jnp.zeros((64, 64), BF)
@@ -292,6 +300,10 @@
         planes = w.offsets(lat[x, :, 0], lat[x, :, 1], y_low[x], y_high[x], zl, zh)
         for oz, plane in enumerate(planes):
             scene[oz, x] = plane
+            if x < 2:
+                near_low[oz, x] = plane
+            if x > 13:
+                near_high[oz, x - 14] = plane
             wide = plane.astype(F32)
             inner[oz] = wide if x == 0 else inner[oz] + wide
     for oz in range(3):
@@ -704,42 +716,46 @@
     lat = latents[0]
     lat_pairs = lat.reshape(16, 8, 2, 16, 64)
 
-    mz, pooled = call(z_message, [message(Z_TILES), like((16, 64), BF)], [info, lat])
+    face = like((16, 16, 64), BF)
+    mz, pooled, y_low, y_high, x_low, x_high, info = call(
+        z_message,
+        [message(Z_TILES), like((16, 64), BF), face, face, face, face, like((1, 3), jnp.int32)],
+        [in_hbm(info), in_hbm(lat)],
+        [pltpu.VMEM((16, 16, 16, 64), BF), pltpu.SemaphoreType.DMA((4,))],
+        far_args=1,
+        smem_outs=1,
+    )
     rz = lax.ppermute(mz, "cz", [(0, 1), (1, 0)])
     out = message(Y_TILES)
-    down, up = call(
-        y_messages, [out, out], [info, lat, lat, rz, pooled], [plane(Z_TILES)], [face_spec(1, 0), face_spec(1, 15)]
-    )
+    down, up = call(y_messages, [out, out], [info, y_low, y_high, rz, pooled], [plane(Z_TILES)])
     rym, ryp = neighbours(down, up, "by")
     out = message(X_TILES)
     planes = [plane(Z_TILES), plane(Y_TILES), plane(Y_TILES)]
     down, up = call(
         x_messages,
         [out, out],
-        [info, lat, lat, rz, rym, ryp, pooled],
+        [info, x_low, x_high, rz, rym, ryp, pooled],
         planes,
-        [face_spec(0, 0), face_spec(0, 15)],
     )
     rxm, rxp = neighbours(down, up, "bx")
 
     temb = time_embedding(timestep, time_weight.shape[0]).reshape(1, -1)
-    raw, scene, columns, taps = call(
+    pair = like((3, 2, 9, 16, 128), BF)
+    raw, scene, columns, taps, near_low, near_high = call(
         interior,
-        [like((1792, 128), F32), like((3, 16, 9, 16, 128), BF), like((3, 9, 128), F32), like((2304, 128), BF)],
+        [like((1792, 128), F32), like((3, 16, 9, 16, 128), BF), like((3, 9, 128), F32), like((2304, 128), BF), pair, pair],
         [info, lat_pairs, rz, rym, ryp, conv_weight],
         planes,
     )
-    pair = (3, 2, 9, 16, 128)
     tables = jnp.asarray(coarse_table(), BF)
     act, ends, patch, stats = call(
         forward,
         [pltpu.HBM((2048, 128), F32), like((2, 3, 9, 16, 128), BF), like((16, 1728), BF), like((devices, 128), F32)],
-        [info, scene, scene, raw, columns, rz, rym, ryp, rxm, rxp, pooled, taps]
+        [info, near_low, near_high, raw, columns, rz, rym, ryp, rxm, rxp, pooled, taps]
         + [coarse_weight.reshape(1728, 64), temb, time_weight.T, tables],
         [pltpu.VMEM((2, 128, 128), F32), pltpu.VMEM((224, 160), BF), pltpu.SemaphoreType.DMA]
         + planes
         + [plane(X_TILES), plane(X_TILES)],
-        [pl.BlockSpec(pair, lambda i: (0, 0, 0, 0, 0)), pl.BlockSpec(pair, lambda i: (0, 7, 0, 0, 0))],
         far_args=1,
     )
     first = exchange(stats)

time: 123 us -> 125 us (1.016)
  Pallas kernels: 24.7 us -> 26.4 us
    pallas_call x10, Pallas kernels: 24.7 us -> 26.4 us  [call(): pl.pallas_call(kernel, grid=(1,), out_shape=outs, in_specs=[smem] + specs...]
    unnamed x23 -> x19, local copies, waits for them, and re-layouts: 2.01 us -> 2.89 us
  transfers between devices with their start and end apart: 8 -> 8, of which waited for: 6 -> 5; matrix products, arithmetic and copies ran while one was open for 0% -> 0% of each run, Pallas kernels for 5% -> 5%
where the time goes in v8:
time: 125 us
  blocking collectives  44 us (35%)
  starting transfers between devices  32.4 us (26%)
  Pallas kernels  26.4 us (21%)
  waiting for transfers between devices  17.1 us (14%)
  local copies, waits for them, and re-layouts  2.89 us (2%)
  between operations  1.5 us (1%)
    pallas_call x10, Pallas kernels, call(): pl.pallas_call(kernel, grid=(1,), out_shape=outs, in_specs=[smem] + specs...  26.4 us
    all_to_all x1, blocking collectives, shards(): pieces = lax.all_to_all(pieces, CHIPS, 0, 0, tiled=True)  25.1 us
    all_to_all x1, blocking collectives, shards(): near = lax.all_to_all(copies, CHIPS, 0, 0, tiled=True)  19 us
    all_to_all x1, starting transfers between devices, exchange(): lax.all_to_all(rows.reshape(rows.shape[0], 1, 128), ('cz',) + CHIPS, 0, 0...  17.6 us
    all_to_all x1, waiting for transfers between devices, exchange(): lax.all_to_all(rows.reshape(rows.shape[0], 1, 128), ('cz',) + CHIPS, 0, 0...  9.84 us
    ppermute x2, starting transfers between devices, neighbours(): before = lax.ppermute(up, axis, [(i, i + 1) for i in range(ends)])  4.92 us
    ppermute x2, waiting for transfers between devices, neighbours(): after = lax.ppermute(down, axis, [(i + 1, i) for i in range(ends)])  3.61 us
    ppermute x1, starting transfers between devices, shards(): rz = lax.ppermute(mz, 'cz', [(0, 1), (1, 0)])  3.33 us
  transfers between devices with their start and end apart: 8, of which 5 were waited for; matrix products, arithmetic and copies ran while one was open for 0% of the time, Pallas kernels for 5%

profile of v8, /device:TPU:1, one launch (start us, length us, event | category | flops | bytes accessed | tf_op | source)
XLA Modules:
  0.0 124.6 jit_solution(2418566442200774141)
XLA Ops:
  0.6 0.0 copy-start.1
  0.7 3.1 %shard_map.170 = (bf16[10,16,128]{2,1,0:T(8,128)(2,1)S(1)}, bf16[16,64]{1,0:T(8,128)(2,1)S(1)}, bf16[16,16,64]{2,1,0:T(8,128)(2,1)S(1)}, bf16[16,16,64]{2,1,0:T(...) custom-call(s32[1,3]{1,0:T(1,128)} %info.1, ...), custom_call_target="tpu_custom_call" | custom-call | tf_op jit(solution)/shard_map/pallas_call | solution.py:31
  3.8 3.3 %collective-permute-start = (bf16[10,16,128]{2,1,0:T(8,128)(2,1)S(1)}, bf16[10,16,128]{2,1,0:T(8,128)(2,1)S(1)}, u32[]{:S(2)}, u32[]{:S(2)}) collective-permute-start(bf16[10,16,128]{2,1,0:T(8,128)(2,1)S(1)} %get-tuple-element.41), channel_id=1, source_target_pairs={{0,1},{1,0},{2,3},{3,2},{4,5},{5,4},{6,7},{7,6},{8,9},{9,8},{10,11... | collective-permute-start | bytes 122888 | tf_op jit(solution)/shard_map/ppermute | solution.py:728
  7.8 0.2 collective-permute-done.rz_in
  8.0 0.7 shard_map.171
  8.7 1.8 %collective-permute-start.1 = (bf16[11,16,128]{2,1,0:T(8,128)(2,1)S(1)}, bf16[11,16,128]{2,1,0:T(8,128)(2,1)S(1)}, u32[]{:S(2)}, u32[]{:S(2)}) collective-permute-start(bf16[11,16,128]{2,1,0:T(8,128)(2,1)S(1)} %get-tuple-element.45), channel_id=1, source_target_pairs={{0,2},{2,4},{4,6},{6,8},{8,10},{10,12},{12,14},{1,3},{3,5},{5,7},{... | collective-permute-start | bytes 135176 | tf_op jit(solution)/shard_map/ppermute | solution.py:690
  10.5 1.3 %collective-permute-start.2 = (bf16[11,16,128]{2,1,0:T(8,128)(2,1)S(1)}, bf16[11,16,128]{2,1,0:T(8,128)(2,1)S(1)}, u32[]{:S(2)}, u32[]{:S(2)}) collective-permute-start(bf16[11,16,128]{2,1,0:T(8,128)(2,1)S(1)} %get-tuple-element.46), channel_id=1, source_target_pairs={{2,0},{4,2},{6,4},{8,6},{10,8},{12,10},{14,12},{3,1},{5,3},{7,5},{... | collective-permute-start | bytes 135176 | tf_op jit(solution)/shard_map/ppermute | solution.py:691
  11.9 3.6 %collective-permute-done.2.ryp_in = bf16[11,16,128]{2,1,0:T(8,128)(2,1)S(1)} collective-permute-done((bf16[11,16,128]{2,1,0:T(8,128)(2,1)S(1)}, bf16[11,16,128]{2,1,0:T(8,128)(2,1)S(1)}, u32[]{:S(2)}, u32[]{:S(2)}) %collective-permute-start.2) | collective-permute-done | bytes 45088 | tf_op jit(solution)/shard_map/ppermute | solution.py:691
  15.5 0.8 shard_map.173
  16.2 3.1 %collective-permute-start.3 = (bf16[14,16,128]{2,1,0:T(8,128)(2,1)S(1)}, bf16[14,16,128]{2,1,0:T(8,128)(2,1)S(1)}, u32[]{:S(2)}, u32[]{:S(2)}) collective-permute-start(bf16[14,16,128]{2,1,0:T(8,128)(2,1)S(1)} %get-tuple-element.53), channel_id=1, source_target_pairs={{0,16},{16,32},{32,48},{48,64},{64,80},{80,96},{96,112},{112,128},... | collective-permute-start | bytes 172040 | tf_op jit(solution)/shard_map/ppermute | solution.py:690
  19.4 1.3 %collective-permute-start.4 = (bf16[14,16,128]{2,1,0:T(8,128)(2,1)S(1)}, bf16[14,16,128]{2,1,0:T(8,128)(2,1)S(1)}, u32[]{:S(2)}, u32[]{:S(2)}) collective-permute-start(bf16[14,16,128]{2,1,0:T(8,128)(2,1)S(1)} %get-tuple-element.54), channel_id=1, source_target_pairs={{16,0},{32,16},{48,32},{64,48},{80,64},{96,80},{112,96},{128,112},... | collective-permute-start | bytes 172040 | tf_op jit(solution)/shard_map/ppermute | solution.py:691
  20.7 1.0 copy-done.4
  21.7 3.5 %shard_map.172 = (f32[1792,128]{1,0:T(8,128)S(1)}, bf16[3,16,9,16,128]{4,3,2,1,0:T(8,128)(2,1)S(1)}, f32[3,9,128]{2,1,0:T(8,128)S(1)}, bf16[2304,128]{1,0:T(8,12...) custom-call(s32[1,3]{1,0:T(1,128)S(1)} %get-tuple-element.40.info, ...), custom_call_target="tpu_custom_call" | custom-call | tf_op jit(solution)/shard_map/pallas_call | solution.py:31
  25.3 1.0 copy-done.3
  26.3 0.8 copy-done.5
  27.0 3.2 %shard_map.174 = (f32[2048,128]{1,0:T(8,128)}, bf16[2,3,9,16,128]{4,3,2,1,0:T(8,128)(2,1)S(1)}, bf16[16,1728]{1,0:T(8,128)(2,1)S(1)}, f32[256,128]{1,0:T(8,128)}) custom-call(s32[1,3]{1,0:T(1,128)S(1)} %get-tuple-element.40.info, bf16[3,2,9,16,128]{4,3,2,1,0:T(8,128)(2,1)S(1)} %get-tuple-element.47.near_low, ...), custom_call_target="tpu_custom_call" | custom-call | tf_op jit(solution)/shard_map/pallas_call | solution.py:31
  30.2 17.6 %all-to-all-start = ((f32[256,1,128]{2,1,0:T(1,128)}), f32[256,1,128]{2,1,0:T(1,128)S(1)}, u32[]{:S(2)}, u32[]{:S(2)}) async-start(f32[256,1,128]{2,1,0:T(1,128)} %bitcast.7), calls=%async_computation | async-start | bytes 262144 | tf_op jit(solution)/shard_map/all_to_all | solution.py:684
  47.9 0.1 copy.21
  48.0 0.1 maximum_bitcast_fusion
  48.1 0.1 fusion.4
  48.1 2.7 %shard_map.175.turned_in = bf16[3,256,2304]{2,1,0:T(8,128)(2,1)} custom-call(s32[1,3]{1,0:T(1,128)S(1)} %get-tuple-element.40.info, bf16[3,16,9,16,128]{4,3,2,1,0:T(8,128)(2,1)S(1)} %get-tuple-element.59.scene, bf16[2,3,9,16,128]{4,3,2,1,0:T(8,128)(2,1)S(1)} %get-tuple-element.60.ends), custom_call_target="tpu_custom_call" | custom-call | tf_op jit(solution)/shard_map/pallas_call | solution.py:31
  50.8 9.8 %all-to-all-done = f32[256,1,128]{2,1,0:T(1,128)S(1)} async-done(((f32[256,1,128]{2,1,0:T(1,128)}), f32[256,1,128]{2,1,0:T(1,128)S(1)}, u32[]{:S(2)}, u32[]{:S(2)}) %all-to-all-start) | async-done | bytes 131104 | tf_op jit(solution)/shard_map/all_to_all | solution.py:684
  60.7 7.3 %shard_map.176 = (f32[2,2064,128]{2,1,0:T(8,128)S(1)}, f32[2048,128]{1,0:T(8,128)S(1)}, bf16[16,8,2,16,64]{4,3,2,1,0:T(8,128)(2,1)}) custom-call(s32[1,3]{1,0:T(1,128)S(1)} %get-tuple-element.40.info, f32[256,128]{1,0:T(8,128)S(1)} %bitcast.23, bf16[16,8,2,16,64]{4,3,2,1,0:T(8,128)(2,1)S(1)} %bitcast.26, f32[1,128]{1,0:T(1,128)S(1)} %get-tuple-element.76.gain, ...), custom_call_target="tpu_custom_call" | custom-call | tf_op jit(solution)/shard_map/pallas_call | solution.py:31
  68.0 0.7 collective-permute-start.5
  68.7 2.3 %collective-permute-done.5.other = f32[2048,128]{1,0:T(8,128)S(1)} collective-permute-done((f32[2048,128]{1,0:T(8,128)S(1)}, f32[2048,128]{1,0:T(8,128)S(1)}, u32[]{:S(2)}, u32[]{:S(2)}) %collective-permute-start.5) | collective-permute-done | bytes 1048608 | tf_op jit(solution)/shard_map/ppermute | solution.py:789
  71.0 1.4 %shard_map.177 = bf16[128,16,128]{2,1,0:T(8,128)(2,1)S(1)} custom-call(s32[1,3]{1,0:T(1,128)S(1)} %get-tuple-element.40.info, f32[2,2064,128]{2,1,0:T(8,128)S(1)} %get-tuple-element.62.mine, f32[2048,128]{1,0:T(8,128)S(1)} %collective-permute-done.5.other, f32[256,128]{1,0:T(8,128)S(1)} %bitcast.24, f32[1,128]{1,0:T(1,128)S(1)} %get-tuple-element.76.gain), custom_call_target="tpu_custom_call" | custom-call | tf_op jit(solution)/shard_map/pallas_call | solution.py:31
  72.4 25.1 %all_to_all.15.pieces = bf16[128,16,128]{2,1,0:T(8,128)(2,1)S(1)} all-to-all(bf16[128,16,128]{2,1,0:T(8,128)(2,1)S(1)} %shard_map.177), channel_id=1, replica_groups=mesh['bx'=16,'by'=8,'cz'=2] {'bx','by'}, dimensions={0} | all-to-all | bytes 1048576 | tf_op jit(solution)/shard_map/all_to_all | solution.py:791
  97.5 1.7 %shard_map.178 = (bf16[128,8,128]{2,1,0:T(8,128)(2,1)S(1)}, f32[64,256]{1,0:T(8,128)}, f32[1,64]{1,0:T(1,128)}, f32[1,64]{1,0:T(1,128)}) custom-call(s32[1,3]{1,0:T(1,128)S(1)} %get-tuple-element.40.info, bf16[128,16,128]{2,1,0:T(8,128)(2,1)S(1)} %all_to_all.15.pieces, f32[256,128]{1,0:T(8,128)S(1)} %bitcast.25, f32[1,128]{1,0:T(1,128)S(1)} %get-tuple-element.76.gain, ...), custom_call_target="tpu_custom_call" | custom-call | tf_op jit(solution)/shard_map/pallas_call | solution.py:31
  99.2 19.0 %all_to_all.16.near = bf16[128,8,128]{2,1,0:T(8,128)(2,1)S(1)} all-to-all(bf16[128,8,128]{2,1,0:T(8,128)(2,1)S(1)} %get-tuple-element.64), channel_id=1, replica_groups=mesh['bx'=16,'by'=8,'cz'=2] {'bx','by'}, dimensions={0} | all-to-all | bytes 524288 | tf_op jit(solution)/shard_map/all_to_all | solution.py:797
  118.2 3.2 %collective-permute-start.6 = (bf16[128,8,128]{2,1,0:T(8,128)(2,1)S(1)}, bf16[128,8,128]{2,1,0:T(8,128)(2,1)S(1)}, u32[]{:S(2)}, u32[]{:S(2)}) collective-permute-start(bf16[128,8,128]{2,1,0:T(8,128)(2,1)S(1)} %all_to_all.16.near), channel_id=1, source_target_pairs={{0,1},{1,0},{2,3},{3,2},{4,5},{5,4},{6,7},{7,6},{8,9},{9,8},{10,11... | collective-permute-start | bytes 786440 | tf_op jit(solution)/shard_map/ppermute | solution.py:798
  121.3 1.2 collective-permute-done.6.far
  122.5 2.1 %shard_map.179 = (f32[27,64,64]{2,1,0:T(8,128)}, f32[27,64,64]{2,1,0:T(8,128)}, f32[64,64]{1,0:T(8,128)}, f32[1,1]{1,0:T(1,128)}) custom-call(s32[1,3]{1,0:T(1,128)S(1)} %get-tuple-element.40.info, bf16[128,8,128]{2,1,0:T(8,128)(2,1)S(1)} %all_to_all.16.near, bf16[128,8,128]{2,1,0:T(8,128)(2,1)S(1)} %collective-permute-done.6.far), custom_call_target="tpu_custom_call" | custom-call | tf_op jit(solution)/shard_map/pallas_call | solution.py:31
  (19 shorter events, 0.1 us)
Async XLA Ops:
  0.6 20.0 %copy-start = (bf16[1,16,16,16,64]{4,3,2,1,0:T(8,128)(2,1)S(1)}, bf16[1,16,16,16,64]{4,3,2,1,0:T(8,128)(2,1)}, u32[]{:S(2)}) copy-start(bf16[1,16,16,16,64]{4,3,2,1,0:T(8,128)(2,1)} %param.11) | copy-start | bytes 1572868
  0.6 24.6 %copy-start.1 = (bf16[16,224,160]{2,1,0:T(8,128)(2,1)S(1)}, bf16[16,224,160]{2,1,0:T(8,128)(2,1)}, u32[]{:S(2)}) copy-start(bf16[16,224,160]{2,1,0:T(8,128)(2,1)} %constant.6.clone.tables) | copy-start | bytes 3440644
  3.8 4.2 %collective-permute-start = (bf16[10,16,128]{2,1,0:T(8,128)(2,1)S(1)}, bf16[10,16,128]{2,1,0:T(8,128)(2,1)S(1)}, u32[]{:S(2)}, u32[]{:S(2)}) collective-permute-start(bf16[10,16,128]{2,1,0:T(8,128)(2,1)S(1)} %get-tuple-element.41), channel_id=1, source_target_pairs={{0,1},{1,0},{2,3},{3,2},{4,5},{5,4},{6,7},{7,6},{8,9},{9,8},{10,11... | collective-permute-start | bytes 122888 | tf_op jit(solution)/shard_map/ppermute | solution.py:728
  8.7 3.2 %collective-permute-start.1 = (bf16[11,16,128]{2,1,0:T(8,128)(2,1)S(1)}, bf16[11,16,128]{2,1,0:T(8,128)(2,1)S(1)}, u32[]{:S(2)}, u32[]{:S(2)}) collective-permute-start(bf16[11,16,128]{2,1,0:T(8,128)(2,1)S(1)} %get-tuple-element.45), channel_id=1, source_target_pairs={{0,2},{2,4},{4,6},{6,8},{8,10},{10,12},{12,14},{1,3},{3,5},{5,7},{... | collective-permute-start | bytes 135176 | tf_op jit(solution)/shard_map/ppermute | solution.py:690
  10.5 5.0 %collective-permute-start.2 = (bf16[11,16,128]{2,1,0:T(8,128)(2,1)S(1)}, bf16[11,16,128]{2,1,0:T(8,128)(2,1)S(1)}, u32[]{:S(2)}, u32[]{:S(2)}) collective-permute-start(bf16[11,16,128]{2,1,0:T(8,128)(2,1)S(1)} %get-tuple-element.46), channel_id=1, source_target_pairs={{2,0},{4,2},{6,4},{8,6},{10,8},{12,10},{14,12},{3,1},{5,3},{7,5},{... | collective-permute-start | bytes 135176 | tf_op jit(solution)/shard_map/ppermute | solution.py:691
  16.2 9.0 %collective-permute-start.3 = (bf16[14,16,128]{2,1,0:T(8,128)(2,1)S(1)}, bf16[14,16,128]{2,1,0:T(8,128)(2,1)S(1)}, u32[]{:S(2)}, u32[]{:S(2)}) collective-permute-start(bf16[14,16,128]{2,1,0:T(8,128)(2,1)S(1)} %get-tuple-element.53), channel_id=1, source_target_pairs={{0,16},{16,32},{32,48},{48,64},{64,80},{80,96},{96,112},{112,128},... | collective-permute-start | bytes 172040 | tf_op jit(solution)/shard_map/ppermute | solution.py:690
  19.4 5.9 %collective-permute-start.4 = (bf16[14,16,128]{2,1,0:T(8,128)(2,1)S(1)}, bf16[14,16,128]{2,1,0:T(8,128)(2,1)S(1)}, u32[]{:S(2)}, u32[]{:S(2)}) collective-permute-start(bf16[14,16,128]{2,1,0:T(8,128)(2,1)S(1)} %get-tuple-element.54), channel_id=1, source_target_pairs={{16,0},{32,16},{48,32},{64,48},{80,64},{96,80},{112,96},{128,112},... | collective-permute-start | bytes 172040 | tf_op jit(solution)/shard_map/ppermute | solution.py:691
  20.7 1.0 copy-start.4
  25.2 1.0 copy-start.3
  26.3 0.8 copy-start.5
  27.0 20.9 %copy-start.6 = (bf16[64,64]{1,0:T(8,128)(2,1)S(1)}, bf16[64,64]{1,0:T(8,128)(2,1)}, u32[]{:S(2)}) copy-start(bf16[64,64]{1,0:T(8,128)(2,1)} %param.17) | copy-start | bytes 24580
  27.0 21.0 %copy-start.7 = (f32[64]{0:T(128)S(1)}, f32[64]{0:T(128)}, u32[]{:S(2)}) copy-start(f32[64]{0:T(128)} %param.19) | copy-start | bytes 772
  27.0 21.0 %copy-start.8 = (f32[64]{0:T(128)S(1)}, f32[64]{0:T(128)}, u32[]{:S(2)}) copy-start(f32[64]{0:T(128)} %param.20) | copy-start | bytes 772
  30.2 30.4 %all-to-all-start = ((f32[256,1,128]{2,1,0:T(1,128)}), f32[256,1,128]{2,1,0:T(1,128)S(1)}, u32[]{:S(2)}, u32[]{:S(2)}) async-start(f32[256,1,128]{2,1,0:T(1,128)} %bitcast.7), calls=%async_computation | async-start | bytes 262144 | tf_op jit(solution)/shard_map/all_to_all | solution.py:684
  48.1 12.5 %copy-start.2 = (bf16[1,16,16,16,64]{4,3,2,1,0:T(8,128)(2,1)S(1)}, bf16[1,16,16,16,64]{4,3,2,1,0:T(8,128)(2,1)}, u32[]{:S(2)}) copy-start(bf16[1,16,16,16,64]{4,3,2,1,0:T(8,128)(2,1)} %param.12) | copy-start | bytes 1572868
  68.0 3.0 %collective-permute-start.5 = (f32[2048,128]{1,0:T(8,128)S(1)}, f32[2048,128]{1,0:T(8,128)S(1)}, u32[]{:S(2)}, u32[]{:S(2)}) collective-permute-start(f32[2048,128]{1,0:T(8,128)S(1)} %get-tuple-element.63), channel_id=1, source_target_pairs={{0,1},{1,0},{2,3},{3,2},{4,5},{5,4},{6,7},{7,6},{8,9},{9,8},{10,11... | collective-permute-start | bytes 3145736 | tf_op jit(solution)/shard_map/ppermute | solution.py:789
  118.2 4.3 %collective-permute-start.6 = (bf16[128,8,128]{2,1,0:T(8,128)(2,1)S(1)}, bf16[128,8,128]{2,1,0:T(8,128)(2,1)S(1)}, u32[]{:S(2)}, u32[]{:S(2)}) collective-permute-start(bf16[128,8,128]{2,1,0:T(8,128)(2,1)S(1)} %all_to_all.16.near), channel_id=1, source_target_pairs={{0,1},{1,0},{2,3},{3,2},{4,5},{5,4},{6,7},{7,6},{8,9},{9,8},{10,11... | collective-permute-start | bytes 786440 | tf_op jit(solution)/shard_map/ppermute | solution.py:798

commit v9 on v7

--- a/solution.py
+++ b/solution.py
@@ -260,9 +260,7 @@
     return ref[i].astype(F32)[j : j + 1]
 
 
-def interior(info, lat, rz_in, rym_in, ryp_in, taps, raw, scene, columns, weight, rz, rym, ryp):
-    for ref, out in ((rz_in, rz), (rym_in, rym), (ryp_in, ryp)):
-        open_message(ref, out)
+def interior(info, lat, rz, rym, ryp, taps, raw, scene, columns, weight):
     nought = jnp.zeros((64, 64), BF)
     for tap in range(9):
         ox, oz = tap // 3, tap % 3
@@ -308,14 +306,14 @@
 
 
 def forward(
-    info, near_low, near_high, raw, columns, rz_in, rym_in, ryp_in, rxm_in, rxp_in, pooled, weight,
+    info, near_low, near_high, raw, columns, rz, rym, ryp, rxm_in, rxp_in, pooled, weight,
     coarse_weight, temb, time_weight, tables, act, ends, patch_out, stats,
-    shift, table, arrived, rz, rym, ryp, rxm, rxp
+    shift, table, arrived, rxm, rxp
 ):
     px, py, pz, kz = bits(info)
     fetch = pltpu.make_async_copy(tables.at[8 * px + 4 * py + 2 * pz + kz], table, arrived)
     fetch.start()
-    for ref, out in ((rz_in, rz), (rym_in, rym), (ryp_in, ryp), (rxm_in, rxm), (rxp_in, rxp)):
+    for ref, out in ((rxm_in, rxm), (rxp_in, rxp)):
         open_message(ref, out)
     w = Window(info, rz, rym, ryp)
     nought = jnp.zeros((16, 64), BF)
@@ -712,12 +710,12 @@
     )
     rym, ryp = neighbours(down, up, "by")
     out = message(X_TILES)
-    planes = [plane(Z_TILES), plane(Y_TILES), plane(Y_TILES)]
-    down, up = call(
+    planes = [like((32 + tiles, 32, 64), BF) for tiles in (Z_TILES, Y_TILES, Y_TILES)]
+    down, up, rz, rym, ryp = call(
         x_messages,
-        [out, out],
+        [out, out] + planes,
         [info, lat, lat, rz, rym, ryp, pooled],
-        planes,
+        (),
         [face_spec(0, 0), face_spec(0, 15)],
     )
     rxm, rxp = neighbours(down, up, "bx")
@@ -727,7 +725,6 @@
         interior,
         [like((1792, 128), F32), like((3, 16, 9, 16, 128), BF), like((3, 9, 128), F32), like((2304, 128), BF)],
         [info, lat_pairs, rz, rym, ryp, conv_weight],
-        planes,
     )
     pair = (3, 2, 9, 16, 128)
     tables = jnp.asarray(coarse_table(), BF)
@@ -737,7 +734,6 @@
         [info, scene, scene, raw, columns, rz, rym, ryp, rxm, rxp, pooled, taps]
         + [coarse_weight.reshape(1728, 64), temb, time_weight.T, tables],
         [pltpu.VMEM((2, 128, 128), F32), pltpu.VMEM((224, 160), BF), pltpu.SemaphoreType.DMA]
-        + planes
         + [plane(X_TILES), plane(X_TILES)],
         [pl.BlockSpec(pair, lambda i: (0, 0, 0, 0, 0)), pl.BlockSpec(pair, lambda i: (0, 7, 0, 0, 0))],
         far_args=1,

time: 123 us -> 123 us (level)
  no operation moved by 1% of the time
where the time goes in v9:
time: 123 us
  blocking collectives  44.1 us (36%)
  starting transfers between devices  33.3 us (27%)
  Pallas kernels  24.5 us (20%)
  waiting for transfers between devices  17.2 us (14%)
  local copies, waits for them, and re-layouts  2.01 us (2%)
  between operations  1.52 us (1%)
    all_to_all x1, blocking collectives, shards(): pieces = lax.all_to_all(pieces, CHIPS, 0, 0, tiled=True)  25.1 us
    pallas_call x10, Pallas kernels, call(): pl.pallas_call(kernel, grid=(1,), out_shape=outs, in_specs=[pl.BlockSpec(...  24.5 us
    all_to_all x1, blocking collectives, shards(): near = lax.all_to_all(copies, CHIPS, 0, 0, tiled=True)  19 us
    all_to_all x1, starting transfers between devices, exchange(): lax.all_to_all(rows.reshape(rows.shape[0], 1, 128), ('cz',) + CHIPS, 0, 0...  18.6 us
    all_to_all x1, waiting for transfers between devices, exchange(): lax.all_to_all(rows.reshape(rows.shape[0], 1, 128), ('cz',) + CHIPS, 0, 0...  9.81 us
    ppermute x2, starting transfers between devices, neighbours(): before = lax.ppermute(up, axis, [(i, i + 1) for i in range(ends)])  4.92 us
    ppermute x2, waiting for transfers between devices, neighbours(): after = lax.ppermute(down, axis, [(i + 1, i) for i in range(ends)])  3.75 us
    ppermute x1, starting transfers between devices, shards(): rz = lax.ppermute(mz, 'cz', [(0, 1), (1, 0)])  3.33 us
  transfers between devices with their start and end apart: 8, of which 6 were waited for; matrix products, arithmetic and copies ran while one was open for 0% of the time, Pallas kernels for 5%

profile of v9, /device:TPU:1, one launch (start us, length us, event | category | flops | bytes accessed | tf_op | source)
XLA Modules:
  0.0 122.8 jit_solution(13561195500126472083)
XLA Ops:
  0.6 1.2 copy-done
  1.9 0.7 copy-done.5
  2.5 1.4 %shard_map.170 = (bf16[10,16,128]{2,1,0:T(8,128)(2,1)S(1)}, bf16[16,64]{1,0:T(8,128)(2,1)S(1)}) custom-call(s32[1,3]{1,0:T(1,128)S(1)} %copy-done.5, bf16[16,16,16,64]{3,2,1,0:T(8,128)(2,1)S(1)} %bitcast.21), custom_call_target="tpu_custom_call" | custom-call | tf_op jit(solution)/shard_map/pallas_call | solution.py:36
  3.9 3.3 %collective-permute-start = (bf16[10,16,128]{2,1,0:T(8,128)(2,1)S(1)}, bf16[10,16,128]{2,1,0:T(8,128)(2,1)S(1)}, u32[]{:S(2)}, u32[]{:S(2)}) collective-permute-start(bf16[10,16,128]{2,1,0:T(8,128)(2,1)S(1)} %get-tuple-element.36), channel_id=1, source_target_pairs={{0,1},{1,0},{2,3},{3,2},{4,5},{5,4},{6,7},{7,6},{8,9},{9,8},{10,11... | collective-permute-start | bytes 122888 | tf_op jit(solution)/shard_map/ppermute | solution.py:706
  7.9 0.2 collective-permute-done.rz_in
  8.1 0.7 shard_map.171
  8.8 1.8 %collective-permute-start.1 = (bf16[11,16,128]{2,1,0:T(8,128)(2,1)S(1)}, bf16[11,16,128]{2,1,0:T(8,128)(2,1)S(1)}, u32[]{:S(2)}, u32[]{:S(2)}) collective-permute-start(bf16[11,16,128]{2,1,0:T(8,128)(2,1)S(1)} %get-tuple-element.38), channel_id=1, source_target_pairs={{0,2},{2,4},{4,6},{6,8},{8,10},{10,12},{12,14},{1,3},{3,5},{5,7},{... | collective-permute-start | bytes 135176 | tf_op jit(solution)/shard_map/ppermute | solution.py:676
  10.6 1.3 %collective-permute-start.2 = (bf16[11,16,128]{2,1,0:T(8,128)(2,1)S(1)}, bf16[11,16,128]{2,1,0:T(8,128)(2,1)S(1)}, u32[]{:S(2)}, u32[]{:S(2)}) collective-permute-start(bf16[11,16,128]{2,1,0:T(8,128)(2,1)S(1)} %get-tuple-element.39), channel_id=1, source_target_pairs={{2,0},{4,2},{6,4},{8,6},{10,8},{12,10},{14,12},{3,1},{5,3},{7,5},{... | collective-permute-start | bytes 135176 | tf_op jit(solution)/shard_map/ppermute | solution.py:677
  11.9 0.0 copy-start.1
  12.0 3.6 %collective-permute-done.2.ryp_in = bf16[11,16,128]{2,1,0:T(8,128)(2,1)S(1)} collective-permute-done((bf16[11,16,128]{2,1,0:T(8,128)(2,1)S(1)}, bf16[11,16,128]{2,1,0:T(8,128)(2,1)S(1)}, u32[]{:S(2)}, u32[]{:S(2)}) %collective-permute-start.2) | collective-permute-done | bytes 45088 | tf_op jit(solution)/shard_map/ppermute | solution.py:677
  15.6 0.9 shard_map.172
  16.4 3.1 %collective-permute-start.3 = (bf16[14,16,128]{2,1,0:T(8,128)(2,1)S(1)}, bf16[14,16,128]{2,1,0:T(8,128)(2,1)S(1)}, u32[]{:S(2)}, u32[]{:S(2)}) collective-permute-start(bf16[14,16,128]{2,1,0:T(8,128)(2,1)S(1)} %get-tuple-element.46), channel_id=1, source_target_pairs={{0,16},{16,32},{32,48},{48,64},{64,80},{80,96},{96,112},{112,128},... | collective-permute-start | bytes 172040 | tf_op jit(solution)/shard_map/ppermute | solution.py:676
  19.5 1.3 %collective-permute-start.4 = (bf16[14,16,128]{2,1,0:T(8,128)(2,1)S(1)}, bf16[14,16,128]{2,1,0:T(8,128)(2,1)S(1)}, u32[]{:S(2)}, u32[]{:S(2)}) collective-permute-start(bf16[14,16,128]{2,1,0:T(8,128)(2,1)S(1)} %get-tuple-element.47), channel_id=1, source_target_pairs={{16,0},{32,16},{48,32},{64,48},{80,64},{96,80},{112,96},{128,112},... | collective-permute-start | bytes 172040 | tf_op jit(solution)/shard_map/ppermute | solution.py:677
  20.9 3.4 %shard_map.173 = (f32[1792,128]{1,0:T(8,128)S(1)}, bf16[3,16,9,16,128]{4,3,2,1,0:T(8,128)(2,1)S(1)}, f32[3,9,128]{2,1,0:T(8,128)S(1)}, bf16[2304,128]{1,0:T(8,128)(2,1)S(1)}) custom-call(s32[1,3]{1,0:T(1,128)S(1)} %copy-done.5, bf16[16,8,2,16,64]{4,3,2,1,0:T(8,128)(2,1)S(1)} %bitcast.26, bf16[33,32,64]{2,1,0:T(8,128)(2,1)S(1)} %get-tuple-element.40.rz, ...), custom_call_target="tpu_custom_call" | custom-call | tf_op jit(solution)/shard_map/pallas_call | solution.py:36
  24.3 0.2 collective-permute-done.4.rxp_in
  24.5 3.0 %shard_map.174 = (f32[2048,128]{1,0:T(8,128)}, bf16[2,3,9,16,128]{4,3,2,1,0:T(8,128)(2,1)S(1)}, bf16[16,1728]{1,0:T(8,128)(2,1)S(1)}, f32[256,128]{1,0:T(8,128)}) custom-call(s32[1,3]{1,0:T(1,128)S(1)} %copy-done.5, bf16[3,16,9,16,128]{4,3,2,1,0:T(8,128)(2,1)S(1)} %get-tuple-element.43.near_low.near_high.scene, ...), custom_call_target="tpu_custom_call" | custom-call | tf_op jit(solution)/shard_map/pallas_call | solution.py:36
  27.5 18.6 %all-to-all-start = ((f32[256,1,128]{2,1,0:T(1,128)}), f32[256,1,128]{2,1,0:T(1,128)S(1)}, u32[]{:S(2)}, u32[]{:S(2)}) async-start(f32[256,1,128]{2,1,0:T(1,128)} %bitcast.7), calls=%async_computation | async-start | bytes 262144 | tf_op jit(solution)/shard_map/all_to_all | solution.py:670
  46.1 0.1 copy.21
  46.3 0.1 maximum_bitcast_fusion
  46.3 0.1 fusion.4
  46.4 2.7 %shard_map.175.turned_in = bf16[3,256,2304]{2,1,0:T(8,128)(2,1)} custom-call(s32[1,3]{1,0:T(1,128)S(1)} %copy-done.6, bf16[3,16,9,16,128]{4,3,2,1,0:T(8,128)(2,1)S(1)} %get-tuple-element.43.near_low.near_high.scene, bf16[2,3,9,16,128]{4,3,2,1,0:T(8,128)(2,1)S(1)} %get-tuple-element.52.ends), custom_call_target="tpu_custom_call" | custom-call | tf_op jit(solution)/shard_map/pallas_call | solution.py:36
  49.1 9.8 %all-to-all-done = f32[256,1,128]{2,1,0:T(1,128)S(1)} async-done(((f32[256,1,128]{2,1,0:T(1,128)}), f32[256,1,128]{2,1,0:T(1,128)S(1)}, u32[]{:S(2)}, u32[]{:S(2)}) %all-to-all-start) | async-done | bytes 131104 | tf_op jit(solution)/shard_map/all_to_all | solution.py:670
  58.9 7.3 %shard_map.176 = (f32[2,2064,128]{2,1,0:T(8,128)S(1)}, f32[2048,128]{1,0:T(8,128)S(1)}, bf16[16,8,2,16,64]{4,3,2,1,0:T(8,128)(2,1)}) custom-call(s32[1,3]{1,0:T(1,128)S(1)} %copy-done.6, f32[256,128]{1,0:T(8,128)S(1)} %bitcast.27, bf16[16,8,2,16,64]{4,3,2,1,0:T(8,128)(2,1)S(1)} %bitcast.30, f32[1,128]{1,0:T(1,128)S(1)} %get-tuple-element.68.gain, ...), custom_call_target="tpu_custom_call" | custom-call | tf_op jit(solution)/shard_map/pallas_call | solution.py:36
  66.3 0.7 collective-permute-start.5
  67.0 2.3 %collective-permute-done.5.other = f32[2048,128]{1,0:T(8,128)S(1)} collective-permute-done((f32[2048,128]{1,0:T(8,128)S(1)}, f32[2048,128]{1,0:T(8,128)S(1)}, u32[]{:S(2)}, u32[]{:S(2)}) %collective-permute-start.5) | collective-permute-done | bytes 1048608 | tf_op jit(solution)/shard_map/ppermute | solution.py:769
  69.3 1.4 %shard_map.177 = bf16[128,16,128]{2,1,0:T(8,128)(2,1)S(1)} custom-call(s32[1,3]{1,0:T(1,128)S(1)} %copy-done.6, f32[2,2064,128]{2,1,0:T(8,128)S(1)} %get-tuple-element.54.mine, f32[2048,128]{1,0:T(8,128)S(1)} %collective-permute-done.5.other, f32[256,128]{1,0:T(8,128)S(1)} %bitcast.28, f32[1,128]{1,0:T(1,128)S(1)} %get-tuple-element.68.gain), custom_call_target="tpu_custom_call" | custom-call | tf_op jit(solution)/shard_map/pallas_call | solution.py:36
  70.7 25.1 %all_to_all.15.pieces = bf16[128,16,128]{2,1,0:T(8,128)(2,1)S(1)} all-to-all(bf16[128,16,128]{2,1,0:T(8,128)(2,1)S(1)} %shard_map.177), channel_id=1, replica_groups=mesh['bx'=16,'by'=8,'cz'=2] {'bx','by'}, dimensions={0} | all-to-all | bytes 1048576 | tf_op jit(solution)/shard_map/all_to_all | solution.py:771
  95.8 1.7 %shard_map.178 = (bf16[128,8,128]{2,1,0:T(8,128)(2,1)S(1)}, f32[64,256]{1,0:T(8,128)}, f32[1,64]{1,0:T(1,128)}, f32[1,64]{1,0:T(1,128)}) custom-call(s32[1,3]{1,0:T(1,128)S(1)} %copy-done.6, bf16[128,16,128]{2,1,0:T(8,128)(2,1)S(1)} %all_to_all.15.pieces, f32[256,128]{1,0:T(8,128)S(1)} %bitcast.29, f32[1,128]{1,0:T(1,128)S(1)} %get-tuple-element.68.gain, ...), custom_call_target="tpu_custom_call" | custom-call | tf_op jit(solution)/shard_map/pallas_call | solution.py:36
  97.5 19.0 %all_to_all.16.near = bf16[128,8,128]{2,1,0:T(8,128)(2,1)S(1)} all-to-all(bf16[128,8,128]{2,1,0:T(8,128)(2,1)S(1)} %get-tuple-element.56), channel_id=1, replica_groups=mesh['bx'=16,'by'=8,'cz'=2] {'bx','by'}, dimensions={0} | all-to-all | bytes 524288 | tf_op jit(solution)/shard_map/all_to_all | solution.py:777
  116.5 3.2 %collective-permute-start.6 = (bf16[128,8,128]{2,1,0:T(8,128)(2,1)S(1)}, bf16[128,8,128]{2,1,0:T(8,128)(2,1)S(1)}, u32[]{:S(2)}, u32[]{:S(2)}) collective-permute-start(bf16[128,8,128]{2,1,0:T(8,128)(2,1)S(1)} %all_to_all.16.near), channel_id=1, source_target_pairs={{0,1},{1,0},{2,3},{3,2},{4,5},{5,4},{6,7},{7,6},{8,9},{9,8},{10,11... | collective-permute-start | bytes 786440 | tf_op jit(solution)/shard_map/ppermute | solution.py:778
  119.6 1.2 collective-permute-done.6.far
  120.8 2.1 %shard_map.179 = (f32[27,64,64]{2,1,0:T(8,128)}, f32[27,64,64]{2,1,0:T(8,128)}, f32[64,64]{1,0:T(8,128)}, f32[1,1]{1,0:T(1,128)}) custom-call(s32[1,3]{1,0:T(1,128)S(1)} %copy-done.6, bf16[128,8,128]{2,1,0:T(8,128)(2,1)S(1)} %all_to_all.16.near, bf16[128,8,128]{2,1,0:T(8,128)(2,1)S(1)} %collective-permute-done.6.far), custom_call_target="tpu_custom_call" | custom-call | tf_op jit(solution)/shard_map/pallas_call | solution.py:36
  (23 shorter events, 0.1 us)
Async XLA Ops:
  0.6 1.2 copy-start
  1.9 0.7 copy-start.5
  3.9 4.2 %collective-permute-start = (bf16[10,16,128]{2,1,0:T(8,128)(2,1)S(1)}, bf16[10,16,128]{2,1,0:T(8,128)(2,1)S(1)}, u32[]{:S(2)}, u32[]{:S(2)}) collective-permute-start(bf16[10,16,128]{2,1,0:T(8,128)(2,1)S(1)} %get-tuple-element.36), channel_id=1, source_target_pairs={{0,1},{1,0},{2,3},{3,2},{4,5},{5,4},{6,7},{7,6},{8,9},{9,8},{10,11... | collective-permute-start | bytes 122888 | tf_op jit(solution)/shard_map/ppermute | solution.py:706
  8.1 12.8 %copy-start.3 = (bf16[27,64,64]{2,1,0:T(8,128)(2,1)S(1)}, bf16[27,64,64]{2,1,0:T(8,128)(2,1)}, u32[]{:S(2)}) copy-start(bf16[27,64,64]{2,1,0:T(8,128)(2,1)} %taps.1) | copy-start | bytes 663556
  8.8 3.2 %collective-permute-start.1 = (bf16[11,16,128]{2,1,0:T(8,128)(2,1)S(1)}, bf16[11,16,128]{2,1,0:T(8,128)(2,1)S(1)}, u32[]{:S(2)}, u32[]{:S(2)}) collective-permute-start(bf16[11,16,128]{2,1,0:T(8,128)(2,1)S(1)} %get-tuple-element.38), channel_id=1, source_target_pairs={{0,2},{2,4},{4,6},{6,8},{8,10},{10,12},{12,14},{1,3},{3,5},{5,7},{... | collective-permute-start | bytes 135176 | tf_op jit(solution)/shard_map/ppermute | solution.py:676
  10.6 5.0 %collective-permute-start.2 = (bf16[11,16,128]{2,1,0:T(8,128)(2,1)S(1)}, bf16[11,16,128]{2,1,0:T(8,128)(2,1)S(1)}, u32[]{:S(2)}, u32[]{:S(2)}) collective-permute-start(bf16[11,16,128]{2,1,0:T(8,128)(2,1)S(1)} %get-tuple-element.39), channel_id=1, source_target_pairs={{2,0},{4,2},{6,4},{8,6},{10,8},{12,10},{14,12},{3,1},{5,3},{7,5},{... | collective-permute-start | bytes 135176 | tf_op jit(solution)/shard_map/ppermute | solution.py:677
  11.9 12.5 %copy-start.1 = (bf16[16,224,160]{2,1,0:T(8,128)(2,1)S(1)}, bf16[16,224,160]{2,1,0:T(8,128)(2,1)}, u32[]{:S(2)}) copy-start(bf16[16,224,160]{2,1,0:T(8,128)(2,1)} %constant.6.clone.tables) | copy-start | bytes 3440644
  11.9 12.5 %copy-start.4 = (bf16[27,64,64]{2,1,0:T(8,128)(2,1)S(1)}, bf16[27,64,64]{2,1,0:T(8,128)(2,1)}, u32[]{:S(2)}) copy-start(bf16[27,64,64]{2,1,0:T(8,128)(2,1)} %param.16) | copy-start | bytes 663556
  12.0 12.5 %copy-start.7 = (bf16[256,64]{0,1:T(8,128)(2,1)S(1)}, bf16[256,64]{0,1:T(8,128)(2,1)}, u32[]{:S(2)}) copy-start(bf16[256,64]{0,1:T(8,128)(2,1)} %param.18) | copy-start | bytes 98308
  16.4 7.9 %collective-permute-start.3 = (bf16[14,16,128]{2,1,0:T(8,128)(2,1)S(1)}, bf16[14,16,128]{2,1,0:T(8,128)(2,1)S(1)}, u32[]{:S(2)}, u32[]{:S(2)}) collective-permute-start(bf16[14,16,128]{2,1,0:T(8,128)(2,1)S(1)} %get-tuple-element.46), channel_id=1, source_target_pairs={{0,16},{16,32},{32,48},{48,64},{64,80},{80,96},{96,112},{112,128},... | collective-permute-start | bytes 172040 | tf_op jit(solution)/shard_map/ppermute | solution.py:676
  19.5 4.9 %collective-permute-start.4 = (bf16[14,16,128]{2,1,0:T(8,128)(2,1)S(1)}, bf16[14,16,128]{2,1,0:T(8,128)(2,1)S(1)}, u32[]{:S(2)}, u32[]{:S(2)}) collective-permute-start(bf16[14,16,128]{2,1,0:T(8,128)(2,1)S(1)} %get-tuple-element.47), channel_id=1, source_target_pairs={{16,0},{32,16},{48,32},{64,48},{80,64},{96,80},{112,96},{128,112},... | collective-permute-start | bytes 172040 | tf_op jit(solution)/shard_map/ppermute | solution.py:677
  24.5 21.7 %copy-start.8 = (bf16[64,64]{1,0:T(8,128)(2,1)S(1)}, bf16[64,64]{1,0:T(8,128)(2,1)}, u32[]{:S(2)}) copy-start(bf16[64,64]{1,0:T(8,128)(2,1)} %param.17) | copy-start | bytes 24580
  24.5 21.7 %copy-start.9 = (f32[64]{0:T(128)S(1)}, f32[64]{0:T(128)}, u32[]{:S(2)}) copy-start(f32[64]{0:T(128)} %param.19) | copy-start | bytes 772
  24.5 21.7 %copy-start.10 = (f32[64]{0:T(128)S(1)}, f32[64]{0:T(128)}, u32[]{:S(2)}) copy-start(f32[64]{0:T(128)} %param.20) | copy-start | bytes 772
  24.5 21.9 %copy-start.6 = (s32[1,3]{1,0:T(1,128)S(1)}, s32[1,3]{1,0:T(1,128)}, u32[]{:S(2)}) copy-start(s32[1,3]{1,0:T(1,128)} %info.19) | copy-start | bytes 40
  27.5 31.4 %all-to-all-start = ((f32[256,1,128]{2,1,0:T(1,128)}), f32[256,1,128]{2,1,0:T(1,128)S(1)}, u32[]{:S(2)}, u32[]{:S(2)}) async-start(f32[256,1,128]{2,1,0:T(1,128)} %bitcast.7), calls=%async_computation | async-start | bytes 262144 | tf_op jit(solution)/shard_map/all_to_all | solution.py:670
  46.4 12.5 %copy-start.2 = (bf16[1,16,16,16,64]{4,3,2,1,0:T(8,128)(2,1)S(1)}, bf16[1,16,16,16,64]{4,3,2,1,0:T(8,128)(2,1)}, u32[]{:S(2)}) copy-start(bf16[1,16,16,16,64]{4,3,2,1,0:T(8,128)(2,1)} %param.12) | copy-start | bytes 1572868
  66.3 3.0 %collective-permute-start.5 = (f32[2048,128]{1,0:T(8,128)S(1)}, f32[2048,128]{1,0:T(8,128)S(1)}, u32[]{:S(2)}, u32[]{:S(2)}) collective-permute-start(f32[2048,128]{1,0:T(8,128)S(1)} %get-tuple-element.55), channel_id=1, source_target_pairs={{0,1},{1,0},{2,3},{3,2},{4,5},{5,4},{6,7},{7,6},{8,9},{9,8},{10,11... | collective-permute-start | bytes 3145736 | tf_op jit(solution)/shard_map/ppermute | solution.py:769
  116.5 4.3 %collective-permute-start.6 = (bf16[128,8,128]{2,1,0:T(8,128)(2,1)S(1)}, bf16[128,8,128]{2,1,0:T(8,128)(2,1)S(1)}, u32[]{:S(2)}, u32[]{:S(2)}) collective-permute-start(bf16[128,8,128]{2,1,0:T(8,128)(2,1)S(1)} %all_to_all.16.near), channel_id=1, source_target_pairs={{0,1},{1,0},{2,3},{3,2},{4,5},{5,4},{6,7},{7,6},{8,9},{9,8},{10,11... | collective-permute-start | bytes 786440 | tf_op jit(solution)/shard_map/ppermute | solution.py:778
